TPU v7x, 128 devices: a whole 4x4x4 slice. The times are simulated.
128 devices in a mesh: dp: 16 (over y, x), seq: 8 (over z, core).
Axes of the slice: x: 4, y: 4, z: 4, core: 2. Of those that a mesh axis runs over, the one named last changes fastest.
Arguments:
- query_tokens: bfloat16 [2048, 512], P('dp'), may hold values from -16 to 16
- owner: int32 [2048], P('dp'), may hold values from 0 to 1
- d_out: bfloat16 [2048, 512], P('dp'), may hold values from -6 to 6
- history: bfloat16 [32, 16384, 512], P('dp', 'seq'), may hold values from -16 to 16
- lengths: int32 [32], P('dp'), may hold values from 2048 to 16384, as said below
- w_query: bfloat16 [512, 512], replicated, may hold values from -1 to 1
- w_key: bfloat16 [512, 512], replicated, may hold values from -1 to 1
- w_value: bfloat16 [512, 512], replicated, may hold values from -0.25 to 0.25
- w_out: bfloat16 [512, 512], replicated, may hold values from -0.25 to 0.25
Outputs:
- query_grad: bfloat16 [2048, 512], P('dp')
- hist_grad: bfloat16 [32, 16384, 512], P('dp', 'seq')
- weight_grads: float32 [512, 4, 512], P(('dp', 'seq'))
Inputs may be any that keep to these rules, and one draw needn't show every extreme that they name: lengths are at least 2048; some request is full.
All inputs are finite; a program needn't handle non-finite values.
Results may differ from a plain program's by a relative error of at most 0.007.
The roundings to bfloat16 on the way count: a program that leaves them out, or rounds other values in their place, can miss the bound.
Values sent between devices are 32-bit elements; how exact they have to be, the bound alone decides.
No kernel may reach another device: no remote copies, remote signals or barrier semaphores. Data moves between devices by JAX's collectives and lax.ppermute only.
A program may use at most 128 MiB of HBM per device.

v0:
```python
import jax
import jax.numpy as jnp
from jax import lax
from jax.experimental import pallas as pl
from jax.experimental.pallas import tpu as pltpu
from jax.sharding import PartitionSpec as P

PAIRS = 4
LOW = -1e30
F32 = jnp.float32
BF16 = jnp.bfloat16
VMEM = pltpu.MemorySpace.VMEM
HBM = pltpu.MemorySpace.HBM
TILE = 512


def dot(left, right):
    return jnp.dot(left, right, preferred_element_type=F32)


def dot_last(left, right):
    return lax.dot_general(left, right, (((1,), (1,)), ((), ())), preferred_element_type=F32)


def dot_first(left, right):
    return lax.dot_general(left, right, (((0,), (0,)), ((), ())), preferred_element_type=F32)


def tiles(ref):
    events = ref.shape[1]
    return [slice(start, start + TILE) for start in range(0, events, TILE)]


def pair_cols(ref, pair, rows):
    cols = slice(128 * pair, 128 * pair + 128)
    return jnp.concatenate([ref[0, rows, cols], ref[1, rows, cols]], axis=1)


def put_pair(ref, pair, rows, value):
    cols = slice(128 * pair, 128 * pair + 128)
    ref[0, rows, cols] = value[:, 0:128]
    ref[1, rows, cols] = value[:, 128:256]


def pair_lanes(pair):
    return slice(256 * pair, 256 * pair + 256)


def seen_in(lim_ref, rows):
    place = lax.broadcasted_iota(jnp.int32, (TILE, 256), 0) + rows.start
    return place < lim_ref[0:1]


def spread(full, own_col, owner_row, blk_ref, blk_t_ref):
    lane = lax.broadcasted_iota(jnp.int32, (128, 128), 1)
    zero = jnp.zeros((64, 128), F32)
    for pair in range(PAIRS):
        part = full[:, 128 * pair : 128 * pair + 128]
        part_t = part.T
        for req in range(2):
            mine = jnp.where(own_col == req, part, 0.0)
            cols = slice(128 * req, 128 * req + 128)
            blk_t_ref[pair, 0:128, cols] = jnp.where(lane < 64, mine, 0.0).astype(BF16)
            blk_t_ref[pair, 128:256, cols] = jnp.where(lane < 64, 0.0, mine).astype(BF16)
            mine_t = jnp.where(owner_row == req, part_t, 0.0)
            top = jnp.concatenate([mine_t[0:64], zero], axis=1)
            low = jnp.concatenate([zero, mine_t[64:128]], axis=1)
            blk_ref[pair, cols, :] = jnp.concatenate([top, low], axis=0).astype(BF16)


def keys_kernel(lens_ref, own_hbm, tok_hbm, wq_hbm, wk_hbm, hist_hbm,
                key_ref, hist_ref, stat_ref, lim_ref, qb_ref, own_ref, qbt_hbm,
                qbt_ref, tok_ref, wq_ref, wk_ref, sems):
    small = [(own_hbm, own_ref), (tok_hbm, tok_ref), (wq_hbm, wq_ref), (wk_hbm, wk_ref)]
    small = [pltpu.make_async_copy(src, dst, sems.at[i]) for i, (src, dst) in enumerate(small)]
    for copy in small:
        copy.start()
    chunks = []
    for rows in tiles(hist_ref):
        for req in range(2):
            copy = pltpu.make_async_copy(
                hist_hbm.at[req, rows], hist_ref.at[req, rows], sems.at[4 + len(chunks)])
            copy.start()
            chunks.append(copy)
    for copy in small:
        copy.wait()
    owner_row = jnp.broadcast_to(own_ref[...], (128, 128))
    base = lax.axis_index("seq") * hist_ref.shape[1]
    lim = jnp.where(own_ref[...] == 0, lens_ref[0], lens_ref[1]) - base
    lim_ref[...] = jnp.broadcast_to(jnp.concatenate([lim, lim], axis=1), (8, 256))
    q = dot(tok_ref[...], wq_ref[...]).astype(BF16).astype(F32) * 0.125
    spread(q, owner_row.T, owner_row[0:1], qb_ref, qbt_ref)
    qbt_copy = pltpu.make_async_copy(qbt_ref, qbt_hbm, sems.at[4 + len(chunks)])
    qbt_copy.start()

    peak = [jnp.full((1, 256), LOW, F32) for _ in range(PAIRS)]
    total = [jnp.zeros((1, 256), F32) for _ in range(PAIRS)]
    for index, rows in enumerate(tiles(hist_ref)):
        for req in range(2):
            chunks[2 * index + req].wait()
            key_ref[req, rows] = dot(hist_ref[req, rows], wk_ref[...]).astype(BF16)
        seen = seen_in(lim_ref, rows)
        for pair in range(PAIRS):
            score = jnp.where(seen, dot(pair_cols(key_ref, pair, rows), qb_ref[pair]), LOW)
            new = jnp.maximum(peak[pair], jnp.max(score, axis=0, keepdims=True))
            fresh = jnp.sum(jnp.exp(score - new), axis=0, keepdims=True)
            total[pair] = total[pair] * jnp.exp(peak[pair] - new) + fresh
            peak[pair] = new
    stat_ref[...] = jnp.concatenate(peak + total, axis=0)
    qbt_copy.wait()


def values_kernel(wv_hbm, dout_hbm, wout_hbm, own_ref, hist_ref,
                  val_ref, gb_ref, gbt_ref, wv_ref, dout_ref, wout_ref, sems):
    copies = [(wv_hbm, wv_ref), (dout_hbm, dout_ref), (wout_hbm, wout_ref)]
    copies = [pltpu.make_async_copy(src, dst, sems.at[i]) for i, (src, dst) in enumerate(copies)]
    for copy in copies:
        copy.start()
    copies[0].wait()
    for rows in tiles(hist_ref):
        for req in range(2):
            val_ref[req, rows] = dot(hist_ref[req, rows], wv_ref[...]).astype(BF16)
    copies[1].wait()
    copies[2].wait()
    owner_row = jnp.broadcast_to(own_ref[...], (128, 128))
    g = dot_last(dout_ref[...], wout_ref[...]).astype(BF16).astype(F32)
    spread(g, owner_row.T, owner_row[0:1], gb_ref, gbt_ref)


def probs_kernel(*refs):
    stats = refs[0:8]
    lim_ref, qb_ref, gb_ref, key_ref, val_ref, prob_ref, delta_ref = refs[8:]
    top = stats[0][0:4]
    for stat in stats[1:]:
        top = jnp.maximum(top, stat[0:4])
    norm = jnp.zeros((4, 256), F32)
    for stat in stats:
        norm += stat[4:8] * jnp.exp(stat[0:4] - top)
    shift = top + jnp.log(norm)
    delta = [jnp.zeros((1, 256), F32) for _ in range(PAIRS)]
    for rows in tiles(key_ref):
        seen = seen_in(lim_ref, rows)
        for pair in range(PAIRS):
            score = dot(pair_cols(key_ref, pair, rows), qb_ref[pair])
            prob = jnp.where(seen, jnp.exp(score - shift[pair : pair + 1]), 0.0).astype(BF16)
            prob_ref[rows, pair_lanes(pair)] = prob
            slope = dot(pair_cols(val_ref, pair, rows), gb_ref[pair])
            delta[pair] += jnp.sum(prob.astype(F32) * slope, axis=0, keepdims=True)
    delta_ref[...] = jnp.concatenate(delta + [jnp.zeros((4, 256), F32)], axis=0)


def put_shares(out_ref, value):
    for row in range(0, 512, 4):
        dp, seq = row // 32, (row // 4) % 8
        out_ref[seq, 4 * dp : 4 * dp + 4] = value[row : row + 4]


def put_shares(out_ref, value):
    for row in range(0, 512, 4):
        dp, seq = row // 32, (row // 4) % 8
        out_ref[seq, 4 * dp : 4 * dp + 4] = value[row : row + 4]


def halve(shares, keep_ref, send_ref):
    me = lax.axis_index("seq")
    for slot in range(4):
        chip = lax.rem(me // 2 + slot, 4)
        keep_ref[slot] = shares[2 * chip + lax.rem(me, 2)]
        send_ref[slot] = shares[2 * chip + 1 - lax.rem(me, 2)]


def value_grads_kernel(prob_ref, hist_ref, gbt_ref, dv_hbm, keep_ref, send_ref,
                       dv_ref, wgrad, shares, sems):
    copies = []
    for rows in tiles(hist_ref):
        for pair in range(PAIRS):
            grad = dot(prob_ref[rows, pair_lanes(pair)], gbt_ref[pair]).astype(BF16)
            put_pair(dv_ref, pair, rows, grad)
        for req in range(2):
            copy = pltpu.make_async_copy(
                dv_ref.at[req, rows], dv_hbm.at[req, rows], sems.at[len(copies)])
            copy.start()
            copies.append(copy)
    wgrad[...] = dot_first(hist_ref[0], dv_ref[0])
    wgrad[...] += dot_first(hist_ref[1], dv_ref[1])
    put_shares(shares, wgrad)
    halve(shares, keep_ref, send_ref)
    for copy in copies:
        copy.wait()


def attention_kernel(own_ref, prob_ref, val_ref, token_ref, att_ref):
    first = own_ref[...] == 0
    for pair in range(PAIRS):
        blk = jnp.zeros((256, 256), F32)
        for rows in tiles(val_ref):
            blk += dot_first(pair_cols(val_ref, pair, rows), prob_ref[rows, pair_lanes(pair)])
        for head in range(2):
            lanes = slice(128 * head, 128 * head + 128)
            one = blk[64 * head : 64 * head + 64, lanes]
            two = blk[128 + 64 * head : 192 + 64 * head, lanes]
            start = 128 * pair + 64 * head
            att_ref[start : start + 64] = jnp.where(first, one, two)


def query_part_kernel(*refs):
    deltas = refs[0:8]
    (own_ref, prob_ref, key_ref, val_ref, gb_ref, att_ref, keep_ref, recv_ref,
     ds_hbm, out_ref, part0, part1, part2, part3, ds_ref, sems) = refs[8:]
    delta = deltas[0][0:4]
    for other in deltas[1:]:
        delta += other[0:4]
    own_col = jnp.broadcast_to(own_ref[...], (128, 128)).T
    lane = lax.broadcasted_iota(jnp.int32, (128, 128), 1)
    copies = []
    blks = [jnp.zeros((256, 256), F32) for _ in range(PAIRS)]
    for rows in tiles(key_ref):
        for pair in range(PAIRS):
            prob = prob_ref[rows, pair_lanes(pair)].astype(F32)
            slope = dot(pair_cols(val_ref, pair, rows), gb_ref[pair])
            ds = (prob * (slope - delta[pair : pair + 1])).astype(BF16)
            ds_ref[rows, pair_lanes(pair)] = ds
            blks[pair] += dot_first(ds, pair_cols(key_ref, pair, rows))
        copy = pltpu.make_async_copy(ds_ref.at[rows], ds_hbm.at[rows], sems.at[len(copies)])
        copy.start()
        copies.append(copy)
    for pair in range(PAIRS):
        blk = blks[pair]
        one = jnp.where(own_col == 0, blk[:128, :128], blk[:128, 128:])
        two = jnp.where(own_col == 0, blk[128:, :128], blk[128:, 128:])
        dq = jnp.where(lane < 64, one, two)
        for dev in range(8):
            out_ref[dev, 0:16, 128 * pair : 128 * pair + 128] = dq[16 * dev : 16 * dev + 16]
    for row in range(0, 512, 4):
        dp, seq = row // 32, (row // 4) % 8
        lanes = slice(128 * (dp // 4), 128 * (dp // 4) + 128)
        start = 16 + 4 * (dp % 4)
        out_ref[seq, start : start + 4, lanes] = att_ref[row : row + 4]
    for slot, part in enumerate((part0, part1, part2, part3)):
        part[...] = keep_ref[slot] + recv_ref[slot]
    for copy in copies:
        copy.wait()


def key_grads_kernel(ds_hbm, hist_hbm, qbt_hbm, dk_hbm, keep_ref, send_ref,
                     ds_ref, hist_ref, qbt_ref, dk_ref, wgrad, shares, sems, out_sems):
    first = pltpu.make_async_copy(qbt_hbm, qbt_ref, sems.at[0])
    first.start()
    ins = []
    for index, rows in enumerate(tiles(hist_ref)):
        copy = pltpu.make_async_copy(ds_hbm.at[rows], ds_ref.at[rows], sems.at[1 + index])
        copy.start()
        ins.append(copy)
    loads = []
    for req in range(2):
        copy = pltpu.make_async_copy(
            hist_hbm.at[req], hist_ref.at[req], sems.at[1 + len(ins) + req])
        copy.start()
        loads.append(copy)
    first.wait()
    outs = []
    for index, rows in enumerate(tiles(hist_ref)):
        ins[index].wait()
        for pair in range(PAIRS):
            grad = dot(ds_ref[rows, pair_lanes(pair)], qbt_ref[pair]).astype(BF16)
            put_pair(dk_ref, pair, rows, grad)
        for req in range(2):
            copy = pltpu.make_async_copy(
                dk_ref.at[req, rows], dk_hbm.at[req, rows], out_sems.at[len(outs)])
            copy.start()
            outs.append(copy)
    loads[0].wait()
    wgrad[...] = dot_first(hist_ref[0], dk_ref[0])
    loads[1].wait()
    wgrad[...] += dot_first(hist_ref[1], dk_ref[1])
    put_shares(shares, wgrad)
    halve(shares, keep_ref, send_ref)
    for copy in outs:
        copy.wait()


def gather_kernel(part_ref, token_ref, dq_ref, att_ref):
    summed = jnp.sum(part_ref[...], axis=0)
    for dev in range(8):
        dq_ref[dev] = summed[0:16]
    for quarter in range(4):
        lanes = slice(128 * quarter, 128 * quarter + 128)
        att_ref[16 * quarter : 16 * quarter + 16] = summed[16:32, lanes]


def halves_kernel(keep_ref, recv_ref, token_ref, part0, part1, part2, part3):
    for slot, part in enumerate((part0, part1, part2, part3)):
        part[...] = keep_ref[slot] + recv_ref[slot]


def hist_grads_kernel(dk_hbm, dv_hbm, wk_hbm, wv_hbm, token_ref, out_hbm, done_ref,
                      dk_ref, dv_ref, wk_ref, wv_ref, buf, sems, out_sems):
    weights = [pltpu.make_async_copy(wk_hbm, wk_ref, sems.at[0]),
               pltpu.make_async_copy(wv_hbm, wv_ref, sems.at[1])]
    for copy in weights:
        copy.start()
    ins = []
    for req in range(2):
        for rows in tiles(buf):
            two = []
            for src, dst in ((dk_hbm, dk_ref), (dv_hbm, dv_ref)):
                copy = pltpu.make_async_copy(
                    src.at[req, rows], dst.at[req, rows], sems.at[2 + 2 * len(ins) + len(two)])
                copy.start()
                two.append(copy)
            ins.append(two)
    for copy in weights:
        copy.wait()
    copies = []
    for req in range(2):
        for rows in tiles(buf):
            for copy in ins[len(copies)]:
                copy.wait()
            buf[req, rows] = (dot_last(dk_ref[req, rows], wk_ref[...])
                              + dot_last(dv_ref[req, rows], wv_ref[...])).astype(BF16)
            copy = pltpu.make_async_copy(
                buf.at[req, rows], out_hbm.at[req, rows], out_sems.at[len(copies)])
            copy.start()
            copies.append(copy)
    done_ref[...] = jnp.zeros(done_ref.shape, F32)
    for copy in copies:
        copy.wait()


def outer_kernel(*refs):
    keys = refs[0:4]
    vals = refs[4:8]
    dq_ref, tok_ref, att_ref, dout_ref, token_ref, out_ref = refs[8:]
    dq = (dq_ref[...].reshape(128, 512) * 0.125).astype(BF16)
    row = lax.broadcasted_iota(jnp.int32, (64, 512), 0)
    col = lax.broadcasted_iota(jnp.int32, (64, 512), 1)
    feature = (row // 4) * 32 + lax.axis_index("seq") * 4 + row % 4
    pick = jnp.where(col == feature, 1.0, 0.0).astype(BF16)
    tok = dot_last(pick, tok_ref[...]).astype(BF16)
    parts = [dot(tok, dq),
             keys[0][...] + keys[1][...] + keys[2][...] + keys[3][...],
             vals[0][...] + vals[1][...] + vals[2][...] + vals[3][...],
             dot(att_ref[...].astype(BF16), dout_ref[...])]
    for dp in range(16):
        for part in range(4):
            out_ref[dp, 4 * part : 4 * part + 4] = parts[part][4 * dp : 4 * dp + 4]


def query_grad_kernel(dq_ref, wq_ref, token_ref, out_ref):
    dq = (dq_ref[...].reshape(128, 512) * 0.125).astype(BF16)
    out_ref[...] = dot_last(dq, wq_ref[...]).astype(BF16)


def final_kernel(part_ref, out_ref):
    summed = jnp.sum(part_ref[...], axis=0)
    for part in range(4):
        out_ref[:, part, :] = summed[4 * part : 4 * part + 4]


IN_VMEM = pl.BlockSpec(memory_space=VMEM)
IN_HBM = pl.BlockSpec(memory_space=pl.ANY)
IN_SMEM = pl.BlockSpec(memory_space=pltpu.MemorySpace.SMEM)


def call(kernel, args, outs, scratch=(), limit=26):
    specs = {"vmem": IN_VMEM, "hbm": IN_HBM, "smem": IN_SMEM}
    spaces = {"vmem": VMEM, "hbm": HBM}
    ins = [pltpu.with_memory_space_constraint(x, spaces[s]) if s in spaces else x for x, s in args]
    return pl.pallas_call(
        kernel,
        in_specs=[specs[s] for _, s in args],
        out_specs=[specs[s] for s, _, _ in outs],
        out_shape=[spaces[s](shape, dtype) for s, dtype, shape in outs],
        scratch_shapes=scratch,
        compiler_params=pltpu.CompilerParams(vmem_limit_bytes=limit * 1024 * 1024),
    )(*ins)


def swap(x, axis):
    return lax.all_to_all(x, axis, 0, 0)


def up(x, chips):
    return lax.ppermute(x, "seq", [(i, (i + 2 * chips) % 8) for i in range(8)])


def across(x):
    return lax.ppermute(x, "seq", [(i, i ^ 1) for i in range(8)])


def from_chips(x):
    return [x] + [up(x, chips) for chips in (1, 2, 3)]


def per_device(query_tokens, owner, d_out, history, lengths, w_query, w_key, w_value, w_out):
    rows, width = query_tokens.shape
    requests, events, _ = history.shape
    steps = events // TILE
    ev = (requests, events, width)
    mat = (width, width)
    blk = (PAIRS, 256, 256)
    vec = ("vmem", F32, (8, 256))
    pairs = (events, 256 * PAIRS)
    half = ("vmem", F32, (4, 64, width))
    quarter = ("vmem", F32, (64, width))
    dma = pltpu.SemaphoreType.DMA
    v = lambda *xs: [(x, "vmem") for x in xs]
    h = lambda *xs: [(x, "hbm") for x in xs]

    keys, hist, stats, lim, qb, own, qbt = call(
        keys_kernel,
        [(lengths, "smem")] + h(owner.reshape(1, rows), query_tokens, w_query, w_key, history),
        [("vmem", BF16, ev), ("vmem", BF16, ev), vec, ("vmem", jnp.int32, (8, 256)),
         ("vmem", BF16, blk), ("vmem", jnp.int32, (1, rows)), ("hbm", BF16, blk)],
        [pltpu.VMEM(blk, BF16), pltpu.VMEM((rows, width), BF16), pltpu.VMEM(mat, BF16),
         pltpu.VMEM(mat, BF16), dma((5 + 2 * steps,))],
    )
    stats = from_chips(stats)
    values, gb, gbt = call(
        values_kernel,
        h(w_value, d_out, w_out) + v(own, hist),
        [("vmem", BF16, ev), ("vmem", BF16, blk), ("vmem", BF16, blk)],
        [pltpu.VMEM(mat, BF16), pltpu.VMEM((rows, width), BF16), pltpu.VMEM(mat, BF16),
         dma((3,))],
    )
    stats = stats + [across(x) for x in stats]
    probs, delta = call(
        probs_kernel, v(*stats, lim, qb, gb, keys, values), [("vmem", BF16, pairs), vec])
    delta = from_chips(delta)
    dv, keep, send = call(
        value_grads_kernel, v(probs, hist, gbt), [("hbm", BF16, ev), half, half],
        [pltpu.VMEM(ev, BF16), pltpu.VMEM(mat, F32), pltpu.VMEM((8, 64, width), F32),
         dma((2 * steps,))])
    recv = across(send)
    delta = delta + [across(x) for x in delta]
    (att,) = call(
        attention_kernel, v(own, probs, values, keep), [("vmem", F32, (width, rows))])

    ds, part, *wgrad_v = call(
        query_part_kernel, v(*delta, own, probs, keys, values, gb, att, keep, recv),
        [("hbm", BF16, pairs), ("vmem", F32, (8, 32, width))] + [quarter] * 4,
        [pltpu.VMEM(pairs, BF16), dma((steps,))])
    part = swap(part, "seq")
    wgrad_v = [wgrad_v[0]] + [up(wgrad_v[i], i) for i in (1, 2, 3)]
    dk, keep, send = call(
        key_grads_kernel, h(ds, history, qbt), [("hbm", BF16, ev), half, half],
        [pltpu.VMEM(pairs, BF16), pltpu.VMEM(ev, BF16), pltpu.VMEM(blk, BF16),
         pltpu.VMEM(ev, BF16), pltpu.VMEM(mat, F32), pltpu.VMEM((8, 64, width), F32),
         dma((3 + steps,)), dma((2 * steps,))])
    recv = across(send)
    dq, att = call(
        gather_kernel, v(part) + h(dk),
        [("vmem", F32, (8, 16, width)), ("vmem", F32, (64, rows))])
    wgrad_k = call(halves_kernel, v(keep, recv, att), [quarter] * 4)
    dq = swap(dq, "seq")
    token = wgrad_k[0]
    wgrad_k = [wgrad_k[0]] + [up(wgrad_k[i], i) for i in (1, 2, 3)]
    hist_grad, token = call(
        hist_grads_kernel, h(dk, dv, w_key, w_value) + v(token),
        [("hbm", BF16, ev), ("vmem", F32, (8, 128))],
        [pltpu.VMEM(ev, BF16), pltpu.VMEM(ev, BF16), pltpu.VMEM(mat, BF16),
         pltpu.VMEM(mat, BF16), pltpu.VMEM(ev, BF16), dma((2 + 4 * steps,)), dma((2 * steps,))])
    (outer,) = call(
        outer_kernel, v(*wgrad_k, *wgrad_v, dq, query_tokens, att, d_out, token),
        [("vmem", F32, (16, 16, width))])
    token = outer
    outer = swap(outer, "dp")
    (query_grad,) = call(
        query_grad_kernel, v(dq, w_query, token), [("vmem", BF16, (rows, width))])
    (weight_part,) = call(final_kernel, v(outer), [("vmem", F32, (4, 4, width))])
    return query_grad, hist_grad, weight_part


def solution(mesh):
    return jax.shard_map(
        per_device,
        mesh=mesh,
        in_specs=(
            P("dp", None),
            P("dp"),
            P("dp", None),
            P("dp", "seq", None),
            P("dp"),
            P(),
            P(),
            P(),
            P(),
        ),
        out_specs=(P("dp", None), P("dp", "seq", None), P(("dp", "seq"), None, None)),
        check_vma=False,
    )
```

profile of v0, /device:TPU:0, one launch (start us, length us, event | category | flops | bytes accessed | tf_op | source)
XLA Modules:
  0.0 99.6 jit_solution(15900435732724317106)
XLA Ops:
  0.6 0.6 copy-done.3
  1.3 8.6 %shard_map.112 = (bf16[2,2048,512]{2,1,0:T(8,128)(2,1)S(1)}, bf16[2,2048,512]{2,1,0:T(8,128)(2,1)S(1)}, f32[8,256]{1,0:T(8,128)S(1)}, s32[8,256]{1,0:T(8,128)S(1...) custom-call(s32[2]{0:T(128)S(1)} %copy-done.3, s32[1,128]{1,0:T(1,128)} %bitcast.1, ...), custom_call_target="tpu_custom_call" | custom-call | tf_op jit(solution)/shard_map/pallas_call | solution.py:369
  9.9 4.2 %collective-permute-start.2 = (f32[8,256]{1,0:T(8,128)S(1)}, f32[8,256]{1,0:T(8,128)S(1)}, u32[]{:S(2)}, u32[]{:S(2)}) collective-permute-start(f32[8,256]{1,0:T(8,128)S(1)} %get-tuple-element.35.refs_0_), channel_id=1, source_target_pairs={{0,6},{1,7},{2,0},{3,1},{4,2},{5,3},{6,4},{7,5},{8,14},{9,15},{10,... | collective-permute-start | bytes 24584 | tf_op jit(solution)/shard_map/ppermute | solution.py:384
  14.1 1.3 %collective-permute-start = (f32[8,256]{1,0:T(8,128)S(1)}, f32[8,256]{1,0:T(8,128)S(1)}, u32[]{:S(2)}, u32[]{:S(2)}) collective-permute-start(f32[8,256]{1,0:T(8,128)S(1)} %get-tuple-element.35.refs_0_), channel_id=1, source_target_pairs={{0,2},{1,3},{2,4},{3,5},{4,6},{5,7},{6,0},{7,1},{8,10},{9,11},{10,... | collective-permute-start | bytes 24584 | tf_op jit(solution)/shard_map/ppermute | solution.py:384
  15.9 3.4 %collective-permute-done.1.refs_2_ = f32[8,256]{1,0:T(8,128)S(1)} collective-permute-done((f32[8,256]{1,0:T(8,128)S(1)}, f32[8,256]{1,0:T(8,128)S(1)}, u32[]{:S(2)}, u32[]{:S(2)}) %collective-permute-start.1) | collective-permute-done | bytes 8224 | tf_op jit(solution)/shard_map/ppermute | solution.py:384
  19.7 3.9 %shard_map.113 = (bf16[2,2048,512]{2,1,0:T(8,128)(2,1)S(1)}, bf16[4,256,256]{2,1,0:T(8,128)(2,1)S(1)}, bf16[4,256,256]{2,1,0:T(8,128)(2,1)S(1)}) custom-call(bf16[512,512]{1,0:T(8,128)(2,1)} %wv_hbm.3, bf16[128,512]{1,0:T(8,128)(2,1)} %refs_11_.1, bf16[512,512]{1,0:T(8,128)(2,1)} %wout_hbm.1, s32[1,128]{1,0:T(1,128)S(1)} %get-tuple-element.38.own_ref.refs_8_, ...), custom_call_target="tpu_custom_call" | custom-call | tf_op jit(solution)/shard_map/pallas_call | solution.py:369
  23.7 3.1 %shard_map.114 = (bf16[2048,1024]{1,0:T(8,128)(2,1)S(1)}, f32[8,256]{1,0:T(8,128)S(1)}) custom-call(f32[8,256]{1,0:T(8,128)S(1)} %get-tuple-element.35.refs_0_, f32[8,256]{1,0:T(8,128)S(1)} %collective-permute-done.refs_1_, f32[8,256]{1,0:T(8,128)S(1)} %collective-permute-done.1.refs_2_, f32[8,256]{1,0:T(8,128)S(1)} %collective-permute-done.2.refs_3_, ...), custom_call_target="tpu_custom_call" | custom-call | tf_op jit(solution)/shard_map/pallas_call | solution.py:369
  26.8 4.2 %shard_map.115 = (bf16[2,2048,512]{2,1,0:T(8,128)(2,1)}, f32[4,64,512]{2,1,0:T(8,128)S(1)}, f32[4,64,512]{2,1,0:T(8,128)S(1)}) custom-call(bf16[2048,1024]{1,0:T(8,128)(2,1)S(1)} %get-tuple-element.44.prob_ref.refs_9_, bf16[2,2048,512]{2,1,0:T(8,128)(2,1)S(1)} %get-tuple-element.39.hist_ref, bf16[4,256,256]{2,1,0:T(8,128)(2,1)S(1)} %get-tuple-element.45.gbt_ref), custom_call_target="tpu_custom_call" | custom-call | tf_op jit(solution)/shard_map/pallas_call | solution.py:369
  31.1 0.6 collective-permute-start.9
  31.8 1.4 %collective-permute-start.8 = (f32[8,256]{1,0:T(8,128)S(1)}, f32[8,256]{1,0:T(8,128)S(1)}, u32[]{:S(2)}, u32[]{:S(2)}) collective-permute-start(f32[8,256]{1,0:T(8,128)S(1)} %get-tuple-element.43.refs_0_), channel_id=1, source_target_pairs={{0,4},{1,5},{2,6},{3,7},{4,0},{5,1},{6,2},{7,3},{8,12},{9,13},{10,... | collective-permute-start | bytes 24584 | tf_op jit(solution)/shard_map/ppermute | solution.py:384
  33.1 1.4 %collective-permute-start.7 = (f32[8,256]{1,0:T(8,128)S(1)}, f32[8,256]{1,0:T(8,128)S(1)}, u32[]{:S(2)}, u32[]{:S(2)}) collective-permute-start(f32[8,256]{1,0:T(8,128)S(1)} %get-tuple-element.43.refs_0_), channel_id=1, source_target_pairs={{0,2},{1,3},{2,4},{3,5},{4,6},{5,7},{6,0},{7,1},{8,10},{9,11},{10,... | collective-permute-start | bytes 24584 | tf_op jit(solution)/shard_map/ppermute | solution.py:384
  35.1 1.8 %collective-permute-done.8.refs_2_ = f32[8,256]{1,0:T(8,128)S(1)} collective-permute-done((f32[8,256]{1,0:T(8,128)S(1)}, f32[8,256]{1,0:T(8,128)S(1)}, u32[]{:S(2)}, u32[]{:S(2)}) %collective-permute-start.8) | collective-permute-done | bytes 8224 | tf_op jit(solution)/shard_map/ppermute | solution.py:384
  36.9 1.1 %collective-permute-done.7.refs_1_ = f32[8,256]{1,0:T(8,128)S(1)} collective-permute-done((f32[8,256]{1,0:T(8,128)S(1)}, f32[8,256]{1,0:T(8,128)S(1)}, u32[]{:S(2)}, u32[]{:S(2)}) %collective-permute-start.7) | collective-permute-done | bytes 8224 | tf_op jit(solution)/shard_map/ppermute | solution.py:384
  38.0 1.3 %shard_map.116.refs_13_ = f32[512,128]{1,0:T(8,128)S(1)} custom-call(s32[1,128]{1,0:T(1,128)S(1)} %get-tuple-element.38.own_ref.refs_8_, bf16[2048,1024]{1,0:T(8,128)(2,1)S(1)} %get-tuple-element.44.prob_ref.refs_9_, bf16[2,2048,512]{2,1,0:T(8,128)(2,1)S(1)} %get-tuple-element.42.refs_12_.val_ref.refs_11_, f32[4,64,512]{2,1,0:T(8,128)S(1)} %get-tuple-element.46.token_ref.refs_14_), custom_call_target="tpu_custom_call" | custom-call | tf_op jit(solution)/shard_map/pallas_call | solution.py:369
  39.4 4.8 %shard_map.117 = (bf16[2048,1024]{1,0:T(8,128)(2,1)}, f32[8,32,512]{2,1,0:T(8,128)}, f32[64,512]{1,0:T(8,128)S(1)}, f32[64,512]{1,0:T(8,128)S(1)}, f32[64,512]{1,0:T(8,128)S(1)}, /*index=5*/f32[64,512]{1,0:T(8,128)S(1)}) custom-call(f32[8,256]{1,0:T(8,128)S(1)} %get-tuple-element.43.refs_0_, f32[8,256]{1,0:T(8,128)S(1)} %collective-permute-done.7.refs_1_, ...), custom_call_target="tpu_custom_call" | custom-call | tf_op jit(solution)/shard_map/pallas_call | solution.py:369
  44.2 3.5 %all-to-all-start = ((f32[8,32,512]{2,1,0:T(8,128)}), f32[8,32,512]{2,1,0:T(8,128)S(1)}, u32[]{:S(2)}, u32[]{:S(2)}) async-start(f32[8,32,512]{2,1,0:T(8,128)} %get-tuple-element.48), calls=%async_computation | async-start | bytes 1048576 | tf_op jit(solution)/shard_map/all_to_all | solution.py:380
  47.7 6.7 %shard_map.118 = (bf16[2,2048,512]{2,1,0:T(8,128)(2,1)}, f32[4,64,512]{2,1,0:T(8,128)S(1)}, f32[4,64,512]{2,1,0:T(8,128)S(1)}) custom-call(bf16[2048,1024]{1,0:T(8,128)(2,1)} %get-tuple-element.49.ds_hbm, bf16[2,2048,512]{2,1,0:T(8,128)(2,1)} %hist_hbm.3, bf16[4,256,256]{2,1,0:T(8,128)(2,1)} %get-tuple-element.50.qbt_hbm), custom_call_target="tpu_custom_call" | custom-call | tf_op jit(solution)/shard_map/pallas_call | solution.py:369
  55.0 1.6 %collective-permute-start.19 = (f32[64,512]{1,0:T(8,128)S(1)}, f32[64,512]{1,0:T(8,128)S(1)}, u32[]{:S(2)}, u32[]{:S(2)}) collective-permute-start(f32[64,512]{1,0:T(8,128)S(1)} %get-tuple-element.61), channel_id=1, source_target_pairs={{0,2},{1,3},{2,4},{3,5},{4,6},{5,7},{6,0},{7,1},{8,10},{9,11},{10,... | collective-permute-start | bytes 393224 | tf_op jit(solution)/shard_map/ppermute | solution.py:384
  56.6 1.4 %all-to-all-done.part_ref = f32[8,32,512]{2,1,0:T(8,128)S(1)} async-done(((f32[8,32,512]{2,1,0:T(8,128)}), f32[8,32,512]{2,1,0:T(8,128)S(1)}, u32[]{:S(2)}, u32[]{:S(2)}) %all-to-all-start) | async-done | bytes 524320 | tf_op jit(solution)/shard_map/all_to_all | solution.py:380
  58.0 0.8 shard_map.119
  58.7 3.4 %all-to-all-start.1 = ((f32[8,16,512]{2,1,0:T(8,128)}), f32[8,16,512]{2,1,0:T(8,128)S(1)}, u32[]{:S(2)}, u32[]{:S(2)}) async-start(f32[8,16,512]{2,1,0:T(8,128)} %get-tuple-element.52), calls=%async_computation.1 | async-start | bytes 524288 | tf_op jit(solution)/shard_map/all_to_all | solution.py:380
  62.1 3.4 %collective-permute-start.20 = (f32[64,512]{1,0:T(8,128)S(1)}, f32[64,512]{1,0:T(8,128)S(1)}, u32[]{:S(2)}, u32[]{:S(2)}) collective-permute-start(f32[64,512]{1,0:T(8,128)S(1)} %get-tuple-element.62), channel_id=1, source_target_pairs={{0,4},{1,5},{2,6},{3,7},{4,0},{5,1},{6,2},{7,3},{8,12},{9,13},{10,... | collective-permute-start | bytes 393224 | tf_op jit(solution)/shard_map/ppermute | solution.py:384
  65.6 1.2 %collective-permute-start.21 = (f32[64,512]{1,0:T(8,128)S(1)}, f32[64,512]{1,0:T(8,128)S(1)}, u32[]{:S(2)}, u32[]{:S(2)}) collective-permute-start(f32[64,512]{1,0:T(8,128)S(1)} %get-tuple-element.63), channel_id=1, source_target_pairs={{0,6},{1,7},{2,0},{3,1},{4,2},{5,3},{6,4},{7,5},{8,14},{9,15},{10,... | collective-permute-start | bytes 393224 | tf_op jit(solution)/shard_map/ppermute | solution.py:384
  66.8 0.9 collective-permute-start.16
  67.7 0.7 collective-permute-start.17
  68.5 2.5 %collective-permute-start.18 = (f32[64,512]{1,0:T(8,128)S(1)}, f32[64,512]{1,0:T(8,128)S(1)}, u32[]{:S(2)}, u32[]{:S(2)}) collective-permute-start(f32[64,512]{1,0:T(8,128)S(1)} %get-tuple-element.59), channel_id=1, source_target_pairs={{0,6},{1,7},{2,0},{3,1},{4,2},{5,3},{6,4},{7,5},{8,14},{9,15},{10,... | collective-permute-start | bytes 393224 | tf_op jit(solution)/shard_map/ppermute | solution.py:384
  71.0 8.5 %shard_map.121 = (bf16[2,2048,512]{2,1,0:T(8,128)(2,1)}, f32[8,128]{1,0:T(8,128)S(1)}) custom-call(bf16[2,2048,512]{2,1,0:T(8,128)(2,1)} %get-tuple-element.51.token_ref.dk_hbm, bf16[2,2048,512]{2,1,0:T(8,128)(2,1)} %get-tuple-element.64.dv_hbm, bf16[512,512]{1,0:T(8,128)(2,1)} %wk_hbm.3, bf16[512,512]{1,0:T(8,128)(2,1)} %wv_hbm.3, ...), custom_call_target="tpu_custom_call" | custom-call | tf_op jit(solution)/shard_map/pallas_call | solution.py:369
  79.6 1.2 %shard_map.122.token_ref = f32[16,16,512]{2,1,0:T(8,128)} custom-call(f32[64,512]{1,0:T(8,128)S(1)} %get-tuple-element.56.token_ref.refs_0_, f32[64,512]{1,0:T(8,128)S(1)} %collective-permute-done.16.refs_1_, f32[64,512]{1,0:T(8,128)S(1)} %collective-permute-done.17.refs_2_, f32[64,512]{1,0:T(8,128)S(1)} %collective-permute-done.18.refs_3_, ...), custom_call_target="tpu_custom_call" | custom-call | tf_op jit(solution)/shard_map/pallas_call | solution.py:369
  80.8 7.0 %all-to-all-start.2 = ((f32[16,16,512]{2,1,0:T(8,128)}), f32[16,16,512]{2,1,0:T(8,128)S(1)}, u32[]{:S(2)}, u32[]{:S(2)}) async-start(f32[16,16,512]{2,1,0:T(8,128)} %shard_map.122.token_ref), calls=%async_computation.2 | async-start | bytes 1048576 | tf_op jit(solution)/shard_map/all_to_all | solution.py:380
  87.9 1.4 %shard_map.123 = bf16[128,512]{1,0:T(8,128)(2,1)S(1)} custom-call(f32[8,16,512]{2,1,0:T(8,128)S(1)} %all-to-all-done.1.refs_8_.dq_ref, bf16[512,512]{1,0:T(8,128)(2,1)S(1)} %copy-done, f32[16,16,512]{2,1,0:T(8,128)} %shard_map.122.token_ref), custom_call_target="tpu_custom_call" | custom-call | tf_op jit(solution)/shard_map/pallas_call | solution.py:369
  89.3 0.7 copy.12
  89.9 9.1 %all-to-all-done.2.part_ref = f32[16,16,512]{2,1,0:T(8,128)S(1)} async-done(((f32[16,16,512]{2,1,0:T(8,128)}), f32[16,16,512]{2,1,0:T(8,128)S(1)}, u32[]{:S(2)}, u32[]{:S(2)}) %all-to-all-start.2) | async-done | bytes 524320 | tf_op jit(solution)/shard_map/all_to_all | solution.py:380
  (41 shorter events, 2.9 us)
Async XLA Ops:
  0.6 0.7 copy-start.3
  9.9 5.6 %collective-permute-start.2 = (f32[8,256]{1,0:T(8,128)S(1)}, f32[8,256]{1,0:T(8,128)S(1)}, u32[]{:S(2)}, u32[]{:S(2)}) collective-permute-start(f32[8,256]{1,0:T(8,128)S(1)} %get-tuple-element.35.refs_0_), channel_id=1, source_target_pairs={{0,6},{1,7},{2,0},{3,1},{4,2},{5,3},{6,4},{7,5},{8,14},{9,15},{10,... | collective-permute-start | bytes 24584 | tf_op jit(solution)/shard_map/ppermute | solution.py:384
  14.1 5.2 %collective-permute-start.1 = (f32[8,256]{1,0:T(8,128)S(1)}, f32[8,256]{1,0:T(8,128)S(1)}, u32[]{:S(2)}, u32[]{:S(2)}) collective-permute-start(f32[8,256]{1,0:T(8,128)S(1)} %get-tuple-element.35.refs_0_), channel_id=1, source_target_pairs={{0,4},{1,5},{2,6},{3,7},{4,0},{5,1},{6,2},{7,3},{8,12},{9,13},{10,... | collective-permute-start | bytes 24584 | tf_op jit(solution)/shard_map/ppermute | solution.py:384
  14.1 5.2 %collective-permute-start = (f32[8,256]{1,0:T(8,128)S(1)}, f32[8,256]{1,0:T(8,128)S(1)}, u32[]{:S(2)}, u32[]{:S(2)}) collective-permute-start(f32[8,256]{1,0:T(8,128)S(1)} %get-tuple-element.35.refs_0_), channel_id=1, source_target_pairs={{0,2},{1,3},{2,4},{3,5},{4,6},{5,7},{6,0},{7,1},{8,10},{9,11},{10,... | collective-permute-start | bytes 24584 | tf_op jit(solution)/shard_map/ppermute | solution.py:384
  15.3 8.3 %collective-permute-start.3 = (f32[8,256]{1,0:T(8,128)S(1)}, f32[8,256]{1,0:T(8,128)S(1)}, u32[]{:S(2)}, u32[]{:S(2)}) collective-permute-start(f32[8,256]{1,0:T(8,128)S(1)} %get-tuple-element.35.refs_0_), channel_id=1, source_target_pairs={{0,1},{1,0},{2,3},{3,2},{4,5},{5,4},{6,7},{7,6},{8,9},{9,8},{10,11... | collective-permute-start | bytes 24584 | tf_op jit(solution)/shard_map/ppermute | solution.py:388
  15.4 8.2 %collective-permute-start.6 = (f32[8,256]{1,0:T(8,128)S(1)}, f32[8,256]{1,0:T(8,128)S(1)}, u32[]{:S(2)}, u32[]{:S(2)}) collective-permute-start(f32[8,256]{1,0:T(8,128)S(1)} %collective-permute-done.2.refs_3_), channel_id=1, source_target_pairs={{0,1},{1,0},{2,3},{3,2},{4,5},{5,4},{6,7},{7,6},{8,9},{9,8},{10,11... | collective-permute-start | bytes 24584 | tf_op jit(solution)/shard_map/ppermute | solution.py:388
  19.2 4.4 %collective-permute-start.5 = (f32[8,256]{1,0:T(8,128)S(1)}, f32[8,256]{1,0:T(8,128)S(1)}, u32[]{:S(2)}, u32[]{:S(2)}) collective-permute-start(f32[8,256]{1,0:T(8,128)S(1)} %collective-permute-done.1.refs_2_), channel_id=1, source_target_pairs={{0,1},{1,0},{2,3},{3,2},{4,5},{5,4},{6,7},{7,6},{8,9},{9,8},{10,11... | collective-permute-start | bytes 24584 | tf_op jit(solution)/shard_map/ppermute | solution.py:388
  19.2 4.4 %collective-permute-start.4 = (f32[8,256]{1,0:T(8,128)S(1)}, f32[8,256]{1,0:T(8,128)S(1)}, u32[]{:S(2)}, u32[]{:S(2)}) collective-permute-start(f32[8,256]{1,0:T(8,128)S(1)} %collective-permute-done.refs_1_), channel_id=1, source_target_pairs={{0,1},{1,0},{2,3},{3,2},{4,5},{5,4},{6,7},{7,6},{8,9},{9,8},{10,11... | collective-permute-start | bytes 24584 | tf_op jit(solution)/shard_map/ppermute | solution.py:388
  31.0 8.3 %collective-permute-start.14 = (f32[4,64,512]{2,1,0:T(8,128)S(1)}, f32[4,64,512]{2,1,0:T(8,128)S(1)}, u32[]{:S(2)}, u32[]{:S(2)}) collective-permute-start(f32[4,64,512]{2,1,0:T(8,128)S(1)} %get-tuple-element.47), channel_id=1, source_target_pairs={{0,1},{1,0},{2,3},{3,2},{4,5},{5,4},{6,7},{7,6},{8,9},{9,8},{10,11... | collective-permute-start | bytes 1572872 | tf_op jit(solution)/shard_map/ppermute | solution.py:388
  31.1 3.7 %collective-permute-start.9 = (f32[8,256]{1,0:T(8,128)S(1)}, f32[8,256]{1,0:T(8,128)S(1)}, u32[]{:S(2)}, u32[]{:S(2)}) collective-permute-start(f32[8,256]{1,0:T(8,128)S(1)} %get-tuple-element.43.refs_0_), channel_id=1, source_target_pairs={{0,6},{1,7},{2,0},{3,1},{4,2},{5,3},{6,4},{7,5},{8,14},{9,15},{10,... | collective-permute-start | bytes 24584 | tf_op jit(solution)/shard_map/ppermute | solution.py:384
  31.8 5.2 %collective-permute-start.8 = (f32[8,256]{1,0:T(8,128)S(1)}, f32[8,256]{1,0:T(8,128)S(1)}, u32[]{:S(2)}, u32[]{:S(2)}) collective-permute-start(f32[8,256]{1,0:T(8,128)S(1)} %get-tuple-element.43.refs_0_), channel_id=1, source_target_pairs={{0,4},{1,5},{2,6},{3,7},{4,0},{5,1},{6,2},{7,3},{8,12},{9,13},{10,... | collective-permute-start | bytes 24584 | tf_op jit(solution)/shard_map/ppermute | solution.py:384
  33.1 4.9 %collective-permute-start.7 = (f32[8,256]{1,0:T(8,128)S(1)}, f32[8,256]{1,0:T(8,128)S(1)}, u32[]{:S(2)}, u32[]{:S(2)}) collective-permute-start(f32[8,256]{1,0:T(8,128)S(1)} %get-tuple-element.43.refs_0_), channel_id=1, source_target_pairs={{0,2},{1,3},{2,4},{3,5},{4,6},{5,7},{6,0},{7,1},{8,10},{9,11},{10,... | collective-permute-start | bytes 24584 | tf_op jit(solution)/shard_map/ppermute | solution.py:384
  34.6 4.8 %collective-permute-start.10 = (f32[8,256]{1,0:T(8,128)S(1)}, f32[8,256]{1,0:T(8,128)S(1)}, u32[]{:S(2)}, u32[]{:S(2)}) collective-permute-start(f32[8,256]{1,0:T(8,128)S(1)} %get-tuple-element.43.refs_0_), channel_id=1, source_target_pairs={{0,1},{1,0},{2,3},{3,2},{4,5},{5,4},{6,7},{7,6},{8,9},{9,8},{10,11... | collective-permute-start | bytes 24584 | tf_op jit(solution)/shard_map/ppermute | solution.py:388
  34.8 4.5 %collective-permute-start.13 = (f32[8,256]{1,0:T(8,128)S(1)}, f32[8,256]{1,0:T(8,128)S(1)}, u32[]{:S(2)}, u32[]{:S(2)}) collective-permute-start(f32[8,256]{1,0:T(8,128)S(1)} %collective-permute-done.9.refs_3_), channel_id=1, source_target_pairs={{0,1},{1,0},{2,3},{3,2},{4,5},{5,4},{6,7},{7,6},{8,9},{9,8},{10,11... | collective-permute-start | bytes 24584 | tf_op jit(solution)/shard_map/ppermute | solution.py:388
  36.9 2.4 %collective-permute-start.12 = (f32[8,256]{1,0:T(8,128)S(1)}, f32[8,256]{1,0:T(8,128)S(1)}, u32[]{:S(2)}, u32[]{:S(2)}) collective-permute-start(f32[8,256]{1,0:T(8,128)S(1)} %collective-permute-done.8.refs_2_), channel_id=1, source_target_pairs={{0,1},{1,0},{2,3},{3,2},{4,5},{5,4},{6,7},{7,6},{8,9},{9,8},{10,11... | collective-permute-start | bytes 24584 | tf_op jit(solution)/shard_map/ppermute | solution.py:388
  38.0 1.3 %collective-permute-start.11 = (f32[8,256]{1,0:T(8,128)S(1)}, f32[8,256]{1,0:T(8,128)S(1)}, u32[]{:S(2)}, u32[]{:S(2)}) collective-permute-start(f32[8,256]{1,0:T(8,128)S(1)} %collective-permute-done.7.refs_1_), channel_id=1, source_target_pairs={{0,1},{1,0},{2,3},{3,2},{4,5},{5,4},{6,7},{7,6},{8,9},{9,8},{10,11... | collective-permute-start | bytes 24584 | tf_op jit(solution)/shard_map/ppermute | solution.py:388
  44.2 13.8 %all-to-all-start = ((f32[8,32,512]{2,1,0:T(8,128)}), f32[8,32,512]{2,1,0:T(8,128)S(1)}, u32[]{:S(2)}, u32[]{:S(2)}) async-start(f32[8,32,512]{2,1,0:T(8,128)} %get-tuple-element.48), calls=%async_computation | async-start | bytes 1048576 | tf_op jit(solution)/shard_map/all_to_all | solution.py:380
  54.4 12.3 %collective-permute-start.15 = (f32[4,64,512]{2,1,0:T(8,128)S(1)}, f32[4,64,512]{2,1,0:T(8,128)S(1)}, u32[]{:S(2)}, u32[]{:S(2)}) collective-permute-start(f32[4,64,512]{2,1,0:T(8,128)S(1)} %get-tuple-element.54), channel_id=1, source_target_pairs={{0,1},{1,0},{2,3},{3,2},{4,5},{5,4},{6,7},{7,6},{8,9},{9,8},{10,11... | collective-permute-start | bytes 1572872 | tf_op jit(solution)/shard_map/ppermute | solution.py:388
  55.0 13.5 %collective-permute-start.19 = (f32[64,512]{1,0:T(8,128)S(1)}, f32[64,512]{1,0:T(8,128)S(1)}, u32[]{:S(2)}, u32[]{:S(2)}) collective-permute-start(f32[64,512]{1,0:T(8,128)S(1)} %get-tuple-element.61), channel_id=1, source_target_pairs={{0,2},{1,3},{2,4},{3,5},{4,6},{5,7},{6,0},{7,1},{8,10},{9,11},{10,... | collective-permute-start | bytes 393224 | tf_op jit(solution)/shard_map/ppermute | solution.py:384
  58.7 20.9 %all-to-all-start.1 = ((f32[8,16,512]{2,1,0:T(8,128)}), f32[8,16,512]{2,1,0:T(8,128)S(1)}, u32[]{:S(2)}, u32[]{:S(2)}) async-start(f32[8,16,512]{2,1,0:T(8,128)} %get-tuple-element.52), calls=%async_computation.1 | async-start | bytes 524288 | tf_op jit(solution)/shard_map/all_to_all | solution.py:380
  62.1 17.4 %collective-permute-start.20 = (f32[64,512]{1,0:T(8,128)S(1)}, f32[64,512]{1,0:T(8,128)S(1)}, u32[]{:S(2)}, u32[]{:S(2)}) collective-permute-start(f32[64,512]{1,0:T(8,128)S(1)} %get-tuple-element.62), channel_id=1, source_target_pairs={{0,4},{1,5},{2,6},{3,7},{4,0},{5,1},{6,2},{7,3},{8,12},{9,13},{10,... | collective-permute-start | bytes 393224 | tf_op jit(solution)/shard_map/ppermute | solution.py:384
  65.6 14.0 %collective-permute-start.21 = (f32[64,512]{1,0:T(8,128)S(1)}, f32[64,512]{1,0:T(8,128)S(1)}, u32[]{:S(2)}, u32[]{:S(2)}) collective-permute-start(f32[64,512]{1,0:T(8,128)S(1)} %get-tuple-element.63), channel_id=1, source_target_pairs={{0,6},{1,7},{2,0},{3,1},{4,2},{5,3},{6,4},{7,5},{8,14},{9,15},{10,... | collective-permute-start | bytes 393224 | tf_op jit(solution)/shard_map/ppermute | solution.py:384
  66.8 12.8 %collective-permute-start.16 = (f32[64,512]{1,0:T(8,128)S(1)}, f32[64,512]{1,0:T(8,128)S(1)}, u32[]{:S(2)}, u32[]{:S(2)}) collective-permute-start(f32[64,512]{1,0:T(8,128)S(1)} %get-tuple-element.57), channel_id=1, source_target_pairs={{0,2},{1,3},{2,4},{3,5},{4,6},{5,7},{6,0},{7,1},{8,10},{9,11},{10,... | collective-permute-start | bytes 393224 | tf_op jit(solution)/shard_map/ppermute | solution.py:384
  67.7 11.8 %collective-permute-start.17 = (f32[64,512]{1,0:T(8,128)S(1)}, f32[64,512]{1,0:T(8,128)S(1)}, u32[]{:S(2)}, u32[]{:S(2)}) collective-permute-start(f32[64,512]{1,0:T(8,128)S(1)} %get-tuple-element.58), channel_id=1, source_target_pairs={{0,4},{1,5},{2,6},{3,7},{4,0},{5,1},{6,2},{7,3},{8,12},{9,13},{10,... | collective-permute-start | bytes 393224 | tf_op jit(solution)/shard_map/ppermute | solution.py:384
  68.5 11.1 %collective-permute-start.18 = (f32[64,512]{1,0:T(8,128)S(1)}, f32[64,512]{1,0:T(8,128)S(1)}, u32[]{:S(2)}, u32[]{:S(2)}) collective-permute-start(f32[64,512]{1,0:T(8,128)S(1)} %get-tuple-element.59), channel_id=1, source_target_pairs={{0,6},{1,7},{2,0},{3,1},{4,2},{5,3},{6,4},{7,5},{8,14},{9,15},{10,... | collective-permute-start | bytes 393224 | tf_op jit(solution)/shard_map/ppermute | solution.py:384
  71.0 8.6 %copy-start.1 = (bf16[128,512]{1,0:T(8,128)(2,1)S(1)}, bf16[128,512]{1,0:T(8,128)(2,1)}, u32[]{:S(2)}) copy-start(bf16[128,512]{1,0:T(8,128)(2,1)} %refs_9_.1) | copy-start | bytes 393220
  71.0 8.6 %copy-start.2 = (bf16[128,512]{1,0:T(8,128)(2,1)S(1)}, bf16[128,512]{1,0:T(8,128)(2,1)}, u32[]{:S(2)}) copy-start(bf16[128,512]{1,0:T(8,128)(2,1)} %refs_11_.1) | copy-start | bytes 393220
  71.0 16.9 %copy-start = (bf16[512,512]{1,0:T(8,128)(2,1)S(1)}, bf16[512,512]{1,0:T(8,128)(2,1)}, u32[]{:S(2)}) copy-start(bf16[512,512]{1,0:T(8,128)(2,1)} %wq_ref.1) | copy-start | bytes 1572868
  80.8 18.2 %all-to-all-start.2 = ((f32[16,16,512]{2,1,0:T(8,128)}), f32[16,16,512]{2,1,0:T(8,128)S(1)}, u32[]{:S(2)}, u32[]{:S(2)}) async-start(f32[16,16,512]{2,1,0:T(8,128)} %shard_map.122.token_ref), calls=%async_computation.2 | async-start | bytes 1048576 | tf_op jit(solution)/shard_map/all_to_all | solution.py:380
where the time goes:
time: 100 us; the launch traced here: 99.6 us
  Pallas kernels  44.6 us (45%)
  starting transfers between devices  35 us (35%)
  waiting for transfers between devices  17.1 us (17%)
  local copies, waits for them, and re-layouts  1.93 us (2%)
    pallas_call x13, Pallas kernels, call(): pl.pallas_call(kernel, in_specs=[specs[s] for _, s in args], out_specs=[s...  44.6 us
    ppermute x12, starting transfers between devices, up(): return lax.ppermute(x, 'seq', [(i, (i + 2 * chips) % 8) for i in range(8)])  19.3 us
    all_to_all x3, starting transfers between devices, swap(): return lax.all_to_all(x, axis, 0, 0)  13.9 us
    all_to_all x3, waiting for transfers between devices, swap(): return lax.all_to_all(x, axis, 0, 0)  10.4 us
    ppermute x12, waiting for transfers between devices, up(): return lax.ppermute(x, 'seq', [(i, (i + 2 * chips) % 8) for i in range(8)])  6.7 us
  transfers between devices with their start and end apart: 25, of which 7 were waited for; matrix products, arithmetic and copies ran while one was open for 1% of the time, Pallas kernels for 23%

commit v1 on v0

v1 whole, which is shorter than its diff:
```python
import jax
import jax.numpy as jnp
from jax import lax
from jax.experimental import pallas as pl
from jax.experimental.pallas import tpu as pltpu
from jax.sharding import PartitionSpec as P

PAIRS = 4
LOW = -1e30
F32 = jnp.float32
BF16 = jnp.bfloat16
VMEM = pltpu.MemorySpace.VMEM
HBM = pltpu.MemorySpace.HBM
TILE = 1024


def dot(left, right):
    return jnp.dot(left, right, preferred_element_type=F32)


def dot_last(left, right):
    return lax.dot_general(left, right, (((1,), (1,)), ((), ())), preferred_element_type=F32)


def dot_first(left, right):
    return lax.dot_general(left, right, (((0,), (0,)), ((), ())), preferred_element_type=F32)


def tiles(ref):
    events = ref.shape[1]
    return [slice(start, start + TILE) for start in range(0, events, TILE)]


def pair_cols(ref, pair, rows):
    cols = slice(128 * pair, 128 * pair + 128)
    return jnp.concatenate([ref[0, rows, cols], ref[1, rows, cols]], axis=1)


def put_pair(ref, pair, rows, value):
    cols = slice(128 * pair, 128 * pair + 128)
    ref[0, rows, cols] = value[:, 0:128]
    ref[1, rows, cols] = value[:, 128:256]


def pair_lanes(pair):
    return slice(256 * pair, 256 * pair + 256)


def seen_in(lim_ref, rows):
    place = lax.broadcasted_iota(jnp.int32, (TILE, 256), 0) + rows.start
    return place < lim_ref[0:1]


def spread(full, own_col, owner_row, blk_ref, blk_t_ref):
    lane = lax.broadcasted_iota(jnp.int32, (128, 128), 1)
    zero = jnp.zeros((64, 128), F32)
    for pair in range(PAIRS):
        part = full[:, 128 * pair : 128 * pair + 128]
        part_t = part.T
        for req in range(2):
            mine = jnp.where(own_col == req, part, 0.0)
            cols = slice(128 * req, 128 * req + 128)
            blk_t_ref[pair, 0:128, cols] = jnp.where(lane < 64, mine, 0.0).astype(BF16)
            blk_t_ref[pair, 128:256, cols] = jnp.where(lane < 64, 0.0, mine).astype(BF16)
            mine_t = jnp.where(owner_row == req, part_t, 0.0)
            top = jnp.concatenate([mine_t[0:64], zero], axis=1)
            low = jnp.concatenate([zero, mine_t[64:128]], axis=1)
            blk_ref[pair, cols, :] = jnp.concatenate([top, low], axis=0).astype(BF16)


def keys_kernel(lens_hbm, own_hbm, tok_hbm, wq_hbm, wk_hbm, hist_hbm,
                key_ref, hist_ref, stat_ref, lim_ref, qb_ref, own_ref, qbt_ref,
                lens_ref, tok_ref, wq_ref, wk_ref, sems):
    small = [(wq_hbm, wq_ref), (tok_hbm, tok_ref), (own_hbm, own_ref), (lens_hbm, lens_ref),
             (wk_hbm, wk_ref)]
    small = [pltpu.make_async_copy(src, dst, sems.at[i]) for i, (src, dst) in enumerate(small)]
    for copy in small:
        copy.start()
    chunks = []
    for rows in tiles(hist_ref):
        for req in range(2):
            copy = pltpu.make_async_copy(
                hist_hbm.at[req, rows], hist_ref.at[req, rows], sems.at[5 + len(chunks)])
            copy.start()
            chunks.append(copy)
    for copy in small[0:4]:
        copy.wait()
    owner_row = jnp.broadcast_to(own_ref[...], (128, 128))
    base = lax.axis_index("seq") * hist_ref.shape[1]
    lim = jnp.where(own_ref[...] == 0, lens_ref[0], lens_ref[1]) - base
    lim_ref[...] = jnp.broadcast_to(jnp.concatenate([lim, lim], axis=1), (8, 256))
    q = dot(tok_ref[...], wq_ref[...]).astype(BF16).astype(F32) * 0.125
    spread(q, owner_row.T, owner_row[0:1], qb_ref, qbt_ref)
    small[4].wait()
    for index, rows in enumerate(tiles(hist_ref)):
        for req in range(2):
            chunks[2 * index + req].wait()
            key_ref[req, rows] = dot(hist_ref[req, rows], wk_ref[...]).astype(BF16)
    tops, sums = [], []
    for pair in range(PAIRS):
        tops.append([])
        sums.append([])
    for rows in tiles(hist_ref):
        seen = seen_in(lim_ref, rows)
        for pair in range(PAIRS):
            score = jnp.where(seen, dot(pair_cols(key_ref, pair, rows), qb_ref[pair]), LOW)
            top = jnp.max(score, axis=0, keepdims=True)
            tops[pair].append(top)
            sums[pair].append(jnp.sum(jnp.exp(score - top), axis=0, keepdims=True))
    peaks, totals = [], []
    for pair in range(PAIRS):
        peak = tops[pair][0]
        for top in tops[pair][1:]:
            peak = jnp.maximum(peak, top)
        peaks.append(peak)
        totals.append(sum(x * jnp.exp(top - peak) for x, top in zip(sums[pair], tops[pair])))
    stat_ref[...] = jnp.concatenate(peaks + totals, axis=0)


def values_kernel(wv_ref, hist_ref, val_ref):
    for rows in tiles(hist_ref):
        for req in range(2):
            val_ref[req, rows] = dot(hist_ref[req, rows], wv_ref[...]).astype(BF16)


def join_stats_kernel(*refs):
    stats, out_ref = refs[0:4], refs[-1]
    top = stats[0][0:4]
    for stat in stats[1:]:
        top = jnp.maximum(top, stat[0:4])
    norm = jnp.zeros((4, 256), F32)
    for stat in stats:
        norm += stat[4:8] * jnp.exp(stat[0:4] - top)
    out_ref[...] = jnp.concatenate([top, norm], axis=0)


def join_deltas_kernel(*refs):
    refs[-1][...] = refs[0][...] + refs[1][...] + refs[2][...] + refs[3][...]


def out_grads_kernel(dout_ref, wout_ref, own_ref, token_ref, gb_ref, gbt_ref):
    owner_row = jnp.broadcast_to(own_ref[...], (128, 128))
    g = dot_last(dout_ref[...], wout_ref[...]).astype(BF16).astype(F32)
    spread(g, owner_row.T, owner_row[0:1], gb_ref, gbt_ref)


def probs_kernel(one_ref, two_ref, lim_ref, qb_ref, gb_ref, key_ref, val_ref, prob_ref, delta_ref):
    one, two = one_ref[0:4], two_ref[0:4]
    top = jnp.maximum(one, two)
    norm = one_ref[4:8] * jnp.exp(one - top) + two_ref[4:8] * jnp.exp(two - top)
    shift = top + jnp.log(norm)
    delta = [jnp.zeros((1, 256), F32) for _ in range(PAIRS)]
    for rows in tiles(key_ref):
        seen = seen_in(lim_ref, rows)
        for pair in range(PAIRS):
            score = dot(pair_cols(key_ref, pair, rows), qb_ref[pair])
            prob = jnp.where(seen, jnp.exp(score - shift[pair : pair + 1]), 0.0).astype(BF16)
            prob_ref[rows, pair_lanes(pair)] = prob
            slope = dot(pair_cols(val_ref, pair, rows), gb_ref[pair])
            delta[pair] += jnp.sum(prob.astype(F32) * slope, axis=0, keepdims=True)
    delta_ref[...] = jnp.concatenate(delta + [jnp.zeros((4, 256), F32)], axis=0)


def put_shares(out_ref, value):
    for row in range(0, 512, 4):
        dp, seq = row // 32, (row // 4) % 8
        out_ref[seq, 4 * dp : 4 * dp + 4] = value[row : row + 4]


def put_shares(out_ref, value):
    for row in range(0, 512, 4):
        dp, seq = row // 32, (row // 4) % 8
        out_ref[seq, 4 * dp : 4 * dp + 4] = value[row : row + 4]


def halve(shares, keep_ref, send_ref, rows):
    me = lax.axis_index("seq")
    for slot in range(4):
        chip = lax.rem(me // 2 + slot, 4)
        keep_ref[slot, rows] = shares[2 * chip + lax.rem(me, 2)]
        send_ref[slot, rows] = shares[2 * chip + 1 - lax.rem(me, 2)]


def value_grads_kernel(prob_ref, hist_ref, gbt_ref, dv_ref, share_ref, wgrad):
    for rows in tiles(hist_ref):
        for pair in range(PAIRS):
            grad = dot(prob_ref[rows, pair_lanes(pair)], gbt_ref[pair]).astype(BF16)
            put_pair(dv_ref, pair, rows, grad)
    wgrad[...] = dot_first(hist_ref[0], dv_ref[0])
    wgrad[...] += dot_first(hist_ref[1], dv_ref[1])
    put_shares(share_ref, wgrad)


def attention_kernel(own_ref, prob_ref, val_ref, token_ref, att_ref):
    first = own_ref[...] == 0
    for pair in range(PAIRS):
        blk = jnp.zeros((256, 256), F32)
        for rows in tiles(val_ref):
            blk += dot_first(pair_cols(val_ref, pair, rows), prob_ref[rows, pair_lanes(pair)])
        for head in range(2):
            lanes = slice(128 * head, 128 * head + 128)
            one = blk[64 * head : 64 * head + 64, lanes]
            two = blk[128 + 64 * head : 192 + 64 * head, lanes]
            out = jnp.where(first, one, two)
            for row in range(0, 64, 4):
                feature = 128 * pair + 64 * head + row
                dp, seq = feature // 32, (feature // 4) % 8
                start = 4 * (dp % 4)
                att_ref[seq, start : start + 4, 128 * (dp // 4) : 128 * (dp // 4) + 128] = (
                    out[row : row + 4])


def query_part_kernel(one_ref, two_ref, own_ref, prob_ref, key_ref, val_ref, gb_ref, att_ref,
                      share_ref, ds_ref, keep_ref, send_ref, dq_ref):
    delta = one_ref[...] + two_ref[...]
    own_col = jnp.broadcast_to(own_ref[...], (128, 128)).T
    lane = lax.broadcasted_iota(jnp.int32, (128, 128), 1)
    blks = [jnp.zeros((256, 256), F32) for _ in range(PAIRS)]
    for rows in tiles(key_ref):
        for pair in range(PAIRS):
            prob = prob_ref[rows, pair_lanes(pair)].astype(F32)
            slope = dot(pair_cols(val_ref, pair, rows), gb_ref[pair])
            ds = (prob * (slope - delta[pair : pair + 1])).astype(BF16)
            ds_ref[rows, pair_lanes(pair)] = ds
            blks[pair] += dot_first(ds, pair_cols(key_ref, pair, rows))
    for pair in range(PAIRS):
        blk = blks[pair]
        one = jnp.where(own_col == 0, blk[:128, :128], blk[:128, 128:])
        two = jnp.where(own_col == 0, blk[128:, :128], blk[128:, 128:])
        dq = jnp.where(lane < 64, one, two)
        for dev in range(8):
            dq_ref[dev, :, 128 * pair : 128 * pair + 128] = dq[16 * dev : 16 * dev + 16]
    halve(share_ref, keep_ref, send_ref, slice(0, 64))
    halve(dq_ref, keep_ref, send_ref, slice(64, 80))
    halve(att_ref, keep_ref, send_ref, slice(80, 96))


def key_grads_kernel(ds_ref, qbt_ref, dk_ref):
    for rows in tiles(dk_ref):
        for pair in range(PAIRS):
            grad = dot(ds_ref[rows, pair_lanes(pair)], qbt_ref[pair]).astype(BF16)
            put_pair(dk_ref, pair, rows, grad)


def key_weight_kernel(hist_ref, dk_ref, token_ref, keep_ref, send_ref, wgrad, shares):
    wgrad[...] = dot_first(hist_ref[0], dk_ref[0])
    wgrad[...] += dot_first(hist_ref[1], dk_ref[1])
    put_shares(shares, wgrad)
    halve(shares, keep_ref, send_ref, slice(0, 64))


def join_halves_kernel(keep_ref, recv_ref, token_ref, *parts):
    for slot, part in enumerate(parts):
        part[...] = keep_ref[slot] + recv_ref[slot]


def gather_kernel(part0, part1, part2, part3, send_ref, wv_ref, dq_ref, att_ref, same_ref):
    summed = part0[...] + part1[...] + part2[...] + part3[...]
    wv_ref[...] = summed[0:64]
    dq_ref[...] = summed[64:80]
    for quarter in range(4):
        lanes = slice(128 * quarter, 128 * quarter + 128)
        att_ref[16 * quarter : 16 * quarter + 16] = summed[80:96, lanes]


def join_keys_kernel(keep_ref, recv_ref, mine_ref, other_ref, *parts):
    even = lax.rem(lax.axis_index("seq"), 2) == 0
    mine, other = mine_ref[...], other_ref[...]
    for slot, part in enumerate(parts):
        part[0:64] = keep_ref[slot] + recv_ref[slot]
        part[64:80] = jnp.where(even, mine, other)
        part[80:96] = jnp.where(even, other, mine)


def hist_grads(req, dk_ref, dv_ref, wk_ref, wv_ref, out_hbm, done_ref, buf, sems):
    copies = []
    for start in range(0, buf.shape[0], 512):
        rows = slice(start, start + 512)
        buf[rows] = (dot_last(dk_ref[req, rows], wk_ref[...])
                     + dot_last(dv_ref[req, rows], wv_ref[...])).astype(BF16)
        copy = pltpu.make_async_copy(buf.at[rows], out_hbm.at[req, rows], sems.at[len(copies)])
        copy.start()
        copies.append(copy)
    done_ref[...] = jnp.zeros(done_ref.shape, F32)
    for copy in copies:
        copy.wait()


def hist_grads_first_kernel(dk_ref, dv_ref, wk_ref, wv_ref, token_ref, *refs):
    hist_grads(0, dk_ref, dv_ref, wk_ref, wv_ref, *refs)


def hist_grads_second_kernel(dk_ref, dv_ref, wk_ref, wv_ref, token_ref, in_hbm, *refs):
    hist_grads(1, dk_ref, dv_ref, wk_ref, wv_ref, *refs)


def outer_kernel(*refs):
    keys = refs[0:4]
    wv_ref, tok_ref, att_ref, dout_ref, token_ref = refs[4:9]
    outs, (low_ref, dq_ref, all_ref) = refs[9:13], refs[13:]
    me = lax.axis_index("seq")
    for chips, part in enumerate(keys):
        dq_ref[lax.rem(me // 2 + 4 - chips, 4)] = part[64:96]
    dq = (dq_ref[...].reshape(128, 512) * 0.125).astype(BF16)
    low_ref[...] = dq
    row = lax.broadcasted_iota(jnp.int32, (64, 512), 0)
    col = lax.broadcasted_iota(jnp.int32, (64, 512), 1)
    feature = (row // 4) * 32 + me * 4 + row % 4
    pick = jnp.where(col == feature, 1.0, 0.0).astype(BF16)
    tok = dot_last(pick, tok_ref[...]).astype(BF16)
    parts = [dot(tok, dq),
             keys[0][0:64] + keys[1][0:64] + keys[2][0:64] + keys[3][0:64],
             wv_ref[...],
             dot(att_ref[...].astype(BF16), dout_ref[...])]
    for dp in range(16):
        for part in range(4):
            all_ref[dp, 4 * part : 4 * part + 4] = parts[part][4 * dp : 4 * dp + 4]
    y = lax.axis_index("dp") // 4
    for chips, out in enumerate(outs):
        out[...] = all_ref[pl.ds(4 * lax.rem(y + chips, 4), 4)]


def join_y_kernel(*refs):
    parts, outs, (sum_ref,) = refs[0:4], refs[5:9], refs[9:]
    sum_ref[...] = parts[0][...] + parts[1][...] + parts[2][...] + parts[3][...]
    x = lax.rem(lax.axis_index("dp"), 4)
    for chips, out in enumerate(outs):
        out[...] = sum_ref[lax.rem(x + chips, 4)]


def query_grad_kernel(dq_ref, wq_ref, out_ref):
    out_ref[...] = dot_last(dq_ref[...], wq_ref[...]).astype(BF16)


def final_kernel(part0, part1, part2, part3, out_ref):
    summed = part0[...] + part1[...] + part2[...] + part3[...]
    for part in range(4):
        out_ref[:, part, :] = summed[4 * part : 4 * part + 4]


IN_VMEM = pl.BlockSpec(memory_space=VMEM)
IN_HBM = pl.BlockSpec(memory_space=pl.ANY)


def call(kernel, args, outs, scratch=(), aliases=(), limit=26):
    specs = {"vmem": IN_VMEM, "hbm": IN_HBM}
    spaces = {"vmem": VMEM, "hbm": HBM}
    ins = [pltpu.with_memory_space_constraint(x, spaces[s]) for x, s in args]
    return pl.pallas_call(
        kernel,
        in_specs=[specs[s] for _, s in args],
        out_specs=[specs[s] for s, _, _ in outs],
        out_shape=[spaces[s](shape, dtype) for s, dtype, shape in outs],
        scratch_shapes=scratch,
        input_output_aliases=dict(aliases),
        compiler_params=pltpu.CompilerParams(vmem_limit_bytes=limit * 1024 * 1024),
    )(*ins)


def turn(x, to):
    return lax.ppermute(x, "dp", [(i, to(i // 4, i % 4)) for i in range(16)])


def up(x, chips):
    return lax.ppermute(x, "seq", [(i, (i + 2 * chips) % 8) for i in range(8)])


def across(x):
    return lax.ppermute(x, "seq", [(i, i ^ 1) for i in range(8)])


def from_chips(x):
    return [x] + [up(x, chips) for chips in (1, 2, 3)]


def per_device(query_tokens, owner, d_out, history, lengths, w_query, w_key, w_value, w_out):
    rows, width = query_tokens.shape
    requests, events, _ = history.shape
    steps = events // TILE
    ev = (requests, events, width)
    mat = (width, width)
    blk = (PAIRS, 256, 256)
    vec = ("vmem", F32, (8, 256))
    pairs = (events, 256 * PAIRS)
    half = ("vmem", F32, (4, 64, width))
    quarter = ("vmem", F32, (64, width))
    wide_half = ("vmem", F32, (4, 96, width))
    wide = ("vmem", F32, (96, width))
    dma = pltpu.SemaphoreType.DMA
    v = lambda *xs: [(x, "vmem") for x in xs]
    h = lambda *xs: [(x, "hbm") for x in xs]

    keys, hist, stats, lim, qb, own, qbt = call(
        keys_kernel,
        h(lengths, owner.reshape(1, rows), query_tokens, w_query, w_key, history),
        [("vmem", BF16, ev), ("vmem", BF16, ev), vec, ("vmem", jnp.int32, (8, 256)),
         ("vmem", BF16, blk), ("vmem", jnp.int32, (1, rows)), ("vmem", BF16, blk)],
        [pltpu.SMEM((requests,), jnp.int32), pltpu.VMEM((rows, width), BF16),
         pltpu.VMEM(mat, BF16), pltpu.VMEM(mat, BF16), dma((5 + 2 * steps,))],
    )
    stats = from_chips(stats)
    (values,) = call(values_kernel, v(w_value, hist), [("vmem", BF16, ev)])
    (stats,) = call(join_stats_kernel, v(*stats, values), [vec])
    gb, gbt = call(
        out_grads_kernel, v(d_out, w_out, own, stats), [("vmem", BF16, blk), ("vmem", BF16, blk)])
    probs, delta = call(
        probs_kernel, v(stats, across(stats), lim, qb, gb, keys, values),
        [("vmem", BF16, pairs), vec])
    delta = from_chips(delta)
    dv, share = call(
        value_grads_kernel, v(probs, hist, gbt), [("vmem", BF16, ev), ("vmem", F32, (8, 64, width))],
        [pltpu.VMEM(mat, F32)])
    (delta,) = call(join_deltas_kernel, v(*delta, dv), [vec])
    (att,) = call(
        attention_kernel, v(own, probs, values, delta), [("vmem", F32, (8, 16, width))])

    ds, keep, send = call(
        query_part_kernel, v(delta, across(delta), own, probs, keys, values, gb, att, share),
        [("vmem", BF16, pairs), wide_half, wide_half], [pltpu.VMEM((8, 16, width), F32)])
    (dk,) = call(key_grads_kernel, v(ds, qbt), [("vmem", BF16, ev)])
    parts = call(join_halves_kernel, v(keep, across(send), dk), [wide] * 4)
    token = parts[0]
    parts = [parts[0]] + [up(parts[i], i) for i in (1, 2, 3)]
    keep, send = call(
        key_weight_kernel, v(hist, dk, token), [half, half],
        [pltpu.VMEM(mat, F32), pltpu.VMEM((8, 64, width), F32)])
    wgrad_v, dq, att, send = call(
        gather_kernel, v(*parts, send),
        [quarter, ("vmem", F32, (16, width)), ("vmem", F32, (64, rows)), half], aliases={4: 3})
    parts = call(join_keys_kernel, v(keep, across(send), dq, across(dq)), [wide] * 4)
    token = parts[0]
    parts = [parts[0]] + [up(parts[i], i) for i in (1, 2, 3)]
    grad_out = [("hbm", BF16, ev), ("vmem", F32, (8, 128))]
    grad_scratch = [pltpu.VMEM((events, width), BF16), dma((events // 512,))]
    hist_grad, token = call(
        hist_grads_first_kernel, v(dk, dv, w_key, w_value, token), grad_out, grad_scratch)
    *outer, dq = call(
        outer_kernel, v(*parts, wgrad_v, query_tokens, att, d_out, token),
        [("vmem", F32, (4, 16, width))] * 4 + [("vmem", BF16, (rows, width))],
        [pltpu.VMEM((4, 32, width), F32), pltpu.VMEM((16, 16, width), F32)])
    outer = [outer[0]] + [turn(outer[i], lambda y, x: (y + i) % 4 * 4 + x) for i in (1, 2, 3)]
    hist_grad, token = call(
        hist_grads_second_kernel, v(dk, dv, w_key, w_value, dq) + h(hist_grad), grad_out,
        grad_scratch, aliases={5: 0})
    outer = call(
        join_y_kernel, v(*outer, token), [("vmem", F32, (16, width))] * 4,
        [pltpu.VMEM((4, 16, width), F32)])
    outer = [outer[0]] + [turn(outer[i], lambda y, x: y * 4 + (x + i) % 4) for i in (1, 2, 3)]
    (query_grad,) = call(
        query_grad_kernel, v(dq, w_query), [("vmem", BF16, (rows, width))])
    (weight_part,) = call(final_kernel, v(*outer), [("vmem", F32, (4, 4, width))])
    return query_grad, hist_grad, weight_part


def solution(mesh):
    return jax.shard_map(
        per_device,
        mesh=mesh,
        in_specs=(
            P("dp", None),
            P("dp"),
            P("dp", None),
            P("dp", "seq", None),
            P("dp"),
            P(),
            P(),
            P(),
            P(),
        ),
        out_specs=(P("dp", None), P("dp", "seq", None), P(("dp", "seq"), None, None)),
        check_vma=False,
    )
```

time: 100 us -> 85 us (0.85)
  Pallas kernels: 44.6 us -> 31.7 us
  starting transfers between devices: 35 us -> 30.7 us
  waiting for transfers between devices: 17.1 us -> 19.5 us
    all_to_all x3 -> x0, starting transfers between devices: 13.9 us -> none  [swap(): return lax.all_to_all(x, axis, 0, 0)]
    pallas_call x13 -> x20, Pallas kernels: 44.6 us -> 31.7 us  [call(): pl.pallas_call(kernel, in_specs=[specs[s] for _, s in args], out_specs=[s...]
    ppermute x0 -> x6, starting transfers between devices: none -> 11.6 us  [turn(): return lax.ppermute(x, 'dp', [(i, to(i // 4, i % 4)) for i in range(16)])]
    all_to_all x3 -> x0, waiting for transfers between devices: 10.4 us -> none  [swap(): return lax.all_to_all(x, axis, 0, 0)]
    ppermute x12, waiting for transfers between devices: 6.7 us -> 13.9 us  [up(): return lax.ppermute(x, 'seq', [(i, (i + 2 * chips) % 8) for i in range(8)])]
    ppermute x10 -> x5, waiting for transfers between devices: 0.03 us -> 3.12 us  [across(): return lax.ppermute(x, 'seq', [(i, i ^ 1) for i in range(8)])]
    ppermute x0 -> x6, waiting for transfers between devices: none -> 2.45 us  [turn(): return lax.ppermute(x, 'dp', [(i, to(i // 4, i % 4)) for i in range(16)])]
    ppermute x10 -> x5, starting transfers between devices: 1.78 us -> 0.76 us  [across(): return lax.ppermute(x, 'seq', [(i, i ^ 1) for i in range(8)])]
  transfers between devices with their start and end apart: 25 -> 23, of which waited for: 7 -> 13; matrix products, arithmetic and copies ran while one was open for 1% -> 1% of each run, Pallas kernels for 23% -> 21%
where the time goes in v1:
time: 85 us; the launch traced here: 84.9 us
  Pallas kernels  31.7 us (37%)
  starting transfers between devices  30.7 us (36%)
  waiting for transfers between devices  19.5 us (23%)
  local copies, waits for them, and re-layouts  2.17 us (3%)
  between operations  0.91 us (1%)
    pallas_call x20, Pallas kernels, call(): pl.pallas_call(kernel, in_specs=[specs[s] for _, s in args], out_specs=[s...  31.7 us
    ppermute x12, starting transfers between devices, up(): return lax.ppermute(x, 'seq', [(i, (i + 2 * chips) % 8) for i in range(8)])  18.3 us
    ppermute x12, waiting for transfers between devices, up(): return lax.ppermute(x, 'seq', [(i, (i + 2 * chips) % 8) for i in range(8)])  13.9 us
    ppermute x6, starting transfers between devices, turn(): return lax.ppermute(x, 'dp', [(i, to(i // 4, i % 4)) for i in range(16)])  11.6 us
    ppermute x5, waiting for transfers between devices, across(): return lax.ppermute(x, 'seq', [(i, i ^ 1) for i in range(8)])  3.12 us
    ppermute x6, waiting for transfers between devices, turn(): return lax.ppermute(x, 'dp', [(i, to(i // 4, i % 4)) for i in range(16)])  2.45 us
    unnamed x18, local copies, waits for them, and re-layouts  2.17 us
  transfers between devices with their start and end apart: 23, of which 13 were waited for; matrix products, arithmetic and copies ran while one was open for 1% of the time, Pallas kernels for 21%

profile of v1, /device:TPU:0, one launch (start us, length us, event | category | flops | bytes accessed | tf_op | source)
XLA Modules:
  0.0 84.9 jit_solution(9689939101142574469)
XLA Ops:
  0.6 7.2 %shard_map.112 = (bf16[2,2048,512]{2,1,0:T(8,128)(2,1)S(1)}, bf16[2,2048,512]{2,1,0:T(8,128)(2,1)S(1)}, f32[8,256]{1,0:T(8,128)S(1)}, s32[8,256]{1,0:T(8,128)S(1...) custom-call(s32[2]{0:T(128)} %lens_hbm.1, s32[1,128]{1,0:T(1,128)} %bitcast.1, ...), custom_call_target="tpu_custom_call" | custom-call | tf_op jit(solution)/shard_map/pallas_call | solution.py:349
  7.9 4.2 %collective-permute-start.2 = (f32[8,256]{1,0:T(8,128)S(1)}, f32[8,256]{1,0:T(8,128)S(1)}, u32[]{:S(2)}, u32[]{:S(2)}) collective-permute-start(f32[8,256]{1,0:T(8,128)S(1)} %get-tuple-element.47.refs_0_), channel_id=1, source_target_pairs={{0,6},{1,7},{2,0},{3,1},{4,2},{5,3},{6,4},{7,5},{8,14},{9,15},{10,... | collective-permute-start | bytes 24584 | tf_op jit(solution)/shard_map/ppermute | solution.py:365
  12.1 1.3 %collective-permute-start = (f32[8,256]{1,0:T(8,128)S(1)}, f32[8,256]{1,0:T(8,128)S(1)}, u32[]{:S(2)}, u32[]{:S(2)}) collective-permute-start(f32[8,256]{1,0:T(8,128)S(1)} %get-tuple-element.47.refs_0_), channel_id=1, source_target_pairs={{0,2},{1,3},{2,4},{3,5},{4,6},{5,7},{6,0},{7,1},{8,10},{9,11},{10,... | collective-permute-start | bytes 24584 | tf_op jit(solution)/shard_map/ppermute | solution.py:365
  13.3 2.3 %shard_map.113.refs_4_.val_ref = bf16[2,2048,512]{2,1,0:T(8,128)(2,1)S(1)} custom-call(bf16[512,512]{1,0:T(8,128)(2,1)S(1)} %copy-done.3, bf16[2,2048,512]{2,1,0:T(8,128)(2,1)S(1)} %get-tuple-element.46.hist_ref), custom_call_target="tpu_custom_call" | custom-call | tf_op jit(solution)/shard_map/pallas_call | solution.py:349
  15.7 1.5 %collective-permute-done.1.refs_2_ = f32[8,256]{1,0:T(8,128)S(1)} collective-permute-done((f32[8,256]{1,0:T(8,128)S(1)}, f32[8,256]{1,0:T(8,128)S(1)}, u32[]{:S(2)}, u32[]{:S(2)}) %collective-permute-start.1) | collective-permute-done | bytes 8224 | tf_op jit(solution)/shard_map/ppermute | solution.py:365
  18.5 3.0 %shard_map.116 = (bf16[2048,1024]{1,0:T(8,128)(2,1)S(1)}, f32[8,256]{1,0:T(8,128)S(1)}) custom-call(f32[8,256]{1,0:T(8,128)S(1)} %shard_map.114.token_ref.one_ref, f32[8,256]{1,0:T(8,128)S(1)} %collective-permute-done.3.two_ref, s32[8,256]{1,0:T(8,128)S(1)} %get-tuple-element.48.lim_ref, bf16[4,256,256]{2,1,0:T(8,128)(2,1)S(1)} %get-tuple-element.49.qb_ref, ...), custom_call_target="tpu_custom_call" | custom-call | tf_op jit(solution)/shard_map/pallas_call | solution.py:349
  22.3 2.3 %collective-permute-start.5 = (f32[8,256]{1,0:T(8,128)S(1)}, f32[8,256]{1,0:T(8,128)S(1)}, u32[]{:S(2)}, u32[]{:S(2)}) collective-permute-start(f32[8,256]{1,0:T(8,128)S(1)} %get-tuple-element.53.refs_0_), channel_id=1, source_target_pairs={{0,4},{1,5},{2,6},{3,7},{4,0},{5,1},{6,2},{7,3},{8,12},{9,13},{10,... | collective-permute-start | bytes 24584 | tf_op jit(solution)/shard_map/ppermute | solution.py:365
  25.0 3.5 %shard_map.117 = (bf16[2,2048,512]{2,1,0:T(8,128)(2,1)S(1)}, f32[8,64,512]{2,1,0:T(8,128)S(1)}) custom-call(bf16[2048,1024]{1,0:T(8,128)(2,1)S(1)} %get-tuple-element.54.prob_ref, bf16[2,2048,512]{2,1,0:T(8,128)(2,1)S(1)} %get-tuple-element.46.hist_ref, bf16[4,256,256]{2,1,0:T(8,128)(2,1)S(1)} %get-tuple-element.55.gbt_ref), custom_call_target="tpu_custom_call" | custom-call | tf_op jit(solution)/shard_map/pallas_call | solution.py:349
  28.6 0.9 %collective-permute-done.4.refs_1_ = f32[8,256]{1,0:T(8,128)S(1)} collective-permute-done((f32[8,256]{1,0:T(8,128)S(1)}, f32[8,256]{1,0:T(8,128)S(1)}, u32[]{:S(2)}, u32[]{:S(2)}) %collective-permute-start.4) | collective-permute-done | bytes 8224 | tf_op jit(solution)/shard_map/ppermute | solution.py:365
  29.5 1.3 %shard_map.119.att_ref = f32[8,16,512]{2,1,0:T(8,128)S(1)} custom-call(s32[1,128]{1,0:T(1,128)S(1)} %get-tuple-element.50.own_ref, bf16[2048,1024]{1,0:T(8,128)(2,1)S(1)} %get-tuple-element.54.prob_ref, bf16[2,2048,512]{2,1,0:T(8,128)(2,1)S(1)} %shard_map.113.refs_4_.val_ref, f32[8,256]{1,0:T(8,128)S(1)} %shard_map.118.token_ref.one_ref), custom_call_target="tpu_custom_call" | custom-call | tf_op jit(solution)/shard_map/pallas_call | solution.py:349
  31.6 2.7 %shard_map.120 = (bf16[2048,1024]{1,0:T(8,128)(2,1)S(1)}, f32[4,96,512]{2,1,0:T(8,128)S(1)}, f32[4,96,512]{2,1,0:T(8,128)S(1)}) custom-call(f32[8,256]{1,0:T(8,128)S(1)} %shard_map.118.token_ref.one_ref, f32[8,256]{1,0:T(8,128)S(1)} %collective-permute-done.7.two_ref, s32[1,128]{1,0:T(1,128)S(1)} %get-tuple-element.50.own_ref, ...), custom_call_target="tpu_custom_call" | custom-call | tf_op jit(solution)/shard_map/pallas_call | solution.py:349
  34.4 1.3 %shard_map.121.token_ref.dk_ref = bf16[2,2048,512]{2,1,0:T(8,128)(2,1)S(1)} custom-call(bf16[2048,1024]{1,0:T(8,128)(2,1)S(1)} %get-tuple-element.58.ds_ref, bf16[4,256,256]{2,1,0:T(8,128)(2,1)S(1)} %get-tuple-element.59.qbt_ref), custom_call_target="tpu_custom_call" | custom-call | tf_op jit(solution)/shard_map/pallas_call | solution.py:349
  35.7 1.0 %collective-permute-done.8.recv_ref = f32[4,96,512]{2,1,0:T(8,128)S(1)} collective-permute-done((f32[4,96,512]{2,1,0:T(8,128)S(1)}, f32[4,96,512]{2,1,0:T(8,128)S(1)}, u32[]{:S(2)}, u32[]{:S(2)}) %collective-permute-start.8) | collective-permute-done | bytes 786464 | tf_op jit(solution)/shard_map/ppermute | solution.py:369
  36.9 3.4 %collective-permute-start.10 = (f32[96,512]{1,0:T(8,128)S(1)}, f32[96,512]{1,0:T(8,128)S(1)}, u32[]{:S(2)}, u32[]{:S(2)}) collective-permute-start(f32[96,512]{1,0:T(8,128)S(1)} %get-tuple-element.65), channel_id=1, source_target_pairs={{0,4},{1,5},{2,6},{3,7},{4,0},{5,1},{6,2},{7,3},{8,12},{9,13},{10,... | collective-permute-start | bytes 589832 | tf_op jit(solution)/shard_map/ppermute | solution.py:365
  40.3 1.1 %collective-permute-start.11 = (f32[96,512]{1,0:T(8,128)S(1)}, f32[96,512]{1,0:T(8,128)S(1)}, u32[]{:S(2)}, u32[]{:S(2)}) collective-permute-start(f32[96,512]{1,0:T(8,128)S(1)} %get-tuple-element.66), channel_id=1, source_target_pairs={{0,6},{1,7},{2,0},{3,1},{4,2},{5,3},{6,4},{7,5},{8,14},{9,15},{10,... | collective-permute-start | bytes 589832 | tf_op jit(solution)/shard_map/ppermute | solution.py:365
  41.4 2.5 %shard_map.123 = (f32[4,64,512]{2,1,0:T(8,128)S(1)}, f32[4,64,512]{2,1,0:T(8,128)S(1)}) custom-call(bf16[2,2048,512]{2,1,0:T(8,128)(2,1)S(1)} %get-tuple-element.46.hist_ref, bf16[2,2048,512]{2,1,0:T(8,128)(2,1)S(1)} %shard_map.121.token_ref.dk_ref, f32[96,512]{1,0:T(8,128)S(1)} %get-tuple-element.62.token_ref.part0), custom_call_target="tpu_custom_call" | custom-call | tf_op jit(solution)/shard_map/pallas_call | solution.py:349
  43.9 1.7 %collective-permute-done.9.part1 = f32[96,512]{1,0:T(8,128)S(1)} collective-permute-done((f32[96,512]{1,0:T(8,128)S(1)}, f32[96,512]{1,0:T(8,128)S(1)}, u32[]{:S(2)}, u32[]{:S(2)}) %collective-permute-start.9) | collective-permute-done | bytes 196640 | tf_op jit(solution)/shard_map/ppermute | solution.py:365
  45.6 3.8 %collective-permute-done.10.part2 = f32[96,512]{1,0:T(8,128)S(1)} collective-permute-done((f32[96,512]{1,0:T(8,128)S(1)}, f32[96,512]{1,0:T(8,128)S(1)}, u32[]{:S(2)}, u32[]{:S(2)}) %collective-permute-start.10) | collective-permute-done | bytes 196640 | tf_op jit(solution)/shard_map/ppermute | solution.py:365
  50.5 1.4 %collective-permute-done.13.other_ref = f32[16,512]{1,0:T(8,128)S(1)} collective-permute-done((f32[16,512]{1,0:T(8,128)S(1)}, f32[16,512]{1,0:T(8,128)S(1)}, u32[]{:S(2)}, u32[]{:S(2)}) %collective-permute-start.13) | collective-permute-done | bytes 32800 | tf_op jit(solution)/shard_map/ppermute | solution.py:369
  52.0 1.5 %collective-permute-start.14 = (f32[96,512]{1,0:T(8,128)S(1)}, f32[96,512]{1,0:T(8,128)S(1)}, u32[]{:S(2)}, u32[]{:S(2)}) collective-permute-start(f32[96,512]{1,0:T(8,128)S(1)} %get-tuple-element.71), channel_id=1, source_target_pairs={{0,2},{1,3},{2,4},{3,5},{4,6},{5,7},{6,0},{7,1},{8,10},{9,11},{10,... | collective-permute-start | bytes 589832 | tf_op jit(solution)/shard_map/ppermute | solution.py:365
  53.5 2.9 %collective-permute-start.15 = (f32[96,512]{1,0:T(8,128)S(1)}, f32[96,512]{1,0:T(8,128)S(1)}, u32[]{:S(2)}, u32[]{:S(2)}) collective-permute-start(f32[96,512]{1,0:T(8,128)S(1)} %get-tuple-element.72), channel_id=1, source_target_pairs={{0,4},{1,5},{2,6},{3,7},{4,0},{5,1},{6,2},{7,3},{8,12},{9,13},{10,... | collective-permute-start | bytes 589832 | tf_op jit(solution)/shard_map/ppermute | solution.py:365
  56.8 3.2 %shard_map.126 = (bf16[2,2048,512]{2,1,0:T(8,128)(2,1)}, f32[8,128]{1,0:T(8,128)S(1)}) custom-call(bf16[2,2048,512]{2,1,0:T(8,128)(2,1)S(1)} %shard_map.121.token_ref.dk_ref, bf16[2,2048,512]{2,1,0:T(8,128)(2,1)S(1)} %get-tuple-element.56.refs_4_.dv_ref, bf16[512,512]{1,0:T(8,128)(2,1)S(1)} %copy-done.2, bf16[512,512]{1,0:T(8,128)(2,1)S(1)} %copy-done.3, ...), custom_call_target="tpu_custom_call" | custom-call | tf_op jit(solution)/shard_map/pallas_call | solution.py:349
  60.4 5.1 %collective-permute-done.15.refs_2_ = f32[96,512]{1,0:T(8,128)S(1)} collective-permute-done((f32[96,512]{1,0:T(8,128)S(1)}, f32[96,512]{1,0:T(8,128)S(1)}, u32[]{:S(2)}, u32[]{:S(2)}) %collective-permute-start.15) | collective-permute-done | bytes 196640 | tf_op jit(solution)/shard_map/ppermute | solution.py:365
  66.0 1.6 %collective-permute-start.17 = (f32[4,16,512]{2,1,0:T(8,128)S(1)}, f32[4,16,512]{2,1,0:T(8,128)S(1)}, u32[]{:S(2)}, u32[]{:S(2)}) collective-permute-start(f32[4,16,512]{2,1,0:T(8,128)S(1)} %get-tuple-element.81), channel_id=1, source_target_pairs={{0,32},{8,40},{16,48},{24,56},{32,64},{40,72},{48,80},{56,88},{64,... | collective-permute-start | bytes 393224 | tf_op jit(solution)/shard_map/ppermute | solution.py:361
  67.6 2.9 %collective-permute-start.18 = (f32[4,16,512]{2,1,0:T(8,128)S(1)}, f32[4,16,512]{2,1,0:T(8,128)S(1)}, u32[]{:S(2)}, u32[]{:S(2)}) collective-permute-start(f32[4,16,512]{2,1,0:T(8,128)S(1)} %get-tuple-element.82), channel_id=1, source_target_pairs={{0,64},{8,72},{16,80},{24,88},{32,96},{40,104},{48,112},{56,120},{... | collective-permute-start | bytes 393224 | tf_op jit(solution)/shard_map/ppermute | solution.py:361
  70.5 1.3 %collective-permute-start.19 = (f32[4,16,512]{2,1,0:T(8,128)S(1)}, f32[4,16,512]{2,1,0:T(8,128)S(1)}, u32[]{:S(2)}, u32[]{:S(2)}) collective-permute-start(f32[4,16,512]{2,1,0:T(8,128)S(1)} %get-tuple-element.83), channel_id=1, source_target_pairs={{0,96},{8,104},{16,112},{24,120},{32,0},{40,8},{48,16},{56,24},{64... | collective-permute-start | bytes 393224 | tf_op jit(solution)/shard_map/ppermute | solution.py:361
  71.8 3.2 %shard_map.129 = (bf16[2,2048,512]{2,1,0:T(8,128)(2,1)}, f32[8,128]{1,0:T(8,128)S(1)}) custom-call(bf16[2,2048,512]{2,1,0:T(8,128)(2,1)S(1)} %shard_map.121.token_ref.dk_ref, bf16[2,2048,512]{2,1,0:T(8,128)(2,1)S(1)} %get-tuple-element.56.refs_4_.dv_ref, bf16[512,512]{1,0:T(8,128)(2,1)S(1)} %copy-done.2, ...), custom_call_target="tpu_custom_call", output_to_operand_aliasing={{0}: (5, {})} | custom-call | tf_op jit(solution)/shard_map/pallas_call | solution.py:349
  75.1 0.9 %collective-permute-done.18.refs_2_ = f32[4,16,512]{2,1,0:T(8,128)S(1)} collective-permute-done((f32[4,16,512]{2,1,0:T(8,128)S(1)}, f32[4,16,512]{2,1,0:T(8,128)S(1)}, u32[]{:S(2)}, u32[]{:S(2)}) %collective-permute-start.18) | collective-permute-done | bytes 131104 | tf_op jit(solution)/shard_map/ppermute | solution.py:361
  76.0 1.6 %collective-permute-start.20 = (f32[16,512]{1,0:T(8,128)S(1)}, f32[16,512]{1,0:T(8,128)S(1)}, u32[]{:S(2)}, u32[]{:S(2)}) collective-permute-start(f32[16,512]{1,0:T(8,128)S(1)} %get-tuple-element.86), channel_id=1, source_target_pairs={{0,8},{8,16},{16,24},{24,0},{32,40},{40,48},{48,56},{56,32},{64,72... | collective-permute-start | bytes 98312 | tf_op jit(solution)/shard_map/ppermute | solution.py:361
  77.6 2.7 %collective-permute-start.21 = (f32[16,512]{1,0:T(8,128)S(1)}, f32[16,512]{1,0:T(8,128)S(1)}, u32[]{:S(2)}, u32[]{:S(2)}) collective-permute-start(f32[16,512]{1,0:T(8,128)S(1)} %get-tuple-element.87), channel_id=1, source_target_pairs={{0,16},{8,24},{16,0},{24,8},{32,48},{40,56},{48,32},{56,40},{64,80... | collective-permute-start | bytes 98312 | tf_op jit(solution)/shard_map/ppermute | solution.py:361
  80.3 1.4 %collective-permute-start.22 = (f32[16,512]{1,0:T(8,128)S(1)}, f32[16,512]{1,0:T(8,128)S(1)}, u32[]{:S(2)}, u32[]{:S(2)}) collective-permute-start(f32[16,512]{1,0:T(8,128)S(1)} %get-tuple-element.88), channel_id=1, source_target_pairs={{0,24},{8,0},{16,8},{24,16},{32,56},{40,32},{48,40},{56,48},{64,88... | collective-permute-start | bytes 98312 | tf_op jit(solution)/shard_map/ppermute | solution.py:361
  83.0 1.2 %collective-permute-done.22.part3 = f32[16,512]{1,0:T(8,128)S(1)} collective-permute-done((f32[16,512]{1,0:T(8,128)S(1)}, f32[16,512]{1,0:T(8,128)S(1)}, u32[]{:S(2)}, u32[]{:S(2)}) %collective-permute-start.22) | collective-permute-done | bytes 32800 | tf_op jit(solution)/shard_map/ppermute | solution.py:361
  (52 shorter events, 7.9 us)
Async XLA Ops:
  0.6 12.7 %copy-start.3 = (bf16[512,512]{1,0:T(8,128)(2,1)S(1)}, bf16[512,512]{1,0:T(8,128)(2,1)}, u32[]{:S(2)}) copy-start(bf16[512,512]{1,0:T(8,128)(2,1)} %wv_ref.5) | copy-start | bytes 1572868
  7.9 10.6 %copy-start = (bf16[2,2048,512]{2,1,0:T(8,128)(2,1)}, bf16[2,2048,512]{2,1,0:T(8,128)(2,1)S(1)}, u32[]{:S(2)}) copy-start(bf16[2,2048,512]{2,1,0:T(8,128)(2,1)S(1)} %get-tuple-element.52.key_ref) | copy-start | bytes 12582916
  7.9 7.8 %collective-permute-start.2 = (f32[8,256]{1,0:T(8,128)S(1)}, f32[8,256]{1,0:T(8,128)S(1)}, u32[]{:S(2)}, u32[]{:S(2)}) collective-permute-start(f32[8,256]{1,0:T(8,128)S(1)} %get-tuple-element.47.refs_0_), channel_id=1, source_target_pairs={{0,6},{1,7},{2,0},{3,1},{4,2},{5,3},{6,4},{7,5},{8,14},{9,15},{10,... | collective-permute-start | bytes 24584 | tf_op jit(solution)/shard_map/ppermute | solution.py:365
  12.1 5.2 %collective-permute-start.1 = (f32[8,256]{1,0:T(8,128)S(1)}, f32[8,256]{1,0:T(8,128)S(1)}, u32[]{:S(2)}, u32[]{:S(2)}) collective-permute-start(f32[8,256]{1,0:T(8,128)S(1)} %get-tuple-element.47.refs_0_), channel_id=1, source_target_pairs={{0,4},{1,5},{2,6},{3,7},{4,0},{5,1},{6,2},{7,3},{8,12},{9,13},{10,... | collective-permute-start | bytes 24584 | tf_op jit(solution)/shard_map/ppermute | solution.py:365
  12.1 5.2 %collective-permute-start = (f32[8,256]{1,0:T(8,128)S(1)}, f32[8,256]{1,0:T(8,128)S(1)}, u32[]{:S(2)}, u32[]{:S(2)}) collective-permute-start(f32[8,256]{1,0:T(8,128)S(1)} %get-tuple-element.47.refs_0_), channel_id=1, source_target_pairs={{0,2},{1,3},{2,4},{3,5},{4,6},{5,7},{6,0},{7,1},{8,10},{9,11},{10,... | collective-permute-start | bytes 24584 | tf_op jit(solution)/shard_map/ppermute | solution.py:365
  15.7 1.7 %copy-start.6 = (bf16[512,512]{1,0:T(8,128)(2,1)S(1)}, bf16[512,512]{1,0:T(8,128)(2,1)}, u32[]{:S(2)}) copy-start(bf16[512,512]{1,0:T(8,128)(2,1)} %wout_ref.1) | copy-start | bytes 1572868
  15.7 1.7 %copy-start.7 = (bf16[128,512]{1,0:T(8,128)(2,1)S(1)}, bf16[128,512]{1,0:T(8,128)(2,1)}, u32[]{:S(2)}) copy-start(bf16[128,512]{1,0:T(8,128)(2,1)} %refs_7_.1) | copy-start | bytes 393220
  17.3 1.3 %collective-permute-start.3 = (f32[8,256]{1,0:T(8,128)S(1)}, f32[8,256]{1,0:T(8,128)S(1)}, u32[]{:S(2)}, u32[]{:S(2)}) collective-permute-start(f32[8,256]{1,0:T(8,128)S(1)} %shard_map.114.token_ref.one_ref), channel_id=1, source_target_pairs={{0,1},{1,0},{2,3},{3,2},{4,5},{5,4},{6,7},{7,6},{8,9},{9,8},{10,11... | collective-permute-start | bytes 24584 | tf_op jit(solution)/shard_map/ppermute | solution.py:369
  21.5 7.1 %collective-permute-start.6 = (f32[8,256]{1,0:T(8,128)S(1)}, f32[8,256]{1,0:T(8,128)S(1)}, u32[]{:S(2)}, u32[]{:S(2)}) collective-permute-start(f32[8,256]{1,0:T(8,128)S(1)} %get-tuple-element.53.refs_0_), channel_id=1, source_target_pairs={{0,6},{1,7},{2,0},{3,1},{4,2},{5,3},{6,4},{7,5},{8,14},{9,15},{10,... | collective-permute-start | bytes 24584 | tf_op jit(solution)/shard_map/ppermute | solution.py:365
  22.3 6.3 %collective-permute-start.5 = (f32[8,256]{1,0:T(8,128)S(1)}, f32[8,256]{1,0:T(8,128)S(1)}, u32[]{:S(2)}, u32[]{:S(2)}) collective-permute-start(f32[8,256]{1,0:T(8,128)S(1)} %get-tuple-element.53.refs_0_), channel_id=1, source_target_pairs={{0,4},{1,5},{2,6},{3,7},{4,0},{5,1},{6,2},{7,3},{8,12},{9,13},{10,... | collective-permute-start | bytes 24584 | tf_op jit(solution)/shard_map/ppermute | solution.py:365
  24.6 4.9 %collective-permute-start.4 = (f32[8,256]{1,0:T(8,128)S(1)}, f32[8,256]{1,0:T(8,128)S(1)}, u32[]{:S(2)}, u32[]{:S(2)}) collective-permute-start(f32[8,256]{1,0:T(8,128)S(1)} %get-tuple-element.53.refs_0_), channel_id=1, source_target_pairs={{0,2},{1,3},{2,4},{3,5},{4,6},{5,7},{6,0},{7,1},{8,10},{9,11},{10,... | collective-permute-start | bytes 24584 | tf_op jit(solution)/shard_map/ppermute | solution.py:365
  29.4 2.2 %copy-start.1 = (bf16[2,2048,512]{2,1,0:T(8,128)(2,1)S(1)}, bf16[2,2048,512]{2,1,0:T(8,128)(2,1)}, u32[]{:S(2)}) copy-start(bf16[2,2048,512]{2,1,0:T(8,128)(2,1)} %copy-done) | copy-start | bytes 12582916
  29.4 1.3 %collective-permute-start.7 = (f32[8,256]{1,0:T(8,128)S(1)}, f32[8,256]{1,0:T(8,128)S(1)}, u32[]{:S(2)}, u32[]{:S(2)}) collective-permute-start(f32[8,256]{1,0:T(8,128)S(1)} %shard_map.118.token_ref.one_ref), channel_id=1, source_target_pairs={{0,1},{1,0},{2,3},{3,2},{4,5},{5,4},{6,7},{7,6},{8,9},{9,8},{10,11... | collective-permute-start | bytes 24584 | tf_op jit(solution)/shard_map/ppermute | solution.py:369
  34.3 2.4 %collective-permute-start.8 = (f32[4,96,512]{2,1,0:T(8,128)S(1)}, f32[4,96,512]{2,1,0:T(8,128)S(1)}, u32[]{:S(2)}, u32[]{:S(2)}) collective-permute-start(f32[4,96,512]{2,1,0:T(8,128)S(1)} %get-tuple-element.61), channel_id=1, source_target_pairs={{0,1},{1,0},{2,3},{3,2},{4,5},{5,4},{6,7},{7,6},{8,9},{9,8},{10,11... | collective-permute-start | bytes 2359304 | tf_op jit(solution)/shard_map/ppermute | solution.py:369
  36.8 8.8 %collective-permute-start.9 = (f32[96,512]{1,0:T(8,128)S(1)}, f32[96,512]{1,0:T(8,128)S(1)}, u32[]{:S(2)}, u32[]{:S(2)}) collective-permute-start(f32[96,512]{1,0:T(8,128)S(1)} %get-tuple-element.64), channel_id=1, source_target_pairs={{0,2},{1,3},{2,4},{3,5},{4,6},{5,7},{6,0},{7,1},{8,10},{9,11},{10,... | collective-permute-start | bytes 589832 | tf_op jit(solution)/shard_map/ppermute | solution.py:365
  36.9 12.5 %collective-permute-start.10 = (f32[96,512]{1,0:T(8,128)S(1)}, f32[96,512]{1,0:T(8,128)S(1)}, u32[]{:S(2)}, u32[]{:S(2)}) collective-permute-start(f32[96,512]{1,0:T(8,128)S(1)} %get-tuple-element.65), channel_id=1, source_target_pairs={{0,4},{1,5},{2,6},{3,7},{4,0},{5,1},{6,2},{7,3},{8,12},{9,13},{10,... | collective-permute-start | bytes 589832 | tf_op jit(solution)/shard_map/ppermute | solution.py:365
  40.3 9.6 %collective-permute-start.11 = (f32[96,512]{1,0:T(8,128)S(1)}, f32[96,512]{1,0:T(8,128)S(1)}, u32[]{:S(2)}, u32[]{:S(2)}) collective-permute-start(f32[96,512]{1,0:T(8,128)S(1)} %get-tuple-element.66), channel_id=1, source_target_pairs={{0,6},{1,7},{2,0},{3,1},{4,2},{5,3},{6,4},{7,5},{8,14},{9,15},{10,... | collective-permute-start | bytes 589832 | tf_op jit(solution)/shard_map/ppermute | solution.py:365
  41.4 15.4 %copy-start.2 = (bf16[512,512]{1,0:T(8,128)(2,1)S(1)}, bf16[512,512]{1,0:T(8,128)(2,1)}, u32[]{:S(2)}) copy-start(bf16[512,512]{1,0:T(8,128)(2,1)} %wk_ref.3) | copy-start | bytes 1572868
  49.9 2.0 %collective-permute-start.12 = (f32[4,64,512]{2,1,0:T(8,128)S(1)}, f32[4,64,512]{2,1,0:T(8,128)S(1)}, u32[]{:S(2)}, u32[]{:S(2)}) collective-permute-start(f32[4,64,512]{2,1,0:T(8,128)S(1)} %get-tuple-element.68), channel_id=1, source_target_pairs={{0,1},{1,0},{2,3},{3,2},{4,5},{5,4},{6,7},{7,6},{8,9},{9,8},{10,11... | collective-permute-start | bytes 1572872 | tf_op jit(solution)/shard_map/ppermute | solution.py:369
  50.0 1.9 %collective-permute-start.13 = (f32[16,512]{1,0:T(8,128)S(1)}, f32[16,512]{1,0:T(8,128)S(1)}, u32[]{:S(2)}, u32[]{:S(2)}) collective-permute-start(f32[16,512]{1,0:T(8,128)S(1)} %get-tuple-element.69.mine_ref), channel_id=1, source_target_pairs={{0,1},{1,0},{2,3},{3,2},{4,5},{5,4},{6,7},{7,6},{8,9},{9,8},{10,11... | collective-permute-start | bytes 98312 | tf_op jit(solution)/shard_map/ppermute | solution.py:369
  52.0 8.4 %collective-permute-start.14 = (f32[96,512]{1,0:T(8,128)S(1)}, f32[96,512]{1,0:T(8,128)S(1)}, u32[]{:S(2)}, u32[]{:S(2)}) collective-permute-start(f32[96,512]{1,0:T(8,128)S(1)} %get-tuple-element.71), channel_id=1, source_target_pairs={{0,2},{1,3},{2,4},{3,5},{4,6},{5,7},{6,0},{7,1},{8,10},{9,11},{10,... | collective-permute-start | bytes 589832 | tf_op jit(solution)/shard_map/ppermute | solution.py:365
  53.5 12.0 %collective-permute-start.15 = (f32[96,512]{1,0:T(8,128)S(1)}, f32[96,512]{1,0:T(8,128)S(1)}, u32[]{:S(2)}, u32[]{:S(2)}) collective-permute-start(f32[96,512]{1,0:T(8,128)S(1)} %get-tuple-element.72), channel_id=1, source_target_pairs={{0,4},{1,5},{2,6},{3,7},{4,0},{5,1},{6,2},{7,3},{8,12},{9,13},{10,... | collective-permute-start | bytes 589832 | tf_op jit(solution)/shard_map/ppermute | solution.py:365
  56.4 9.1 %collective-permute-start.16 = (f32[96,512]{1,0:T(8,128)S(1)}, f32[96,512]{1,0:T(8,128)S(1)}, u32[]{:S(2)}, u32[]{:S(2)}) collective-permute-start(f32[96,512]{1,0:T(8,128)S(1)} %get-tuple-element.73), channel_id=1, source_target_pairs={{0,6},{1,7},{2,0},{3,1},{4,2},{5,3},{6,4},{7,5},{8,14},{9,15},{10,... | collective-permute-start | bytes 589832 | tf_op jit(solution)/shard_map/ppermute | solution.py:365
  56.8 8.7 %copy-start.5 = (bf16[128,512]{1,0:T(8,128)(2,1)S(1)}, bf16[128,512]{1,0:T(8,128)(2,1)}, u32[]{:S(2)}) copy-start(bf16[128,512]{1,0:T(8,128)(2,1)} %refs_5_.1) | copy-start | bytes 393220
  66.0 9.1 %collective-permute-start.17 = (f32[4,16,512]{2,1,0:T(8,128)S(1)}, f32[4,16,512]{2,1,0:T(8,128)S(1)}, u32[]{:S(2)}, u32[]{:S(2)}) collective-permute-start(f32[4,16,512]{2,1,0:T(8,128)S(1)} %get-tuple-element.81), channel_id=1, source_target_pairs={{0,32},{8,40},{16,48},{24,56},{32,64},{40,72},{48,80},{56,88},{64,... | collective-permute-start | bytes 393224 | tf_op jit(solution)/shard_map/ppermute | solution.py:361
  67.6 8.4 %collective-permute-start.18 = (f32[4,16,512]{2,1,0:T(8,128)S(1)}, f32[4,16,512]{2,1,0:T(8,128)S(1)}, u32[]{:S(2)}, u32[]{:S(2)}) collective-permute-start(f32[4,16,512]{2,1,0:T(8,128)S(1)} %get-tuple-element.82), channel_id=1, source_target_pairs={{0,64},{8,72},{16,80},{24,88},{32,96},{40,104},{48,112},{56,120},{... | collective-permute-start | bytes 393224 | tf_op jit(solution)/shard_map/ppermute | solution.py:361
  70.5 5.5 %collective-permute-start.19 = (f32[4,16,512]{2,1,0:T(8,128)S(1)}, f32[4,16,512]{2,1,0:T(8,128)S(1)}, u32[]{:S(2)}, u32[]{:S(2)}) collective-permute-start(f32[4,16,512]{2,1,0:T(8,128)S(1)} %get-tuple-element.83), channel_id=1, source_target_pairs={{0,96},{8,104},{16,112},{24,120},{32,0},{40,8},{48,16},{56,24},{64... | collective-permute-start | bytes 393224 | tf_op jit(solution)/shard_map/ppermute | solution.py:361
  71.8 9.9 %copy-start.4 = (bf16[512,512]{1,0:T(8,128)(2,1)S(1)}, bf16[512,512]{1,0:T(8,128)(2,1)}, u32[]{:S(2)}) copy-start(bf16[512,512]{1,0:T(8,128)(2,1)} %wq_ref.1) | copy-start | bytes 1572868
  76.0 6.7 %collective-permute-start.20 = (f32[16,512]{1,0:T(8,128)S(1)}, f32[16,512]{1,0:T(8,128)S(1)}, u32[]{:S(2)}, u32[]{:S(2)}) collective-permute-start(f32[16,512]{1,0:T(8,128)S(1)} %get-tuple-element.86), channel_id=1, source_target_pairs={{0,8},{8,16},{16,24},{24,0},{32,40},{40,48},{48,56},{56,32},{64,72... | collective-permute-start | bytes 98312 | tf_op jit(solution)/shard_map/ppermute | solution.py:361
  77.6 5.4 %collective-permute-start.21 = (f32[16,512]{1,0:T(8,128)S(1)}, f32[16,512]{1,0:T(8,128)S(1)}, u32[]{:S(2)}, u32[]{:S(2)}) collective-permute-start(f32[16,512]{1,0:T(8,128)S(1)} %get-tuple-element.87), channel_id=1, source_target_pairs={{0,16},{8,24},{16,0},{24,8},{32,48},{40,56},{48,32},{56,40},{64,80... | collective-permute-start | bytes 98312 | tf_op jit(solution)/shard_map/ppermute | solution.py:361
  80.3 3.9 %collective-permute-start.22 = (f32[16,512]{1,0:T(8,128)S(1)}, f32[16,512]{1,0:T(8,128)S(1)}, u32[]{:S(2)}, u32[]{:S(2)}) collective-permute-start(f32[16,512]{1,0:T(8,128)S(1)} %get-tuple-element.88), channel_id=1, source_target_pairs={{0,24},{8,0},{16,8},{24,16},{32,56},{40,32},{48,40},{56,48},{64,88... | collective-permute-start | bytes 98312 | tf_op jit(solution)/shard_map/ppermute | solution.py:361

commit v2 on v1

--- a/solution.py
+++ b/solution.py
@@ -12,6 +12,7 @@
 VMEM = pltpu.MemorySpace.VMEM
 HBM = pltpu.MemorySpace.HBM
 TILE = 1024
+LIMIT = 8
 
 
 def dot(left, right):
@@ -69,8 +70,8 @@
 
 
 def keys_kernel(lens_hbm, own_hbm, tok_hbm, wq_hbm, wk_hbm, hist_hbm,
-                key_ref, hist_ref, stat_ref, lim_ref, qb_ref, own_ref, qbt_ref,
-                lens_ref, tok_ref, wq_ref, wk_ref, sems):
+                key_ref, hist_ref, stat_ref, expo_ref, top_ref, own_ref, qbt_ref,
+                lens_ref, lim_ref, qb_ref, tok_ref, wq_ref, wk_ref, sems):
     small = [(wq_hbm, wq_ref), (tok_hbm, tok_ref), (own_hbm, own_ref), (lens_hbm, lens_ref),
              (wk_hbm, wk_ref)]
     small = [pltpu.make_async_copy(src, dst, sems.at[i]) for i, (src, dst) in enumerate(small)]
@@ -106,7 +107,9 @@
             score = jnp.where(seen, dot(pair_cols(key_ref, pair, rows), qb_ref[pair]), LOW)
             top = jnp.max(score, axis=0, keepdims=True)
             tops[pair].append(top)
-            sums[pair].append(jnp.sum(jnp.exp(score - top), axis=0, keepdims=True))
+            expo = jnp.exp(score - top)
+            expo_ref[rows, pair_lanes(pair)] = expo
+            sums[pair].append(jnp.sum(expo, axis=0, keepdims=True))
     peaks, totals = [], []
     for pair in range(PAIRS):
         peak = tops[pair][0]
@@ -115,6 +118,9 @@
         peaks.append(peak)
         totals.append(sum(x * jnp.exp(top - peak) for x, top in zip(sums[pair], tops[pair])))
     stat_ref[...] = jnp.concatenate(peaks + totals, axis=0)
+    for pair in range(PAIRS):
+        for index, top in enumerate(tops[pair]):
+            top_ref[index, pair : pair + 1] = top
 
 
 def values_kernel(wv_ref, hist_ref, val_ref):
@@ -144,19 +150,20 @@
     spread(g, owner_row.T, owner_row[0:1], gb_ref, gbt_ref)
 
 
-def probs_kernel(one_ref, two_ref, lim_ref, qb_ref, gb_ref, key_ref, val_ref, prob_ref, delta_ref):
+def probs_kernel(one_ref, two_ref, expo_ref, top_ref, gb_ref, val_ref, prob_ref, slope_ref, delta_ref):
     one, two = one_ref[0:4], two_ref[0:4]
     top = jnp.maximum(one, two)
     norm = one_ref[4:8] * jnp.exp(one - top) + two_ref[4:8] * jnp.exp(two - top)
     shift = top + jnp.log(norm)
     delta = [jnp.zeros((1, 256), F32) for _ in range(PAIRS)]
-    for rows in tiles(key_ref):
-        seen = seen_in(lim_ref, rows)
+    for index, rows in enumerate(tiles(val_ref)):
+        factor = jnp.exp(top_ref[index] - shift)
         for pair in range(PAIRS):
-            score = dot(pair_cols(key_ref, pair, rows), qb_ref[pair])
-            prob = jnp.where(seen, jnp.exp(score - shift[pair : pair + 1]), 0.0).astype(BF16)
-            prob_ref[rows, pair_lanes(pair)] = prob
+            lanes = pair_lanes(pair)
+            prob = (expo_ref[rows, lanes] * factor[pair : pair + 1]).astype(BF16)
+            prob_ref[rows, lanes] = prob
             slope = dot(pair_cols(val_ref, pair, rows), gb_ref[pair])
+            slope_ref[rows, lanes] = slope
             delta[pair] += jnp.sum(prob.astype(F32) * slope, axis=0, keepdims=True)
     delta_ref[...] = jnp.concatenate(delta + [jnp.zeros((4, 256), F32)], axis=0)
 
@@ -210,7 +217,7 @@
                     out[row : row + 4])
 
 
-def query_part_kernel(one_ref, two_ref, own_ref, prob_ref, key_ref, val_ref, gb_ref, att_ref,
+def query_part_kernel(one_ref, two_ref, own_ref, prob_ref, key_ref, slope_ref, att_ref,
                       share_ref, ds_ref, keep_ref, send_ref, dq_ref):
     delta = one_ref[...] + two_ref[...]
     own_col = jnp.broadcast_to(own_ref[...], (128, 128)).T
@@ -219,7 +226,7 @@
     for rows in tiles(key_ref):
         for pair in range(PAIRS):
             prob = prob_ref[rows, pair_lanes(pair)].astype(F32)
-            slope = dot(pair_cols(val_ref, pair, rows), gb_ref[pair])
+            slope = slope_ref[rows, pair_lanes(pair)]
             ds = (prob * (slope - delta[pair : pair + 1])).astype(BF16)
             ds_ref[rows, pair_lanes(pair)] = ds
             blks[pair] += dot_first(ds, pair_cols(key_ref, pair, rows))
@@ -332,17 +339,20 @@
     out_ref[...] = dot_last(dq_ref[...], wq_ref[...]).astype(BF16)
 
 
-def final_kernel(part0, part1, part2, part3, out_ref):
+def final_kernel(part0, part1, part2, part3, out_hbm, out_ref, sem):
     summed = part0[...] + part1[...] + part2[...] + part3[...]
     for part in range(4):
         out_ref[:, part, :] = summed[4 * part : 4 * part + 4]
+    copy = pltpu.make_async_copy(out_ref, out_hbm, sem)
+    copy.start()
+    copy.wait()
 
 
 IN_VMEM = pl.BlockSpec(memory_space=VMEM)
 IN_HBM = pl.BlockSpec(memory_space=pl.ANY)
 
 
-def call(kernel, args, outs, scratch=(), aliases=(), limit=26):
+def call(kernel, args, outs, scratch=(), aliases=(), limit=LIMIT):
     specs = {"vmem": IN_VMEM, "hbm": IN_HBM}
     spaces = {"vmem": VMEM, "hbm": HBM}
     ins = [pltpu.with_memory_space_constraint(x, spaces[s]) for x, s in args]
@@ -390,12 +400,13 @@
     v = lambda *xs: [(x, "vmem") for x in xs]
     h = lambda *xs: [(x, "hbm") for x in xs]
 
-    keys, hist, stats, lim, qb, own, qbt = call(
+    keys, hist, stats, expo, tops, own, qbt = call(
         keys_kernel,
         h(lengths, owner.reshape(1, rows), query_tokens, w_query, w_key, history),
-        [("vmem", BF16, ev), ("vmem", BF16, ev), vec, ("vmem", jnp.int32, (8, 256)),
-         ("vmem", BF16, blk), ("vmem", jnp.int32, (1, rows)), ("vmem", BF16, blk)],
-        [pltpu.SMEM((requests,), jnp.int32), pltpu.VMEM((rows, width), BF16),
+        [("vmem", BF16, ev), ("vmem", BF16, ev), vec, ("vmem", F32, pairs),
+         ("vmem", F32, (steps, PAIRS, 256)), ("vmem", jnp.int32, (1, rows)), ("vmem", BF16, blk)],
+        [pltpu.SMEM((requests,), jnp.int32), pltpu.VMEM((8, 256), jnp.int32),
+         pltpu.VMEM(blk, BF16), pltpu.VMEM((rows, width), BF16),
          pltpu.VMEM(mat, BF16), pltpu.VMEM(mat, BF16), dma((5 + 2 * steps,))],
     )
     stats = from_chips(stats)
@@ -403,9 +414,9 @@
     (stats,) = call(join_stats_kernel, v(*stats, values), [vec])
     gb, gbt = call(
         out_grads_kernel, v(d_out, w_out, own, stats), [("vmem", BF16, blk), ("vmem", BF16, blk)])
-    probs, delta = call(
-        probs_kernel, v(stats, across(stats), lim, qb, gb, keys, values),
-        [("vmem", BF16, pairs), vec])
+    probs, slopes, delta = call(
+        probs_kernel, v(stats, across(stats), expo, tops, gb, values),
+        [("vmem", BF16, pairs), ("vmem", F32, pairs), vec])
     delta = from_chips(delta)
     dv, share = call(
         value_grads_kernel, v(probs, hist, gbt), [("vmem", BF16, ev), ("vmem", F32, (8, 64, width))],
@@ -415,7 +426,7 @@
         attention_kernel, v(own, probs, values, delta), [("vmem", F32, (8, 16, width))])
 
     ds, keep, send = call(
-        query_part_kernel, v(delta, across(delta), own, probs, keys, values, gb, att, share),
+        query_part_kernel, v(delta, across(delta), own, probs, keys, slopes, att, share),
         [("vmem", BF16, pairs), wide_half, wide_half], [pltpu.VMEM((8, 16, width), F32)])
     (dk,) = call(key_grads_kernel, v(ds, qbt), [("vmem", BF16, ev)])
     parts = call(join_halves_kernel, v(keep, across(send), dk), [wide] * 4)
@@ -448,7 +459,9 @@
     outer = [outer[0]] + [turn(outer[i], lambda y, x: y * 4 + (x + i) % 4) for i in (1, 2, 3)]
     (query_grad,) = call(
         query_grad_kernel, v(dq, w_query), [("vmem", BF16, (rows, width))])
-    (weight_part,) = call(final_kernel, v(*outer), [("vmem", F32, (4, 4, width))])
+    (weight_part,) = call(
+        final_kernel, v(*outer), [("hbm", F32, (4, 4, width))],
+        [pltpu.VMEM((4, 4, width), F32), dma])
     return query_grad, hist_grad, weight_part
 
 

time: 85 us -> 82.8 us (0.974)
  local copies, waits for them, and re-layouts: 2.17 us -> 0.69 us
  Pallas kernels: 31.7 us -> 30.6 us
    unnamed x18 -> x13, local copies, waits for them, and re-layouts: 2.17 us -> 0.69 us
    pallas_call x20, Pallas kernels: 31.7 us -> 30.6 us  [call(): pl.pallas_call(kernel, in_specs=[specs[s] for _, s in args], out_specs=[s...]
  transfers between devices with their start and end apart: 23 -> 23, of which waited for: 13 -> 13; matrix products, arithmetic and copies ran while one was open for 1% -> 1% of each run, Pallas kernels for 21% -> 22%
where the time goes in v2:
time: 82.8 us; the launch traced here: 82.7 us
  starting transfers between devices  31.1 us (38%)
  Pallas kernels  30.6 us (37%)
  waiting for transfers between devices  19.2 us (23%)
  between operations  1.06 us (1%)
    pallas_call x20, Pallas kernels, call(): pl.pallas_call(kernel, in_specs=[specs[s] for _, s in args], out_specs=[s...  30.6 us
    ppermute x12, starting transfers between devices, up(): return lax.ppermute(x, 'seq', [(i, (i + 2 * chips) % 8) for i in range(8)])  18.3 us
    ppermute x12, waiting for transfers between devices, up(): return lax.ppermute(x, 'seq', [(i, (i + 2 * chips) % 8) for i in range(8)])  13.9 us
    ppermute x6, starting transfers between devices, turn(): return lax.ppermute(x, 'dp', [(i, to(i // 4, i % 4)) for i in range(16)])  11.6 us
    ppermute x5, waiting for transfers between devices, across(): return lax.ppermute(x, 'seq', [(i, i ^ 1) for i in range(8)])  2.76 us
    ppermute x6, waiting for transfers between devices, turn(): return lax.ppermute(x, 'dp', [(i, to(i // 4, i % 4)) for i in range(16)])  2.44 us
  transfers between devices with their start and end apart: 23, of which 13 were waited for; matrix products, arithmetic and copies ran while one was open for 1% of the time, Pallas kernels for 22%

profile of v2, /device:TPU:0, one launch (start us, length us, event | category | flops | bytes accessed | tf_op | source)
XLA Modules:
  0.0 82.7 jit_solution(10705646154019056815)
XLA Ops:
  0.6 7.6 %shard_map.112 = (bf16[2,2048,512]{2,1,0:T(8,128)(2,1)S(1)}, bf16[2,2048,512]{2,1,0:T(8,128)(2,1)S(1)}, f32[8,256]{1,0:T(8,128)S(1)}, f32[2048,1024]{1,0:T(8,128...) custom-call(s32[2]{0:T(128)} %lens_hbm.1, s32[1,128]{1,0:T(1,128)} %bitcast.1, ...), custom_call_target="tpu_custom_call" | custom-call | tf_op jit(solution)/shard_map/pallas_call | solution.py:359
  8.2 4.2 %collective-permute-start.2 = (f32[8,256]{1,0:T(8,128)S(1)}, f32[8,256]{1,0:T(8,128)S(1)}, u32[]{:S(2)}, u32[]{:S(2)}) collective-permute-start(f32[8,256]{1,0:T(8,128)S(1)} %get-tuple-element.48.refs_0_), channel_id=1, source_target_pairs={{0,6},{1,7},{2,0},{3,1},{4,2},{5,3},{6,4},{7,5},{8,14},{9,15},{10,... | collective-permute-start | bytes 24584 | tf_op jit(solution)/shard_map/ppermute | solution.py:375
  12.4 1.3 %collective-permute-start = (f32[8,256]{1,0:T(8,128)S(1)}, f32[8,256]{1,0:T(8,128)S(1)}, u32[]{:S(2)}, u32[]{:S(2)}) collective-permute-start(f32[8,256]{1,0:T(8,128)S(1)} %get-tuple-element.48.refs_0_), channel_id=1, source_target_pairs={{0,2},{1,3},{2,4},{3,5},{4,6},{5,7},{6,0},{7,1},{8,10},{9,11},{10,... | collective-permute-start | bytes 24584 | tf_op jit(solution)/shard_map/ppermute | solution.py:375
  13.7 2.3 %shard_map.113.refs_4_.val_ref = bf16[2,2048,512]{2,1,0:T(8,128)(2,1)S(1)} custom-call(bf16[512,512]{1,0:T(8,128)(2,1)S(1)} %copy-done.1, bf16[2,2048,512]{2,1,0:T(8,128)(2,1)S(1)} %get-tuple-element.47.hist_ref), custom_call_target="tpu_custom_call" | custom-call | tf_op jit(solution)/shard_map/pallas_call | solution.py:359
  16.1 1.5 %collective-permute-done.1.refs_2_ = f32[8,256]{1,0:T(8,128)S(1)} collective-permute-done((f32[8,256]{1,0:T(8,128)S(1)}, f32[8,256]{1,0:T(8,128)S(1)}, u32[]{:S(2)}, u32[]{:S(2)}) %collective-permute-start.1) | collective-permute-done | bytes 8224 | tf_op jit(solution)/shard_map/ppermute | solution.py:375
  18.9 1.8 %shard_map.116 = (bf16[2048,1024]{1,0:T(8,128)(2,1)S(1)}, f32[2048,1024]{1,0:T(8,128)S(1)}, f32[8,256]{1,0:T(8,128)S(1)}) custom-call(f32[8,256]{1,0:T(8,128)S(1)} %shard_map.114.token_ref.one_ref, f32[8,256]{1,0:T(8,128)S(1)} %collective-permute-done.3.two_ref, f32[2048,1024]{1,0:T(8,128)S(1)} %get-tuple-element.49.expo_ref, ...), custom_call_target="tpu_custom_call" | custom-call | tf_op jit(solution)/shard_map/pallas_call | solution.py:359
  20.7 0.8 collective-permute-start.6
  21.5 2.3 %collective-permute-start.5 = (f32[8,256]{1,0:T(8,128)S(1)}, f32[8,256]{1,0:T(8,128)S(1)}, u32[]{:S(2)}, u32[]{:S(2)}) collective-permute-start(f32[8,256]{1,0:T(8,128)S(1)} %get-tuple-element.53.refs_0_), channel_id=1, source_target_pairs={{0,4},{1,5},{2,6},{3,7},{4,0},{5,1},{6,2},{7,3},{8,12},{9,13},{10,... | collective-permute-start | bytes 24584 | tf_op jit(solution)/shard_map/ppermute | solution.py:375
  24.2 3.5 %shard_map.117 = (bf16[2,2048,512]{2,1,0:T(8,128)(2,1)S(1)}, f32[8,64,512]{2,1,0:T(8,128)S(1)}) custom-call(bf16[2048,1024]{1,0:T(8,128)(2,1)S(1)} %get-tuple-element.54.prob_ref, bf16[2,2048,512]{2,1,0:T(8,128)(2,1)S(1)} %get-tuple-element.47.hist_ref, bf16[4,256,256]{2,1,0:T(8,128)(2,1)S(1)} %get-tuple-element.55.gbt_ref), custom_call_target="tpu_custom_call" | custom-call | tf_op jit(solution)/shard_map/pallas_call | solution.py:359
  27.8 0.9 %collective-permute-done.4.refs_1_ = f32[8,256]{1,0:T(8,128)S(1)} collective-permute-done((f32[8,256]{1,0:T(8,128)S(1)}, f32[8,256]{1,0:T(8,128)S(1)}, u32[]{:S(2)}, u32[]{:S(2)}) %collective-permute-start.4) | collective-permute-done | bytes 8224 | tf_op jit(solution)/shard_map/ppermute | solution.py:375
  28.7 1.3 %shard_map.119.att_ref = f32[8,16,512]{2,1,0:T(8,128)S(1)} custom-call(s32[1,128]{1,0:T(1,128)S(1)} %get-tuple-element.51.own_ref, bf16[2048,1024]{1,0:T(8,128)(2,1)S(1)} %get-tuple-element.54.prob_ref, bf16[2,2048,512]{2,1,0:T(8,128)(2,1)S(1)} %shard_map.113.refs_4_.val_ref, f32[8,256]{1,0:T(8,128)S(1)} %shard_map.118.token_ref.one_ref), custom_call_target="tpu_custom_call" | custom-call | tf_op jit(solution)/shard_map/pallas_call | solution.py:359
  30.0 1.8 %shard_map.120 = (bf16[2048,1024]{1,0:T(8,128)(2,1)S(1)}, f32[4,96,512]{2,1,0:T(8,128)S(1)}, f32[4,96,512]{2,1,0:T(8,128)S(1)}) custom-call(f32[8,256]{1,0:T(8,128)S(1)} %shard_map.118.token_ref.one_ref, f32[8,256]{1,0:T(8,128)S(1)} %collective-permute-done.7.two_ref, s32[1,128]{1,0:T(1,128)S(1)} %get-tuple-element.51.own_ref, ...), custom_call_target="tpu_custom_call" | custom-call | tf_op jit(solution)/shard_map/pallas_call | solution.py:359
  32.4 1.3 %shard_map.121.token_ref.dk_ref = bf16[2,2048,512]{2,1,0:T(8,128)(2,1)S(1)} custom-call(bf16[2048,1024]{1,0:T(8,128)(2,1)S(1)} %get-tuple-element.60.ds_ref, bf16[4,256,256]{2,1,0:T(8,128)(2,1)S(1)} %get-tuple-element.61.qbt_ref), custom_call_target="tpu_custom_call" | custom-call | tf_op jit(solution)/shard_map/pallas_call | solution.py:359
  34.5 3.5 %collective-permute-start.10 = (f32[96,512]{1,0:T(8,128)S(1)}, f32[96,512]{1,0:T(8,128)S(1)}, u32[]{:S(2)}, u32[]{:S(2)}) collective-permute-start(f32[96,512]{1,0:T(8,128)S(1)} %get-tuple-element.67), channel_id=1, source_target_pairs={{0,4},{1,5},{2,6},{3,7},{4,0},{5,1},{6,2},{7,3},{8,12},{9,13},{10,... | collective-permute-start | bytes 589832 | tf_op jit(solution)/shard_map/ppermute | solution.py:375
  37.9 1.1 %collective-permute-start.11 = (f32[96,512]{1,0:T(8,128)S(1)}, f32[96,512]{1,0:T(8,128)S(1)}, u32[]{:S(2)}, u32[]{:S(2)}) collective-permute-start(f32[96,512]{1,0:T(8,128)S(1)} %get-tuple-element.68), channel_id=1, source_target_pairs={{0,6},{1,7},{2,0},{3,1},{4,2},{5,3},{6,4},{7,5},{8,14},{9,15},{10,... | collective-permute-start | bytes 589832 | tf_op jit(solution)/shard_map/ppermute | solution.py:375
  39.0 2.5 %shard_map.123 = (f32[4,64,512]{2,1,0:T(8,128)S(1)}, f32[4,64,512]{2,1,0:T(8,128)S(1)}) custom-call(bf16[2,2048,512]{2,1,0:T(8,128)(2,1)S(1)} %get-tuple-element.47.hist_ref, bf16[2,2048,512]{2,1,0:T(8,128)(2,1)S(1)} %shard_map.121.token_ref.dk_ref, f32[96,512]{1,0:T(8,128)S(1)} %get-tuple-element.64.token_ref.part0), custom_call_target="tpu_custom_call" | custom-call | tf_op jit(solution)/shard_map/pallas_call | solution.py:359
  41.6 1.6 %collective-permute-done.9.part1 = f32[96,512]{1,0:T(8,128)S(1)} collective-permute-done((f32[96,512]{1,0:T(8,128)S(1)}, f32[96,512]{1,0:T(8,128)S(1)}, u32[]{:S(2)}, u32[]{:S(2)}) %collective-permute-start.9) | collective-permute-done | bytes 196640 | tf_op jit(solution)/shard_map/ppermute | solution.py:375
  43.1 4.2 %collective-permute-done.10.part2 = f32[96,512]{1,0:T(8,128)S(1)} collective-permute-done((f32[96,512]{1,0:T(8,128)S(1)}, f32[96,512]{1,0:T(8,128)S(1)}, u32[]{:S(2)}, u32[]{:S(2)}) %collective-permute-start.10) | collective-permute-done | bytes 196640 | tf_op jit(solution)/shard_map/ppermute | solution.py:375
  48.3 1.4 %collective-permute-done.13.other_ref = f32[16,512]{1,0:T(8,128)S(1)} collective-permute-done((f32[16,512]{1,0:T(8,128)S(1)}, f32[16,512]{1,0:T(8,128)S(1)}, u32[]{:S(2)}, u32[]{:S(2)}) %collective-permute-start.13) | collective-permute-done | bytes 32800 | tf_op jit(solution)/shard_map/ppermute | solution.py:379
  49.8 1.4 %collective-permute-start.14 = (f32[96,512]{1,0:T(8,128)S(1)}, f32[96,512]{1,0:T(8,128)S(1)}, u32[]{:S(2)}, u32[]{:S(2)}) collective-permute-start(f32[96,512]{1,0:T(8,128)S(1)} %get-tuple-element.73), channel_id=1, source_target_pairs={{0,2},{1,3},{2,4},{3,5},{4,6},{5,7},{6,0},{7,1},{8,10},{9,11},{10,... | collective-permute-start | bytes 589832 | tf_op jit(solution)/shard_map/ppermute | solution.py:375
  51.2 2.8 %collective-permute-start.15 = (f32[96,512]{1,0:T(8,128)S(1)}, f32[96,512]{1,0:T(8,128)S(1)}, u32[]{:S(2)}, u32[]{:S(2)}) collective-permute-start(f32[96,512]{1,0:T(8,128)S(1)} %get-tuple-element.74), channel_id=1, source_target_pairs={{0,4},{1,5},{2,6},{3,7},{4,0},{5,1},{6,2},{7,3},{8,12},{9,13},{10,... | collective-permute-start | bytes 589832 | tf_op jit(solution)/shard_map/ppermute | solution.py:375
  54.5 3.2 %shard_map.126 = (bf16[2,2048,512]{2,1,0:T(8,128)(2,1)}, f32[8,128]{1,0:T(8,128)S(1)}) custom-call(bf16[2,2048,512]{2,1,0:T(8,128)(2,1)S(1)} %shard_map.121.token_ref.dk_ref, bf16[2,2048,512]{2,1,0:T(8,128)(2,1)S(1)} %get-tuple-element.56.refs_4_.dv_ref, bf16[512,512]{1,0:T(8,128)(2,1)S(1)} %copy-done, bf16[512,512]{1,0:T(8,128)(2,1)S(1)} %copy-done.1, ...), custom_call_target="tpu_custom_call" | custom-call | tf_op jit(solution)/shard_map/pallas_call | solution.py:359
  58.0 5.1 %collective-permute-done.15.refs_2_ = f32[96,512]{1,0:T(8,128)S(1)} collective-permute-done((f32[96,512]{1,0:T(8,128)S(1)}, f32[96,512]{1,0:T(8,128)S(1)}, u32[]{:S(2)}, u32[]{:S(2)}) %collective-permute-start.15) | collective-permute-done | bytes 196640 | tf_op jit(solution)/shard_map/ppermute | solution.py:375
  63.5 1.6 %collective-permute-start.17 = (f32[4,16,512]{2,1,0:T(8,128)S(1)}, f32[4,16,512]{2,1,0:T(8,128)S(1)}, u32[]{:S(2)}, u32[]{:S(2)}) collective-permute-start(f32[4,16,512]{2,1,0:T(8,128)S(1)} %get-tuple-element.83), channel_id=1, source_target_pairs={{0,32},{8,40},{16,48},{24,56},{32,64},{40,72},{48,80},{56,88},{64,... | collective-permute-start | bytes 393224 | tf_op jit(solution)/shard_map/ppermute | solution.py:371
  65.2 2.9 %collective-permute-start.18 = (f32[4,16,512]{2,1,0:T(8,128)S(1)}, f32[4,16,512]{2,1,0:T(8,128)S(1)}, u32[]{:S(2)}, u32[]{:S(2)}) collective-permute-start(f32[4,16,512]{2,1,0:T(8,128)S(1)} %get-tuple-element.84), channel_id=1, source_target_pairs={{0,64},{8,72},{16,80},{24,88},{32,96},{40,104},{48,112},{56,120},{... | collective-permute-start | bytes 393224 | tf_op jit(solution)/shard_map/ppermute | solution.py:371
  68.1 1.3 %collective-permute-start.19 = (f32[4,16,512]{2,1,0:T(8,128)S(1)}, f32[4,16,512]{2,1,0:T(8,128)S(1)}, u32[]{:S(2)}, u32[]{:S(2)}) collective-permute-start(f32[4,16,512]{2,1,0:T(8,128)S(1)} %get-tuple-element.85), channel_id=1, source_target_pairs={{0,96},{8,104},{16,112},{24,120},{32,0},{40,8},{48,16},{56,24},{64... | collective-permute-start | bytes 393224 | tf_op jit(solution)/shard_map/ppermute | solution.py:371
  69.4 3.2 %shard_map.129 = (bf16[2,2048,512]{2,1,0:T(8,128)(2,1)}, f32[8,128]{1,0:T(8,128)S(1)}) custom-call(bf16[2,2048,512]{2,1,0:T(8,128)(2,1)S(1)} %shard_map.121.token_ref.dk_ref, bf16[2,2048,512]{2,1,0:T(8,128)(2,1)S(1)} %get-tuple-element.56.refs_4_.dv_ref, bf16[512,512]{1,0:T(8,128)(2,1)S(1)} %copy-done, ...), custom_call_target="tpu_custom_call", output_to_operand_aliasing={{0}: (5, {})} | custom-call | tf_op jit(solution)/shard_map/pallas_call | solution.py:359
  72.6 0.9 %collective-permute-done.18.refs_2_ = f32[4,16,512]{2,1,0:T(8,128)S(1)} collective-permute-done((f32[4,16,512]{2,1,0:T(8,128)S(1)}, f32[4,16,512]{2,1,0:T(8,128)S(1)}, u32[]{:S(2)}, u32[]{:S(2)}) %collective-permute-start.18) | collective-permute-done | bytes 131104 | tf_op jit(solution)/shard_map/ppermute | solution.py:371
  73.6 1.6 %collective-permute-start.20 = (f32[16,512]{1,0:T(8,128)S(1)}, f32[16,512]{1,0:T(8,128)S(1)}, u32[]{:S(2)}, u32[]{:S(2)}) collective-permute-start(f32[16,512]{1,0:T(8,128)S(1)} %get-tuple-element.88), channel_id=1, source_target_pairs={{0,8},{8,16},{16,24},{24,0},{32,40},{40,48},{48,56},{56,32},{64,72... | collective-permute-start | bytes 98312 | tf_op jit(solution)/shard_map/ppermute | solution.py:371
  75.2 2.7 %collective-permute-start.21 = (f32[16,512]{1,0:T(8,128)S(1)}, f32[16,512]{1,0:T(8,128)S(1)}, u32[]{:S(2)}, u32[]{:S(2)}) collective-permute-start(f32[16,512]{1,0:T(8,128)S(1)} %get-tuple-element.89), channel_id=1, source_target_pairs={{0,16},{8,24},{16,0},{24,8},{32,48},{40,56},{48,32},{56,40},{64,80... | collective-permute-start | bytes 98312 | tf_op jit(solution)/shard_map/ppermute | solution.py:371
  77.9 1.4 %collective-permute-start.22 = (f32[16,512]{1,0:T(8,128)S(1)}, f32[16,512]{1,0:T(8,128)S(1)}, u32[]{:S(2)}, u32[]{:S(2)}) collective-permute-start(f32[16,512]{1,0:T(8,128)S(1)} %get-tuple-element.90), channel_id=1, source_target_pairs={{0,24},{8,0},{16,8},{24,16},{32,56},{40,32},{48,40},{56,48},{64,88... | collective-permute-start | bytes 98312 | tf_op jit(solution)/shard_map/ppermute | solution.py:371
  80.6 1.2 %collective-permute-done.22.part3 = f32[16,512]{1,0:T(8,128)S(1)} collective-permute-done((f32[16,512]{1,0:T(8,128)S(1)}, f32[16,512]{1,0:T(8,128)S(1)}, u32[]{:S(2)}, u32[]{:S(2)}) %collective-permute-start.22) | collective-permute-done | bytes 32800 | tf_op jit(solution)/shard_map/ppermute | solution.py:371
  (47 shorter events, 7.4 us)
Async XLA Ops:
  0.6 13.1 %copy-start.1 = (bf16[512,512]{1,0:T(8,128)(2,1)S(1)}, bf16[512,512]{1,0:T(8,128)(2,1)}, u32[]{:S(2)}) copy-start(bf16[512,512]{1,0:T(8,128)(2,1)} %wv_ref.5) | copy-start | bytes 1572868
  8.2 7.8 %collective-permute-start.2 = (f32[8,256]{1,0:T(8,128)S(1)}, f32[8,256]{1,0:T(8,128)S(1)}, u32[]{:S(2)}, u32[]{:S(2)}) collective-permute-start(f32[8,256]{1,0:T(8,128)S(1)} %get-tuple-element.48.refs_0_), channel_id=1, source_target_pairs={{0,6},{1,7},{2,0},{3,1},{4,2},{5,3},{6,4},{7,5},{8,14},{9,15},{10,... | collective-permute-start | bytes 24584 | tf_op jit(solution)/shard_map/ppermute | solution.py:375
  12.4 5.2 %collective-permute-start.1 = (f32[8,256]{1,0:T(8,128)S(1)}, f32[8,256]{1,0:T(8,128)S(1)}, u32[]{:S(2)}, u32[]{:S(2)}) collective-permute-start(f32[8,256]{1,0:T(8,128)S(1)} %get-tuple-element.48.refs_0_), channel_id=1, source_target_pairs={{0,4},{1,5},{2,6},{3,7},{4,0},{5,1},{6,2},{7,3},{8,12},{9,13},{10,... | collective-permute-start | bytes 24584 | tf_op jit(solution)/shard_map/ppermute | solution.py:375
  12.4 5.2 %collective-permute-start = (f32[8,256]{1,0:T(8,128)S(1)}, f32[8,256]{1,0:T(8,128)S(1)}, u32[]{:S(2)}, u32[]{:S(2)}) collective-permute-start(f32[8,256]{1,0:T(8,128)S(1)} %get-tuple-element.48.refs_0_), channel_id=1, source_target_pairs={{0,2},{1,3},{2,4},{3,5},{4,6},{5,7},{6,0},{7,1},{8,10},{9,11},{10,... | collective-permute-start | bytes 24584 | tf_op jit(solution)/shard_map/ppermute | solution.py:375
  16.0 1.7 %copy-start.4 = (bf16[512,512]{1,0:T(8,128)(2,1)S(1)}, bf16[512,512]{1,0:T(8,128)(2,1)}, u32[]{:S(2)}) copy-start(bf16[512,512]{1,0:T(8,128)(2,1)} %wout_ref.1) | copy-start | bytes 1572868
  16.1 1.7 %copy-start.5 = (bf16[128,512]{1,0:T(8,128)(2,1)S(1)}, bf16[128,512]{1,0:T(8,128)(2,1)}, u32[]{:S(2)}) copy-start(bf16[128,512]{1,0:T(8,128)(2,1)} %refs_7_.1) | copy-start | bytes 393220
  17.6 1.3 %collective-permute-start.3 = (f32[8,256]{1,0:T(8,128)S(1)}, f32[8,256]{1,0:T(8,128)S(1)}, u32[]{:S(2)}, u32[]{:S(2)}) collective-permute-start(f32[8,256]{1,0:T(8,128)S(1)} %shard_map.114.token_ref.one_ref), channel_id=1, source_target_pairs={{0,1},{1,0},{2,3},{3,2},{4,5},{5,4},{6,7},{7,6},{8,9},{9,8},{10,11... | collective-permute-start | bytes 24584 | tf_op jit(solution)/shard_map/ppermute | solution.py:379
  20.7 7.1 %collective-permute-start.6 = (f32[8,256]{1,0:T(8,128)S(1)}, f32[8,256]{1,0:T(8,128)S(1)}, u32[]{:S(2)}, u32[]{:S(2)}) collective-permute-start(f32[8,256]{1,0:T(8,128)S(1)} %get-tuple-element.53.refs_0_), channel_id=1, source_target_pairs={{0,6},{1,7},{2,0},{3,1},{4,2},{5,3},{6,4},{7,5},{8,14},{9,15},{10,... | collective-permute-start | bytes 24584 | tf_op jit(solution)/shard_map/ppermute | solution.py:375
  21.5 6.3 %collective-permute-start.5 = (f32[8,256]{1,0:T(8,128)S(1)}, f32[8,256]{1,0:T(8,128)S(1)}, u32[]{:S(2)}, u32[]{:S(2)}) collective-permute-start(f32[8,256]{1,0:T(8,128)S(1)} %get-tuple-element.53.refs_0_), channel_id=1, source_target_pairs={{0,4},{1,5},{2,6},{3,7},{4,0},{5,1},{6,2},{7,3},{8,12},{9,13},{10,... | collective-permute-start | bytes 24584 | tf_op jit(solution)/shard_map/ppermute | solution.py:375
  23.8 4.9 %collective-permute-start.4 = (f32[8,256]{1,0:T(8,128)S(1)}, f32[8,256]{1,0:T(8,128)S(1)}, u32[]{:S(2)}, u32[]{:S(2)}) collective-permute-start(f32[8,256]{1,0:T(8,128)S(1)} %get-tuple-element.53.refs_0_), channel_id=1, source_target_pairs={{0,2},{1,3},{2,4},{3,5},{4,6},{5,7},{6,0},{7,1},{8,10},{9,11},{10,... | collective-permute-start | bytes 24584 | tf_op jit(solution)/shard_map/ppermute | solution.py:375
  28.7 1.3 %collective-permute-start.7 = (f32[8,256]{1,0:T(8,128)S(1)}, f32[8,256]{1,0:T(8,128)S(1)}, u32[]{:S(2)}, u32[]{:S(2)}) collective-permute-start(f32[8,256]{1,0:T(8,128)S(1)} %shard_map.118.token_ref.one_ref), channel_id=1, source_target_pairs={{0,1},{1,0},{2,3},{3,2},{4,5},{5,4},{6,7},{7,6},{8,9},{9,8},{10,11... | collective-permute-start | bytes 24584 | tf_op jit(solution)/shard_map/ppermute | solution.py:379
  31.8 2.5 %collective-permute-start.8 = (f32[4,96,512]{2,1,0:T(8,128)S(1)}, f32[4,96,512]{2,1,0:T(8,128)S(1)}, u32[]{:S(2)}, u32[]{:S(2)}) collective-permute-start(f32[4,96,512]{2,1,0:T(8,128)S(1)} %get-tuple-element.63), channel_id=1, source_target_pairs={{0,1},{1,0},{2,3},{3,2},{4,5},{5,4},{6,7},{7,6},{8,9},{9,8},{10,11... | collective-permute-start | bytes 2359304 | tf_op jit(solution)/shard_map/ppermute | solution.py:379
  34.4 8.8 %collective-permute-start.9 = (f32[96,512]{1,0:T(8,128)S(1)}, f32[96,512]{1,0:T(8,128)S(1)}, u32[]{:S(2)}, u32[]{:S(2)}) collective-permute-start(f32[96,512]{1,0:T(8,128)S(1)} %get-tuple-element.66), channel_id=1, source_target_pairs={{0,2},{1,3},{2,4},{3,5},{4,6},{5,7},{6,0},{7,1},{8,10},{9,11},{10,... | collective-permute-start | bytes 589832 | tf_op jit(solution)/shard_map/ppermute | solution.py:375
  34.5 12.8 %collective-permute-start.10 = (f32[96,512]{1,0:T(8,128)S(1)}, f32[96,512]{1,0:T(8,128)S(1)}, u32[]{:S(2)}, u32[]{:S(2)}) collective-permute-start(f32[96,512]{1,0:T(8,128)S(1)} %get-tuple-element.67), channel_id=1, source_target_pairs={{0,4},{1,5},{2,6},{3,7},{4,0},{5,1},{6,2},{7,3},{8,12},{9,13},{10,... | collective-permute-start | bytes 589832 | tf_op jit(solution)/shard_map/ppermute | solution.py:375
  37.9 9.7 %collective-permute-start.11 = (f32[96,512]{1,0:T(8,128)S(1)}, f32[96,512]{1,0:T(8,128)S(1)}, u32[]{:S(2)}, u32[]{:S(2)}) collective-permute-start(f32[96,512]{1,0:T(8,128)S(1)} %get-tuple-element.68), channel_id=1, source_target_pairs={{0,6},{1,7},{2,0},{3,1},{4,2},{5,3},{6,4},{7,5},{8,14},{9,15},{10,... | collective-permute-start | bytes 589832 | tf_op jit(solution)/shard_map/ppermute | solution.py:375
  39.0 15.4 %copy-start = (bf16[512,512]{1,0:T(8,128)(2,1)S(1)}, bf16[512,512]{1,0:T(8,128)(2,1)}, u32[]{:S(2)}) copy-start(bf16[512,512]{1,0:T(8,128)(2,1)} %wk_ref.3) | copy-start | bytes 1572868
  47.7 2.0 %collective-permute-start.12 = (f32[4,64,512]{2,1,0:T(8,128)S(1)}, f32[4,64,512]{2,1,0:T(8,128)S(1)}, u32[]{:S(2)}, u32[]{:S(2)}) collective-permute-start(f32[4,64,512]{2,1,0:T(8,128)S(1)} %get-tuple-element.70), channel_id=1, source_target_pairs={{0,1},{1,0},{2,3},{3,2},{4,5},{5,4},{6,7},{7,6},{8,9},{9,8},{10,11... | collective-permute-start | bytes 1572872 | tf_op jit(solution)/shard_map/ppermute | solution.py:379
  47.8 1.9 %collective-permute-start.13 = (f32[16,512]{1,0:T(8,128)S(1)}, f32[16,512]{1,0:T(8,128)S(1)}, u32[]{:S(2)}, u32[]{:S(2)}) collective-permute-start(f32[16,512]{1,0:T(8,128)S(1)} %get-tuple-element.71.mine_ref), channel_id=1, source_target_pairs={{0,1},{1,0},{2,3},{3,2},{4,5},{5,4},{6,7},{7,6},{8,9},{9,8},{10,11... | collective-permute-start | bytes 98312 | tf_op jit(solution)/shard_map/ppermute | solution.py:379
  49.8 8.2 %collective-permute-start.14 = (f32[96,512]{1,0:T(8,128)S(1)}, f32[96,512]{1,0:T(8,128)S(1)}, u32[]{:S(2)}, u32[]{:S(2)}) collective-permute-start(f32[96,512]{1,0:T(8,128)S(1)} %get-tuple-element.73), channel_id=1, source_target_pairs={{0,2},{1,3},{2,4},{3,5},{4,6},{5,7},{6,0},{7,1},{8,10},{9,11},{10,... | collective-permute-start | bytes 589832 | tf_op jit(solution)/shard_map/ppermute | solution.py:375
  51.2 11.9 %collective-permute-start.15 = (f32[96,512]{1,0:T(8,128)S(1)}, f32[96,512]{1,0:T(8,128)S(1)}, u32[]{:S(2)}, u32[]{:S(2)}) collective-permute-start(f32[96,512]{1,0:T(8,128)S(1)} %get-tuple-element.74), channel_id=1, source_target_pairs={{0,4},{1,5},{2,6},{3,7},{4,0},{5,1},{6,2},{7,3},{8,12},{9,13},{10,... | collective-permute-start | bytes 589832 | tf_op jit(solution)/shard_map/ppermute | solution.py:375
  54.0 9.1 %collective-permute-start.16 = (f32[96,512]{1,0:T(8,128)S(1)}, f32[96,512]{1,0:T(8,128)S(1)}, u32[]{:S(2)}, u32[]{:S(2)}) collective-permute-start(f32[96,512]{1,0:T(8,128)S(1)} %get-tuple-element.75), channel_id=1, source_target_pairs={{0,6},{1,7},{2,0},{3,1},{4,2},{5,3},{6,4},{7,5},{8,14},{9,15},{10,... | collective-permute-start | bytes 589832 | tf_op jit(solution)/shard_map/ppermute | solution.py:375
  54.5 8.7 %copy-start.3 = (bf16[128,512]{1,0:T(8,128)(2,1)S(1)}, bf16[128,512]{1,0:T(8,128)(2,1)}, u32[]{:S(2)}) copy-start(bf16[128,512]{1,0:T(8,128)(2,1)} %refs_5_.1) | copy-start | bytes 393220
  63.5 9.1 %collective-permute-start.17 = (f32[4,16,512]{2,1,0:T(8,128)S(1)}, f32[4,16,512]{2,1,0:T(8,128)S(1)}, u32[]{:S(2)}, u32[]{:S(2)}) collective-permute-start(f32[4,16,512]{2,1,0:T(8,128)S(1)} %get-tuple-element.83), channel_id=1, source_target_pairs={{0,32},{8,40},{16,48},{24,56},{32,64},{40,72},{48,80},{56,88},{64,... | collective-permute-start | bytes 393224 | tf_op jit(solution)/shard_map/ppermute | solution.py:371
  65.2 8.4 %collective-permute-start.18 = (f32[4,16,512]{2,1,0:T(8,128)S(1)}, f32[4,16,512]{2,1,0:T(8,128)S(1)}, u32[]{:S(2)}, u32[]{:S(2)}) collective-permute-start(f32[4,16,512]{2,1,0:T(8,128)S(1)} %get-tuple-element.84), channel_id=1, source_target_pairs={{0,64},{8,72},{16,80},{24,88},{32,96},{40,104},{48,112},{56,120},{... | collective-permute-start | bytes 393224 | tf_op jit(solution)/shard_map/ppermute | solution.py:371
  68.1 5.5 %collective-permute-start.19 = (f32[4,16,512]{2,1,0:T(8,128)S(1)}, f32[4,16,512]{2,1,0:T(8,128)S(1)}, u32[]{:S(2)}, u32[]{:S(2)}) collective-permute-start(f32[4,16,512]{2,1,0:T(8,128)S(1)} %get-tuple-element.85), channel_id=1, source_target_pairs={{0,96},{8,104},{16,112},{24,120},{32,0},{40,8},{48,16},{56,24},{64... | collective-permute-start | bytes 393224 | tf_op jit(solution)/shard_map/ppermute | solution.py:371
  69.4 9.9 %copy-start.2 = (bf16[512,512]{1,0:T(8,128)(2,1)S(1)}, bf16[512,512]{1,0:T(8,128)(2,1)}, u32[]{:S(2)}) copy-start(bf16[512,512]{1,0:T(8,128)(2,1)} %wq_ref.1) | copy-start | bytes 1572868
  73.6 6.7 %collective-permute-start.20 = (f32[16,512]{1,0:T(8,128)S(1)}, f32[16,512]{1,0:T(8,128)S(1)}, u32[]{:S(2)}, u32[]{:S(2)}) collective-permute-start(f32[16,512]{1,0:T(8,128)S(1)} %get-tuple-element.88), channel_id=1, source_target_pairs={{0,8},{8,16},{16,24},{24,0},{32,40},{40,48},{48,56},{56,32},{64,72... | collective-permute-start | bytes 98312 | tf_op jit(solution)/shard_map/ppermute | solution.py:371
  75.2 5.4 %collective-permute-start.21 = (f32[16,512]{1,0:T(8,128)S(1)}, f32[16,512]{1,0:T(8,128)S(1)}, u32[]{:S(2)}, u32[]{:S(2)}) collective-permute-start(f32[16,512]{1,0:T(8,128)S(1)} %get-tuple-element.89), channel_id=1, source_target_pairs={{0,16},{8,24},{16,0},{24,8},{32,48},{40,56},{48,32},{56,40},{64,80... | collective-permute-start | bytes 98312 | tf_op jit(solution)/shard_map/ppermute | solution.py:371
  77.9 3.9 %collective-permute-start.22 = (f32[16,512]{1,0:T(8,128)S(1)}, f32[16,512]{1,0:T(8,128)S(1)}, u32[]{:S(2)}, u32[]{:S(2)}) collective-permute-start(f32[16,512]{1,0:T(8,128)S(1)} %get-tuple-element.90), channel_id=1, source_target_pairs={{0,24},{8,0},{16,8},{24,16},{32,56},{40,32},{48,40},{56,48},{64,88... | collective-permute-start | bytes 98312 | tf_op jit(solution)/shard_map/ppermute | solution.py:371

commit v3 on v2

--- a/solution.py
+++ b/solution.py
@@ -48,7 +48,7 @@
 
 
 def seen_in(lim_ref, rows):
-    place = lax.broadcasted_iota(jnp.int32, (TILE, 256), 0) + rows.start
+    place = lax.broadcasted_iota(jnp.int32, (rows.stop - rows.start, 256), 0) + rows.start
     return place < lim_ref[0:1]
 
 
@@ -78,7 +78,8 @@
     for copy in small:
         copy.start()
     chunks = []
-    for rows in tiles(hist_ref):
+    blocks = [slice(0, 512), slice(512, 1536), slice(1536, 2048)]
+    for rows in blocks:
         for req in range(2):
             copy = pltpu.make_async_copy(
                 hist_hbm.at[req, rows], hist_ref.at[req, rows], sems.at[5 + len(chunks)])
@@ -93,23 +94,40 @@
     q = dot(tok_ref[...], wq_ref[...]).astype(BF16).astype(F32) * 0.125
     spread(q, owner_row.T, owner_row[0:1], qb_ref, qbt_ref)
     small[4].wait()
-    for index, rows in enumerate(tiles(hist_ref)):
+    tops = [[] for _ in range(PAIRS)]
+    sums = [[] for _ in range(PAIRS)]
+
+    def project(rows):
         for req in range(2):
-            chunks[2 * index + req].wait()
             key_ref[req, rows] = dot(hist_ref[req, rows], wk_ref[...]).astype(BF16)
-    tops, sums = [], []
-    for pair in range(PAIRS):
-        tops.append([])
-        sums.append([])
-    for rows in tiles(hist_ref):
+
+    def score_tile(rows, pair):
         seen = seen_in(lim_ref, rows)
-        for pair in range(PAIRS):
-            score = jnp.where(seen, dot(pair_cols(key_ref, pair, rows), qb_ref[pair]), LOW)
-            top = jnp.max(score, axis=0, keepdims=True)
-            tops[pair].append(top)
-            expo = jnp.exp(score - top)
-            expo_ref[rows, pair_lanes(pair)] = expo
-            sums[pair].append(jnp.sum(expo, axis=0, keepdims=True))
+        score = jnp.where(seen, dot(pair_cols(key_ref, pair, rows), qb_ref[pair]), LOW)
+        top = jnp.max(score, axis=0, keepdims=True)
+        expo = jnp.exp(score - top)
+        expo_ref[rows, pair_lanes(pair)] = expo
+        tops[pair].append(top)
+        sums[pair].append(jnp.sum(expo, axis=0, keepdims=True))
+
+    waiting = []
+    for index, rows in enumerate(blocks):
+        chunks[2 * index].wait()
+        chunks[2 * index + 1].wait()
+        size = 256 if len(waiting) == PAIRS else 128
+        starts = list(range(rows.start, rows.stop, size)) if waiting else []
+        if not waiting:
+            project(rows)
+        every = max(len(waiting) // max(len(starts), 1), 1)
+        for count, item in enumerate(waiting):
+            if count % every == 0:
+                start = starts[count // every]
+                project(slice(start, start + size))
+            score_tile(*item)
+        waiting = [(slice(start, start + TILE // 2), pair)
+                   for start in range(rows.start, rows.stop, TILE // 2) for pair in range(PAIRS)]
+    for item in waiting:
+        score_tile(*item)
     peaks, totals = [], []
     for pair in range(PAIRS):
         peak = tops[pair][0]
@@ -156,7 +174,8 @@
     norm = one_ref[4:8] * jnp.exp(one - top) + two_ref[4:8] * jnp.exp(two - top)
     shift = top + jnp.log(norm)
     delta = [jnp.zeros((1, 256), F32) for _ in range(PAIRS)]
-    for index, rows in enumerate(tiles(val_ref)):
+    for index in range(top_ref.shape[0]):
+        rows = slice(index * (TILE // 2), (index + 1) * (TILE // 2))
         factor = jnp.exp(top_ref[index] - shift)
         for pair in range(PAIRS):
             lanes = pair_lanes(pair)
@@ -404,10 +423,10 @@
         keys_kernel,
         h(lengths, owner.reshape(1, rows), query_tokens, w_query, w_key, history),
         [("vmem", BF16, ev), ("vmem", BF16, ev), vec, ("vmem", F32, pairs),
-         ("vmem", F32, (steps, PAIRS, 256)), ("vmem", jnp.int32, (1, rows)), ("vmem", BF16, blk)],
+         ("vmem", F32, (2 * steps, PAIRS, 256)), ("vmem", jnp.int32, (1, rows)), ("vmem", BF16, blk)],
         [pltpu.SMEM((requests,), jnp.int32), pltpu.VMEM((8, 256), jnp.int32),
          pltpu.VMEM(blk, BF16), pltpu.VMEM((rows, width), BF16),
-         pltpu.VMEM(mat, BF16), pltpu.VMEM(mat, BF16), dma((5 + 2 * steps,))],
+         pltpu.VMEM(mat, BF16), pltpu.VMEM(mat, BF16), dma((11,))],
     )
     stats = from_chips(stats)
     (values,) = call(values_kernel, v(w_value, hist), [("vmem", BF16, ev)])

time: 82.8 us -> 82.5 us (level)
  no operation moved by 1% of the time
where the time goes in v3:
time: 82.5 us; the launch traced here: 82.4 us
  starting transfers between devices  31.1 us (38%)
  Pallas kernels  30.4 us (37%)
  waiting for transfers between devices  19.1 us (23%)
  between operations  1.06 us (1%)
    pallas_call x20, Pallas kernels, call(): pl.pallas_call(kernel, in_specs=[specs[s] for _, s in args], out_specs=[s...  30.4 us
    ppermute x12, starting transfers between devices, up(): return lax.ppermute(x, 'seq', [(i, (i + 2 * chips) % 8) for i in range(8)])  18.3 us
    ppermute x12, waiting for transfers between devices, up(): return lax.ppermute(x, 'seq', [(i, (i + 2 * chips) % 8) for i in range(8)])  13.9 us
    ppermute x6, starting transfers between devices, turn(): return lax.ppermute(x, 'dp', [(i, to(i // 4, i % 4)) for i in range(16)])  11.6 us
    ppermute x5, waiting for transfers between devices, across(): return lax.ppermute(x, 'seq', [(i, i ^ 1) for i in range(8)])  2.76 us
    ppermute x6, waiting for transfers between devices, turn(): return lax.ppermute(x, 'dp', [(i, to(i // 4, i % 4)) for i in range(16)])  2.44 us
  transfers between devices with their start and end apart: 23, of which 13 were waited for; matrix products, arithmetic and copies ran while one was open for 1% of the time, Pallas kernels for 22%

profile of v3, /device:TPU:0, one launch (start us, length us, event | category | flops | bytes accessed | tf_op | source)
XLA Modules:
  0.0 82.4 jit_solution(17163638706682393625)
XLA Ops:
  0.6 7.0 %shard_map.112 = (bf16[2,2048,512]{2,1,0:T(8,128)(2,1)S(1)}, bf16[2,2048,512]{2,1,0:T(8,128)(2,1)S(1)}, f32[8,256]{1,0:T(8,128)S(1)}, f32[2048,1024]{1,0:T(8,128...) custom-call(s32[2]{0:T(128)} %lens_hbm.1, s32[1,128]{1,0:T(1,128)} %bitcast.1, ...), custom_call_target="tpu_custom_call" | custom-call | tf_op jit(solution)/shard_map/pallas_call | solution.py:378
  7.7 4.2 %collective-permute-start.2 = (f32[8,256]{1,0:T(8,128)S(1)}, f32[8,256]{1,0:T(8,128)S(1)}, u32[]{:S(2)}, u32[]{:S(2)}) collective-permute-start(f32[8,256]{1,0:T(8,128)S(1)} %get-tuple-element.48.refs_0_), channel_id=1, source_target_pairs={{0,6},{1,7},{2,0},{3,1},{4,2},{5,3},{6,4},{7,5},{8,14},{9,15},{10,... | collective-permute-start | bytes 24584 | tf_op jit(solution)/shard_map/ppermute | solution.py:394
  11.9 1.3 %collective-permute-start = (f32[8,256]{1,0:T(8,128)S(1)}, f32[8,256]{1,0:T(8,128)S(1)}, u32[]{:S(2)}, u32[]{:S(2)}) collective-permute-start(f32[8,256]{1,0:T(8,128)S(1)} %get-tuple-element.48.refs_0_), channel_id=1, source_target_pairs={{0,2},{1,3},{2,4},{3,5},{4,6},{5,7},{6,0},{7,1},{8,10},{9,11},{10,... | collective-permute-start | bytes 24584 | tf_op jit(solution)/shard_map/ppermute | solution.py:394
  13.1 2.3 %shard_map.113.refs_4_.val_ref = bf16[2,2048,512]{2,1,0:T(8,128)(2,1)S(1)} custom-call(bf16[512,512]{1,0:T(8,128)(2,1)S(1)} %copy-done.1, bf16[2,2048,512]{2,1,0:T(8,128)(2,1)S(1)} %get-tuple-element.47.hist_ref), custom_call_target="tpu_custom_call" | custom-call | tf_op jit(solution)/shard_map/pallas_call | solution.py:378
  15.5 1.5 %collective-permute-done.1.refs_2_ = f32[8,256]{1,0:T(8,128)S(1)} collective-permute-done((f32[8,256]{1,0:T(8,128)S(1)}, f32[8,256]{1,0:T(8,128)S(1)}, u32[]{:S(2)}, u32[]{:S(2)}) %collective-permute-start.1) | collective-permute-done | bytes 8224 | tf_op jit(solution)/shard_map/ppermute | solution.py:394
  18.3 1.9 %shard_map.116 = (bf16[2048,1024]{1,0:T(8,128)(2,1)S(1)}, f32[2048,1024]{1,0:T(8,128)S(1)}, f32[8,256]{1,0:T(8,128)S(1)}) custom-call(f32[8,256]{1,0:T(8,128)S(1)} %shard_map.114.token_ref.one_ref, f32[8,256]{1,0:T(8,128)S(1)} %collective-permute-done.3.two_ref, f32[2048,1024]{1,0:T(8,128)S(1)} %get-tuple-element.49.expo_ref, ...), custom_call_target="tpu_custom_call" | custom-call | tf_op jit(solution)/shard_map/pallas_call | solution.py:378
  20.2 0.8 collective-permute-start.6
  21.0 2.3 %collective-permute-start.5 = (f32[8,256]{1,0:T(8,128)S(1)}, f32[8,256]{1,0:T(8,128)S(1)}, u32[]{:S(2)}, u32[]{:S(2)}) collective-permute-start(f32[8,256]{1,0:T(8,128)S(1)} %get-tuple-element.53.refs_0_), channel_id=1, source_target_pairs={{0,4},{1,5},{2,6},{3,7},{4,0},{5,1},{6,2},{7,3},{8,12},{9,13},{10,... | collective-permute-start | bytes 24584 | tf_op jit(solution)/shard_map/ppermute | solution.py:394
  23.7 3.5 %shard_map.117 = (bf16[2,2048,512]{2,1,0:T(8,128)(2,1)S(1)}, f32[8,64,512]{2,1,0:T(8,128)S(1)}) custom-call(bf16[2048,1024]{1,0:T(8,128)(2,1)S(1)} %get-tuple-element.54.prob_ref, bf16[2,2048,512]{2,1,0:T(8,128)(2,1)S(1)} %get-tuple-element.47.hist_ref, bf16[4,256,256]{2,1,0:T(8,128)(2,1)S(1)} %get-tuple-element.55.gbt_ref), custom_call_target="tpu_custom_call" | custom-call | tf_op jit(solution)/shard_map/pallas_call | solution.py:378
  27.3 0.9 %collective-permute-done.4.refs_1_ = f32[8,256]{1,0:T(8,128)S(1)} collective-permute-done((f32[8,256]{1,0:T(8,128)S(1)}, f32[8,256]{1,0:T(8,128)S(1)}, u32[]{:S(2)}, u32[]{:S(2)}) %collective-permute-start.4) | collective-permute-done | bytes 8224 | tf_op jit(solution)/shard_map/ppermute | solution.py:394
  28.2 1.3 %shard_map.119.att_ref = f32[8,16,512]{2,1,0:T(8,128)S(1)} custom-call(s32[1,128]{1,0:T(1,128)S(1)} %get-tuple-element.51.own_ref, bf16[2048,1024]{1,0:T(8,128)(2,1)S(1)} %get-tuple-element.54.prob_ref, bf16[2,2048,512]{2,1,0:T(8,128)(2,1)S(1)} %shard_map.113.refs_4_.val_ref, f32[8,256]{1,0:T(8,128)S(1)} %shard_map.118.token_ref.one_ref), custom_call_target="tpu_custom_call" | custom-call | tf_op jit(solution)/shard_map/pallas_call | solution.py:378
  29.5 2.0 %shard_map.120 = (bf16[2048,1024]{1,0:T(8,128)(2,1)S(1)}, f32[4,96,512]{2,1,0:T(8,128)S(1)}, f32[4,96,512]{2,1,0:T(8,128)S(1)}) custom-call(f32[8,256]{1,0:T(8,128)S(1)} %shard_map.118.token_ref.one_ref, f32[8,256]{1,0:T(8,128)S(1)} %collective-permute-done.7.two_ref, s32[1,128]{1,0:T(1,128)S(1)} %get-tuple-element.51.own_ref, ...), custom_call_target="tpu_custom_call" | custom-call | tf_op jit(solution)/shard_map/pallas_call | solution.py:378
  32.1 1.3 %shard_map.121.token_ref.dk_ref = bf16[2,2048,512]{2,1,0:T(8,128)(2,1)S(1)} custom-call(bf16[2048,1024]{1,0:T(8,128)(2,1)S(1)} %get-tuple-element.60.ds_ref, bf16[4,256,256]{2,1,0:T(8,128)(2,1)S(1)} %get-tuple-element.61.qbt_ref), custom_call_target="tpu_custom_call" | custom-call | tf_op jit(solution)/shard_map/pallas_call | solution.py:378
  34.2 3.5 %collective-permute-start.10 = (f32[96,512]{1,0:T(8,128)S(1)}, f32[96,512]{1,0:T(8,128)S(1)}, u32[]{:S(2)}, u32[]{:S(2)}) collective-permute-start(f32[96,512]{1,0:T(8,128)S(1)} %get-tuple-element.67), channel_id=1, source_target_pairs={{0,4},{1,5},{2,6},{3,7},{4,0},{5,1},{6,2},{7,3},{8,12},{9,13},{10,... | collective-permute-start | bytes 589832 | tf_op jit(solution)/shard_map/ppermute | solution.py:394
  37.7 1.1 %collective-permute-start.11 = (f32[96,512]{1,0:T(8,128)S(1)}, f32[96,512]{1,0:T(8,128)S(1)}, u32[]{:S(2)}, u32[]{:S(2)}) collective-permute-start(f32[96,512]{1,0:T(8,128)S(1)} %get-tuple-element.68), channel_id=1, source_target_pairs={{0,6},{1,7},{2,0},{3,1},{4,2},{5,3},{6,4},{7,5},{8,14},{9,15},{10,... | collective-permute-start | bytes 589832 | tf_op jit(solution)/shard_map/ppermute | solution.py:394
  38.7 2.5 %shard_map.123 = (f32[4,64,512]{2,1,0:T(8,128)S(1)}, f32[4,64,512]{2,1,0:T(8,128)S(1)}) custom-call(bf16[2,2048,512]{2,1,0:T(8,128)(2,1)S(1)} %get-tuple-element.47.hist_ref, bf16[2,2048,512]{2,1,0:T(8,128)(2,1)S(1)} %shard_map.121.token_ref.dk_ref, f32[96,512]{1,0:T(8,128)S(1)} %get-tuple-element.64.token_ref.part0), custom_call_target="tpu_custom_call" | custom-call | tf_op jit(solution)/shard_map/pallas_call | solution.py:378
  41.3 1.6 %collective-permute-done.9.part1 = f32[96,512]{1,0:T(8,128)S(1)} collective-permute-done((f32[96,512]{1,0:T(8,128)S(1)}, f32[96,512]{1,0:T(8,128)S(1)}, u32[]{:S(2)}, u32[]{:S(2)}) %collective-permute-start.9) | collective-permute-done | bytes 196640 | tf_op jit(solution)/shard_map/ppermute | solution.py:394
  42.8 4.2 %collective-permute-done.10.part2 = f32[96,512]{1,0:T(8,128)S(1)} collective-permute-done((f32[96,512]{1,0:T(8,128)S(1)}, f32[96,512]{1,0:T(8,128)S(1)}, u32[]{:S(2)}, u32[]{:S(2)}) %collective-permute-start.10) | collective-permute-done | bytes 196640 | tf_op jit(solution)/shard_map/ppermute | solution.py:394
  48.0 1.4 %collective-permute-done.13.other_ref = f32[16,512]{1,0:T(8,128)S(1)} collective-permute-done((f32[16,512]{1,0:T(8,128)S(1)}, f32[16,512]{1,0:T(8,128)S(1)}, u32[]{:S(2)}, u32[]{:S(2)}) %collective-permute-start.13) | collective-permute-done | bytes 32800 | tf_op jit(solution)/shard_map/ppermute | solution.py:398
  49.5 1.4 %collective-permute-start.14 = (f32[96,512]{1,0:T(8,128)S(1)}, f32[96,512]{1,0:T(8,128)S(1)}, u32[]{:S(2)}, u32[]{:S(2)}) collective-permute-start(f32[96,512]{1,0:T(8,128)S(1)} %get-tuple-element.73), channel_id=1, source_target_pairs={{0,2},{1,3},{2,4},{3,5},{4,6},{5,7},{6,0},{7,1},{8,10},{9,11},{10,... | collective-permute-start | bytes 589832 | tf_op jit(solution)/shard_map/ppermute | solution.py:394
  50.9 2.8 %collective-permute-start.15 = (f32[96,512]{1,0:T(8,128)S(1)}, f32[96,512]{1,0:T(8,128)S(1)}, u32[]{:S(2)}, u32[]{:S(2)}) collective-permute-start(f32[96,512]{1,0:T(8,128)S(1)} %get-tuple-element.74), channel_id=1, source_target_pairs={{0,4},{1,5},{2,6},{3,7},{4,0},{5,1},{6,2},{7,3},{8,12},{9,13},{10,... | collective-permute-start | bytes 589832 | tf_op jit(solution)/shard_map/ppermute | solution.py:394
  54.2 3.2 %shard_map.126 = (bf16[2,2048,512]{2,1,0:T(8,128)(2,1)}, f32[8,128]{1,0:T(8,128)S(1)}) custom-call(bf16[2,2048,512]{2,1,0:T(8,128)(2,1)S(1)} %shard_map.121.token_ref.dk_ref, bf16[2,2048,512]{2,1,0:T(8,128)(2,1)S(1)} %get-tuple-element.56.refs_4_.dv_ref, bf16[512,512]{1,0:T(8,128)(2,1)S(1)} %copy-done, bf16[512,512]{1,0:T(8,128)(2,1)S(1)} %copy-done.1, ...), custom_call_target="tpu_custom_call" | custom-call | tf_op jit(solution)/shard_map/pallas_call | solution.py:378
  57.8 5.1 %collective-permute-done.15.refs_2_ = f32[96,512]{1,0:T(8,128)S(1)} collective-permute-done((f32[96,512]{1,0:T(8,128)S(1)}, f32[96,512]{1,0:T(8,128)S(1)}, u32[]{:S(2)}, u32[]{:S(2)}) %collective-permute-start.15) | collective-permute-done | bytes 196640 | tf_op jit(solution)/shard_map/ppermute | solution.py:394
  63.3 1.6 %collective-permute-start.17 = (f32[4,16,512]{2,1,0:T(8,128)S(1)}, f32[4,16,512]{2,1,0:T(8,128)S(1)}, u32[]{:S(2)}, u32[]{:S(2)}) collective-permute-start(f32[4,16,512]{2,1,0:T(8,128)S(1)} %get-tuple-element.83), channel_id=1, source_target_pairs={{0,32},{8,40},{16,48},{24,56},{32,64},{40,72},{48,80},{56,88},{64,... | collective-permute-start | bytes 393224 | tf_op jit(solution)/shard_map/ppermute | solution.py:390
  64.9 2.9 %collective-permute-start.18 = (f32[4,16,512]{2,1,0:T(8,128)S(1)}, f32[4,16,512]{2,1,0:T(8,128)S(1)}, u32[]{:S(2)}, u32[]{:S(2)}) collective-permute-start(f32[4,16,512]{2,1,0:T(8,128)S(1)} %get-tuple-element.84), channel_id=1, source_target_pairs={{0,64},{8,72},{16,80},{24,88},{32,96},{40,104},{48,112},{56,120},{... | collective-permute-start | bytes 393224 | tf_op jit(solution)/shard_map/ppermute | solution.py:390
  67.8 1.3 %collective-permute-start.19 = (f32[4,16,512]{2,1,0:T(8,128)S(1)}, f32[4,16,512]{2,1,0:T(8,128)S(1)}, u32[]{:S(2)}, u32[]{:S(2)}) collective-permute-start(f32[4,16,512]{2,1,0:T(8,128)S(1)} %get-tuple-element.85), channel_id=1, source_target_pairs={{0,96},{8,104},{16,112},{24,120},{32,0},{40,8},{48,16},{56,24},{64... | collective-permute-start | bytes 393224 | tf_op jit(solution)/shard_map/ppermute | solution.py:390
  69.1 3.2 %shard_map.129 = (bf16[2,2048,512]{2,1,0:T(8,128)(2,1)}, f32[8,128]{1,0:T(8,128)S(1)}) custom-call(bf16[2,2048,512]{2,1,0:T(8,128)(2,1)S(1)} %shard_map.121.token_ref.dk_ref, bf16[2,2048,512]{2,1,0:T(8,128)(2,1)S(1)} %get-tuple-element.56.refs_4_.dv_ref, bf16[512,512]{1,0:T(8,128)(2,1)S(1)} %copy-done, ...), custom_call_target="tpu_custom_call", output_to_operand_aliasing={{0}: (5, {})} | custom-call | tf_op jit(solution)/shard_map/pallas_call | solution.py:378
  72.4 0.9 %collective-permute-done.18.refs_2_ = f32[4,16,512]{2,1,0:T(8,128)S(1)} collective-permute-done((f32[4,16,512]{2,1,0:T(8,128)S(1)}, f32[4,16,512]{2,1,0:T(8,128)S(1)}, u32[]{:S(2)}, u32[]{:S(2)}) %collective-permute-start.18) | collective-permute-done | bytes 131104 | tf_op jit(solution)/shard_map/ppermute | solution.py:390
  73.3 1.6 %collective-permute-start.20 = (f32[16,512]{1,0:T(8,128)S(1)}, f32[16,512]{1,0:T(8,128)S(1)}, u32[]{:S(2)}, u32[]{:S(2)}) collective-permute-start(f32[16,512]{1,0:T(8,128)S(1)} %get-tuple-element.88), channel_id=1, source_target_pairs={{0,8},{8,16},{16,24},{24,0},{32,40},{40,48},{48,56},{56,32},{64,72... | collective-permute-start | bytes 98312 | tf_op jit(solution)/shard_map/ppermute | solution.py:390
  74.9 2.7 %collective-permute-start.21 = (f32[16,512]{1,0:T(8,128)S(1)}, f32[16,512]{1,0:T(8,128)S(1)}, u32[]{:S(2)}, u32[]{:S(2)}) collective-permute-start(f32[16,512]{1,0:T(8,128)S(1)} %get-tuple-element.89), channel_id=1, source_target_pairs={{0,16},{8,24},{16,0},{24,8},{32,48},{40,56},{48,32},{56,40},{64,80... | collective-permute-start | bytes 98312 | tf_op jit(solution)/shard_map/ppermute | solution.py:390
  77.6 1.4 %collective-permute-start.22 = (f32[16,512]{1,0:T(8,128)S(1)}, f32[16,512]{1,0:T(8,128)S(1)}, u32[]{:S(2)}, u32[]{:S(2)}) collective-permute-start(f32[16,512]{1,0:T(8,128)S(1)} %get-tuple-element.90), channel_id=1, source_target_pairs={{0,24},{8,0},{16,8},{24,16},{32,56},{40,32},{48,40},{56,48},{64,88... | collective-permute-start | bytes 98312 | tf_op jit(solution)/shard_map/ppermute | solution.py:390
  80.3 1.2 %collective-permute-done.22.part3 = f32[16,512]{1,0:T(8,128)S(1)} collective-permute-done((f32[16,512]{1,0:T(8,128)S(1)}, f32[16,512]{1,0:T(8,128)S(1)}, u32[]{:S(2)}, u32[]{:S(2)}) %collective-permute-start.22) | collective-permute-done | bytes 32800 | tf_op jit(solution)/shard_map/ppermute | solution.py:390
  (47 shorter events, 7.4 us)
Async XLA Ops:
  0.6 12.5 %copy-start.1 = (bf16[512,512]{1,0:T(8,128)(2,1)S(1)}, bf16[512,512]{1,0:T(8,128)(2,1)}, u32[]{:S(2)}) copy-start(bf16[512,512]{1,0:T(8,128)(2,1)} %wv_ref.5) | copy-start | bytes 1572868
  7.7 7.8 %collective-permute-start.2 = (f32[8,256]{1,0:T(8,128)S(1)}, f32[8,256]{1,0:T(8,128)S(1)}, u32[]{:S(2)}, u32[]{:S(2)}) collective-permute-start(f32[8,256]{1,0:T(8,128)S(1)} %get-tuple-element.48.refs_0_), channel_id=1, source_target_pairs={{0,6},{1,7},{2,0},{3,1},{4,2},{5,3},{6,4},{7,5},{8,14},{9,15},{10,... | collective-permute-start | bytes 24584 | tf_op jit(solution)/shard_map/ppermute | solution.py:394
  11.9 5.2 %collective-permute-start.1 = (f32[8,256]{1,0:T(8,128)S(1)}, f32[8,256]{1,0:T(8,128)S(1)}, u32[]{:S(2)}, u32[]{:S(2)}) collective-permute-start(f32[8,256]{1,0:T(8,128)S(1)} %get-tuple-element.48.refs_0_), channel_id=1, source_target_pairs={{0,4},{1,5},{2,6},{3,7},{4,0},{5,1},{6,2},{7,3},{8,12},{9,13},{10,... | collective-permute-start | bytes 24584 | tf_op jit(solution)/shard_map/ppermute | solution.py:394
  11.9 5.2 %collective-permute-start = (f32[8,256]{1,0:T(8,128)S(1)}, f32[8,256]{1,0:T(8,128)S(1)}, u32[]{:S(2)}, u32[]{:S(2)}) collective-permute-start(f32[8,256]{1,0:T(8,128)S(1)} %get-tuple-element.48.refs_0_), channel_id=1, source_target_pairs={{0,2},{1,3},{2,4},{3,5},{4,6},{5,7},{6,0},{7,1},{8,10},{9,11},{10,... | collective-permute-start | bytes 24584 | tf_op jit(solution)/shard_map/ppermute | solution.py:394
  15.5 1.7 %copy-start.4 = (bf16[512,512]{1,0:T(8,128)(2,1)S(1)}, bf16[512,512]{1,0:T(8,128)(2,1)}, u32[]{:S(2)}) copy-start(bf16[512,512]{1,0:T(8,128)(2,1)} %wout_ref.1) | copy-start | bytes 1572868
  15.5 1.7 %copy-start.5 = (bf16[128,512]{1,0:T(8,128)(2,1)S(1)}, bf16[128,512]{1,0:T(8,128)(2,1)}, u32[]{:S(2)}) copy-start(bf16[128,512]{1,0:T(8,128)(2,1)} %refs_7_.1) | copy-start | bytes 393220
  17.0 1.3 %collective-permute-start.3 = (f32[8,256]{1,0:T(8,128)S(1)}, f32[8,256]{1,0:T(8,128)S(1)}, u32[]{:S(2)}, u32[]{:S(2)}) collective-permute-start(f32[8,256]{1,0:T(8,128)S(1)} %shard_map.114.token_ref.one_ref), channel_id=1, source_target_pairs={{0,1},{1,0},{2,3},{3,2},{4,5},{5,4},{6,7},{7,6},{8,9},{9,8},{10,11... | collective-permute-start | bytes 24584 | tf_op jit(solution)/shard_map/ppermute | solution.py:398
  20.2 7.1 %collective-permute-start.6 = (f32[8,256]{1,0:T(8,128)S(1)}, f32[8,256]{1,0:T(8,128)S(1)}, u32[]{:S(2)}, u32[]{:S(2)}) collective-permute-start(f32[8,256]{1,0:T(8,128)S(1)} %get-tuple-element.53.refs_0_), channel_id=1, source_target_pairs={{0,6},{1,7},{2,0},{3,1},{4,2},{5,3},{6,4},{7,5},{8,14},{9,15},{10,... | collective-permute-start | bytes 24584 | tf_op jit(solution)/shard_map/ppermute | solution.py:394
  21.0 6.3 %collective-permute-start.5 = (f32[8,256]{1,0:T(8,128)S(1)}, f32[8,256]{1,0:T(8,128)S(1)}, u32[]{:S(2)}, u32[]{:S(2)}) collective-permute-start(f32[8,256]{1,0:T(8,128)S(1)} %get-tuple-element.53.refs_0_), channel_id=1, source_target_pairs={{0,4},{1,5},{2,6},{3,7},{4,0},{5,1},{6,2},{7,3},{8,12},{9,13},{10,... | collective-permute-start | bytes 24584 | tf_op jit(solution)/shard_map/ppermute | solution.py:394
  23.3 4.9 %collective-permute-start.4 = (f32[8,256]{1,0:T(8,128)S(1)}, f32[8,256]{1,0:T(8,128)S(1)}, u32[]{:S(2)}, u32[]{:S(2)}) collective-permute-start(f32[8,256]{1,0:T(8,128)S(1)} %get-tuple-element.53.refs_0_), channel_id=1, source_target_pairs={{0,2},{1,3},{2,4},{3,5},{4,6},{5,7},{6,0},{7,1},{8,10},{9,11},{10,... | collective-permute-start | bytes 24584 | tf_op jit(solution)/shard_map/ppermute | solution.py:394
  28.2 1.3 %collective-permute-start.7 = (f32[8,256]{1,0:T(8,128)S(1)}, f32[8,256]{1,0:T(8,128)S(1)}, u32[]{:S(2)}, u32[]{:S(2)}) collective-permute-start(f32[8,256]{1,0:T(8,128)S(1)} %shard_map.118.token_ref.one_ref), channel_id=1, source_target_pairs={{0,1},{1,0},{2,3},{3,2},{4,5},{5,4},{6,7},{7,6},{8,9},{9,8},{10,11... | collective-permute-start | bytes 24584 | tf_op jit(solution)/shard_map/ppermute | solution.py:398
  31.5 2.5 %collective-permute-start.8 = (f32[4,96,512]{2,1,0:T(8,128)S(1)}, f32[4,96,512]{2,1,0:T(8,128)S(1)}, u32[]{:S(2)}, u32[]{:S(2)}) collective-permute-start(f32[4,96,512]{2,1,0:T(8,128)S(1)} %get-tuple-element.63), channel_id=1, source_target_pairs={{0,1},{1,0},{2,3},{3,2},{4,5},{5,4},{6,7},{7,6},{8,9},{9,8},{10,11... | collective-permute-start | bytes 2359304 | tf_op jit(solution)/shard_map/ppermute | solution.py:398
  34.1 8.8 %collective-permute-start.9 = (f32[96,512]{1,0:T(8,128)S(1)}, f32[96,512]{1,0:T(8,128)S(1)}, u32[]{:S(2)}, u32[]{:S(2)}) collective-permute-start(f32[96,512]{1,0:T(8,128)S(1)} %get-tuple-element.66), channel_id=1, source_target_pairs={{0,2},{1,3},{2,4},{3,5},{4,6},{5,7},{6,0},{7,1},{8,10},{9,11},{10,... | collective-permute-start | bytes 589832 | tf_op jit(solution)/shard_map/ppermute | solution.py:394
  34.2 12.8 %collective-permute-start.10 = (f32[96,512]{1,0:T(8,128)S(1)}, f32[96,512]{1,0:T(8,128)S(1)}, u32[]{:S(2)}, u32[]{:S(2)}) collective-permute-start(f32[96,512]{1,0:T(8,128)S(1)} %get-tuple-element.67), channel_id=1, source_target_pairs={{0,4},{1,5},{2,6},{3,7},{4,0},{5,1},{6,2},{7,3},{8,12},{9,13},{10,... | collective-permute-start | bytes 589832 | tf_op jit(solution)/shard_map/ppermute | solution.py:394
  37.7 9.7 %collective-permute-start.11 = (f32[96,512]{1,0:T(8,128)S(1)}, f32[96,512]{1,0:T(8,128)S(1)}, u32[]{:S(2)}, u32[]{:S(2)}) collective-permute-start(f32[96,512]{1,0:T(8,128)S(1)} %get-tuple-element.68), channel_id=1, source_target_pairs={{0,6},{1,7},{2,0},{3,1},{4,2},{5,3},{6,4},{7,5},{8,14},{9,15},{10,... | collective-permute-start | bytes 589832 | tf_op jit(solution)/shard_map/ppermute | solution.py:394
  38.7 15.4 %copy-start = (bf16[512,512]{1,0:T(8,128)(2,1)S(1)}, bf16[512,512]{1,0:T(8,128)(2,1)}, u32[]{:S(2)}) copy-start(bf16[512,512]{1,0:T(8,128)(2,1)} %wk_ref.3) | copy-start | bytes 1572868
  47.4 2.0 %collective-permute-start.12 = (f32[4,64,512]{2,1,0:T(8,128)S(1)}, f32[4,64,512]{2,1,0:T(8,128)S(1)}, u32[]{:S(2)}, u32[]{:S(2)}) collective-permute-start(f32[4,64,512]{2,1,0:T(8,128)S(1)} %get-tuple-element.70), channel_id=1, source_target_pairs={{0,1},{1,0},{2,3},{3,2},{4,5},{5,4},{6,7},{7,6},{8,9},{9,8},{10,11... | collective-permute-start | bytes 1572872 | tf_op jit(solution)/shard_map/ppermute | solution.py:398
  47.5 1.9 %collective-permute-start.13 = (f32[16,512]{1,0:T(8,128)S(1)}, f32[16,512]{1,0:T(8,128)S(1)}, u32[]{:S(2)}, u32[]{:S(2)}) collective-permute-start(f32[16,512]{1,0:T(8,128)S(1)} %get-tuple-element.71.mine_ref), channel_id=1, source_target_pairs={{0,1},{1,0},{2,3},{3,2},{4,5},{5,4},{6,7},{7,6},{8,9},{9,8},{10,11... | collective-permute-start | bytes 98312 | tf_op jit(solution)/shard_map/ppermute | solution.py:398
  49.5 8.2 %collective-permute-start.14 = (f32[96,512]{1,0:T(8,128)S(1)}, f32[96,512]{1,0:T(8,128)S(1)}, u32[]{:S(2)}, u32[]{:S(2)}) collective-permute-start(f32[96,512]{1,0:T(8,128)S(1)} %get-tuple-element.73), channel_id=1, source_target_pairs={{0,2},{1,3},{2,4},{3,5},{4,6},{5,7},{6,0},{7,1},{8,10},{9,11},{10,... | collective-permute-start | bytes 589832 | tf_op jit(solution)/shard_map/ppermute | solution.py:394
  50.9 11.9 %collective-permute-start.15 = (f32[96,512]{1,0:T(8,128)S(1)}, f32[96,512]{1,0:T(8,128)S(1)}, u32[]{:S(2)}, u32[]{:S(2)}) collective-permute-start(f32[96,512]{1,0:T(8,128)S(1)} %get-tuple-element.74), channel_id=1, source_target_pairs={{0,4},{1,5},{2,6},{3,7},{4,0},{5,1},{6,2},{7,3},{8,12},{9,13},{10,... | collective-permute-start | bytes 589832 | tf_op jit(solution)/shard_map/ppermute | solution.py:394
  53.7 9.1 %collective-permute-start.16 = (f32[96,512]{1,0:T(8,128)S(1)}, f32[96,512]{1,0:T(8,128)S(1)}, u32[]{:S(2)}, u32[]{:S(2)}) collective-permute-start(f32[96,512]{1,0:T(8,128)S(1)} %get-tuple-element.75), channel_id=1, source_target_pairs={{0,6},{1,7},{2,0},{3,1},{4,2},{5,3},{6,4},{7,5},{8,14},{9,15},{10,... | collective-permute-start | bytes 589832 | tf_op jit(solution)/shard_map/ppermute | solution.py:394
  54.2 8.6 %copy-start.3 = (bf16[128,512]{1,0:T(8,128)(2,1)S(1)}, bf16[128,512]{1,0:T(8,128)(2,1)}, u32[]{:S(2)}) copy-start(bf16[128,512]{1,0:T(8,128)(2,1)} %refs_5_.1) | copy-start | bytes 393220
  63.3 9.1 %collective-permute-start.17 = (f32[4,16,512]{2,1,0:T(8,128)S(1)}, f32[4,16,512]{2,1,0:T(8,128)S(1)}, u32[]{:S(2)}, u32[]{:S(2)}) collective-permute-start(f32[4,16,512]{2,1,0:T(8,128)S(1)} %get-tuple-element.83), channel_id=1, source_target_pairs={{0,32},{8,40},{16,48},{24,56},{32,64},{40,72},{48,80},{56,88},{64,... | collective-permute-start | bytes 393224 | tf_op jit(solution)/shard_map/ppermute | solution.py:390
  64.9 8.4 %collective-permute-start.18 = (f32[4,16,512]{2,1,0:T(8,128)S(1)}, f32[4,16,512]{2,1,0:T(8,128)S(1)}, u32[]{:S(2)}, u32[]{:S(2)}) collective-permute-start(f32[4,16,512]{2,1,0:T(8,128)S(1)} %get-tuple-element.84), channel_id=1, source_target_pairs={{0,64},{8,72},{16,80},{24,88},{32,96},{40,104},{48,112},{56,120},{... | collective-permute-start | bytes 393224 | tf_op jit(solution)/shard_map/ppermute | solution.py:390
  67.8 5.5 %collective-permute-start.19 = (f32[4,16,512]{2,1,0:T(8,128)S(1)}, f32[4,16,512]{2,1,0:T(8,128)S(1)}, u32[]{:S(2)}, u32[]{:S(2)}) collective-permute-start(f32[4,16,512]{2,1,0:T(8,128)S(1)} %get-tuple-element.85), channel_id=1, source_target_pairs={{0,96},{8,104},{16,112},{24,120},{32,0},{40,8},{48,16},{56,24},{64... | collective-permute-start | bytes 393224 | tf_op jit(solution)/shard_map/ppermute | solution.py:390
  69.1 9.9 %copy-start.2 = (bf16[512,512]{1,0:T(8,128)(2,1)S(1)}, bf16[512,512]{1,0:T(8,128)(2,1)}, u32[]{:S(2)}) copy-start(bf16[512,512]{1,0:T(8,128)(2,1)} %wq_ref.1) | copy-start | bytes 1572868
  73.3 6.7 %collective-permute-start.20 = (f32[16,512]{1,0:T(8,128)S(1)}, f32[16,512]{1,0:T(8,128)S(1)}, u32[]{:S(2)}, u32[]{:S(2)}) collective-permute-start(f32[16,512]{1,0:T(8,128)S(1)} %get-tuple-element.88), channel_id=1, source_target_pairs={{0,8},{8,16},{16,24},{24,0},{32,40},{40,48},{48,56},{56,32},{64,72... | collective-permute-start | bytes 98312 | tf_op jit(solution)/shard_map/ppermute | solution.py:390
  74.9 5.4 %collective-permute-start.21 = (f32[16,512]{1,0:T(8,128)S(1)}, f32[16,512]{1,0:T(8,128)S(1)}, u32[]{:S(2)}, u32[]{:S(2)}) collective-permute-start(f32[16,512]{1,0:T(8,128)S(1)} %get-tuple-element.89), channel_id=1, source_target_pairs={{0,16},{8,24},{16,0},{24,8},{32,48},{40,56},{48,32},{56,40},{64,80... | collective-permute-start | bytes 98312 | tf_op jit(solution)/shard_map/ppermute | solution.py:390
  77.6 3.9 %collective-permute-start.22 = (f32[16,512]{1,0:T(8,128)S(1)}, f32[16,512]{1,0:T(8,128)S(1)}, u32[]{:S(2)}, u32[]{:S(2)}) collective-permute-start(f32[16,512]{1,0:T(8,128)S(1)} %get-tuple-element.90), channel_id=1, source_target_pairs={{0,24},{8,0},{16,8},{24,16},{32,56},{40,32},{48,40},{56,48},{64,88... | collective-permute-start | bytes 98312 | tf_op jit(solution)/shard_map/ppermute | solution.py:390
